TPU v7x, 32 devices: a whole 2x2x4 slice. The times are simulated.
32 devices in a mesh: gx: 4 (over x, core), gy: 8 (over z, y).
Axes of the slice: x: 2, y: 2, z: 4, core: 2. Of those that a mesh axis runs over, the one named last changes fastest.
Arguments:
- intensity: float32 [32, 512, 1024], P(None, 'gx', 'gy'), may hold values from -6 to 6
- weight: float32 [32, 512, 1024], P(None, 'gx', 'gy'), may hold values from 0.2 to 5
- spacing: int32 [3], replicated, may hold values from 10 to 12
- anchor: int32 [3], replicated, may hold values from 0 to 5
- reach: int32 [1], replicated, may hold values from 36 to 49
Outputs:
- delta_pdf: float32 [32, 512, 1024], P('gx', 'gy')
All inputs are finite; a program needn't handle non-finite values.
Results may differ from a plain program's by a relative error of at most 0.00007.
Values sent between devices are 32-bit elements; how exact they have to be, the bound alone decides.
No kernel may reach another device: no remote copies, remote signals or barrier semaphores. Data moves between devices by JAX's collectives and lax.ppermute only.
A program may use at most 128 MiB of HBM per device.

v0:
```python
import functools
import math

import jax
import jax.numpy as jnp
import numpy as np
from jax import lax
from jax.experimental import pallas as pl
from jax.experimental.pallas import tpu as pltpu
from jax.sharding import PartitionSpec as P

MIN_SPACING = 10
HALO = 3
LANES = 128
VMEM_LIMIT = 40 * 1024 * 1024
ANY = pl.BlockSpec(memory_space=pl.ANY)
SMEM = pl.BlockSpec(memory_space=pltpu.SMEM)
VMEM = pl.BlockSpec(memory_space=pltpu.VMEM)


def hole_slots(depth):
    whole, left = divmod(depth, MIN_SPACING)
    return min(depth, 3 * whole + min(3, left))


def clean_chunks(count):
    first = min(2, count)
    return [part for part in (first, count - first) if part]


@functools.lru_cache(maxsize=None)
def cosine_split(length):
    freq = np.arange(length, dtype=np.int64)
    phase = (freq[:, None] * (2 * freq[None, :] + 1)) % (4 * length)
    matrix = np.cos(phase * (math.pi / (2 * length))) * math.sqrt(2.0 / length)
    high = matrix.astype(jnp.bfloat16)
    low = (matrix - high.astype(np.float64)).astype(jnp.bfloat16)
    return high, low


def split(value):
    high = value.astype(jnp.bfloat16)
    return high, (value - high.astype(jnp.float32)).astype(jnp.bfloat16)


def params(**more):
    return pltpu.CompilerParams(vmem_limit_bytes=VMEM_LIMIT, **more)


def floor_mod(value, by):
    rest = lax.rem(value, by)
    return jnp.where(rest < 0, rest + by, rest)


def order_layers(table, at, first, depth, spacing, anchor):
    phase = floor_mod(first - anchor, spacing)
    front = jnp.int32(0)
    back = jnp.int32(depth - 1)
    for step in range(depth):
        hole = (phase <= 1) | (phase == spacing - 1)
        table[at + jnp.where(hole, back, front)] = first + step
        front = jnp.where(hole, front, front + 1)
        back = jnp.where(hole, back - 1, back)
        phase = jnp.where(phase + 1 == spacing, 0, phase + 1)


def is_hole_layer(layer, spacing, anchor):
    phase = floor_mod(layer - anchor, spacing)
    return (phase <= 1) | (phase == spacing - 1)


def squared_dist(position, spacing, anchor):
    step = spacing.astype(jnp.float32)
    from_anchor = (position - anchor).astype(jnp.float32)
    turns = jnp.floor((from_anchor + 0.5) / step)
    offset = from_anchor - turns * step
    dist = jnp.minimum(offset, step - offset)
    return dist * dist


def gather_kernel(sizes, slot, count, spacing, anchor, layers, *rest):
    groups, depth = sizes
    outs, (table, sems) = rest[:groups], rest[groups:]
    me = lax.axis_index("gx")
    for group in range(groups):
        order_layers(table, group * depth, group * depth, depth, spacing[0], anchor[0])
    copies = []
    for k in range(groups):
        for part in range(count):
            layer = table[(me ^ k) * depth + slot + part]
            copies.append(
                pltpu.make_async_copy(layers.at[layer], outs[k].at[part], sems.at[k * count + part])
            )
    for copy in copies:
        copy.start()
    for copy in copies:
        copy.wait()


def gather_clean(spacing, anchor, layers, groups, slot, count):
    depth = layers.shape[0] // groups
    return pl.pallas_call(
        functools.partial(gather_kernel, (groups, depth), slot, count),
        out_shape=[jax.ShapeDtypeStruct((count,) + layers.shape[1:], jnp.float32)] * groups,
        in_specs=[SMEM, SMEM, ANY],
        out_specs=[ANY] * groups,
        scratch_shapes=[
            pltpu.SMEM((groups * depth,), jnp.int32),
            pltpu.SemaphoreType.DMA((groups * count,)),
        ],
        compiler_params=params(),
        name="gather_clean",
    )(spacing, anchor, layers)


def punch_kernel(sizes, spacing, anchor, reach, layers, weights, v_out, w_out, first_out, last_out, table, sems):
    groups, depth, held = sizes
    rows = v_out.shape[1]
    total = groups * held
    x_start = lax.axis_index("gx") * rows
    y_start = lax.axis_index("gy") * LANES
    for group in range(groups):
        order_layers(table, group * depth, group * depth, depth, spacing[0], anchor[0])
    copies = []
    for at in range(total):
        layer = table[(at // held) * depth + depth - held + at % held]
        copies.append(pltpu.make_async_copy(layers.at[layer], v_out.at[at], sems.at[at]))
        copies.append(pltpu.make_async_copy(weights.at[layer], w_out.at[at], sems.at[total + at]))
    for copy in copies:
        copy.start()
    shape = (rows, LANES)
    x_at = x_start + lax.broadcasted_iota(jnp.int32, shape, 0)
    lane = lax.broadcasted_iota(jnp.int32, shape, 1)
    plane = squared_dist(x_at, spacing[1], anchor[1]) + squared_dist(y_start + lane, spacing[2], anchor[2])
    flat = plane <= reach[0].astype(jnp.float32)
    for copy in copies:
        copy.wait()
    per_pack = LANES // HALO
    first = last = None
    for at in range(2 * total):
        if at < total:
            layer = table[(at // held) * depth + depth - held + at % held]
            tall = jnp.where(is_hole_layer(layer, spacing[0], anchor[0]), 1.0, 0.0)
            tile = jnp.where(flat & (jnp.full(shape, tall) > 0.5), 0.0, v_out[at])
            v_out[at] = tile
        else:
            tile = w_out[at - total]
        place = at % per_pack
        if place == 0:
            first = tile
            last = pltpu.roll(tile, HALO, 1)
        else:
            here = (lane >= HALO * place) & (lane < HALO * place + HALO)
            first = jnp.where(here, pltpu.roll(tile, HALO * place, 1), first)
            last = jnp.where(here, pltpu.roll(tile, HALO * (place + 1), 1), last)
        if place == per_pack - 1 or at == 2 * total - 1:
            first_out[at // per_pack] = first
            last_out[at // per_pack] = last


def punch(spacing, anchor, reach, layers, weights, groups, held):
    depth = layers.shape[0] // groups
    total = groups * held
    packs = -(-2 * total // (LANES // HALO))
    tile = layers.shape[1:]
    return pl.pallas_call(
        functools.partial(punch_kernel, (groups, depth, held)),
        out_shape=[jax.ShapeDtypeStruct((count,) + tile, jnp.float32) for count in (total, total, packs, packs)],
        in_specs=[SMEM, SMEM, SMEM, ANY, ANY],
        out_specs=[VMEM] * 4,
        scratch_shapes=[
            pltpu.SMEM((groups * depth,), jnp.int32),
            pltpu.SemaphoreType.DMA((2 * total,)),
        ],
        compiler_params=params(),
        name="punch",
    )(spacing, anchor, reach, layers, weights)


def edge_kernel(v, w, left, right, top, bottom):
    rows = v.shape[1]
    at = 0
    for ref in (v, w, left, right):
        count = ref.shape[0]
        top[at : at + count] = ref[:, :8]
        bottom[at : at + count] = ref[:, rows - 8 :]
        at += count


def edges(v, w, left, right):
    count = 2 * (v.shape[0] + left.shape[0])
    return pl.pallas_call(
        edge_kernel,
        out_shape=[jax.ShapeDtypeStruct((count, 8, LANES), jnp.float32)] * 2,
        in_specs=[VMEM] * 4,
        out_specs=[VMEM] * 2,
        compiler_params=params(),
        name="edges",
    )(v, w, left, right)


def fill_kernel(sizes, spacing, anchor, reach, v_in, w_in, left, right, above, below, *rest):
    groups, depth, held, full_x, full_y = sizes
    outs, (table, result) = rest[:groups], rest[groups:]
    total = groups * held
    packs = left.shape[0]
    rows = v_in.shape[1]
    me = lax.axis_index("gx")
    x_start = me * rows
    y_start = lax.axis_index("gy") * LANES
    for group in range(groups):
        order_layers(table, group * depth, group * depth, depth, spacing[0], anchor[0])
    tall = rows + 16
    shape = (tall, 2 * LANES)
    lane = lax.broadcasted_iota(jnp.int32, shape, 1)
    x_at = x_start - 8 + lax.broadcasted_iota(jnp.int32, shape, 0)
    y_at = y_start + jnp.where(lane < LANES + LANES // 2, lane, lane - 2 * LANES)
    plane = squared_dist(x_at, spacing[1], anchor[1]) + squared_dist(y_at, spacing[2], anchor[2])
    inside = (x_at >= 0) & (x_at < full_x) & (y_at >= 0) & (y_at < full_y)
    known = (lane < LANES + HALO) | (lane >= 2 * LANES - HALO)
    flat = (plane <= reach[0].astype(jnp.float32)) & inside & known
    flat_f = jnp.where(flat, 1.0, 0.0)
    per_pack = LANES // HALO
    edge_lane = lax.broadcasted_iota(jnp.int32, (tall, LANES), 1)

    def column(up, middle, down):
        return jnp.concatenate([up, middle, down], axis=0)

    def extended(ref, at, array):
        own = column(above[array], ref[at], below[array])
        pack = lax.div(array, per_pack)
        place = lax.rem(array, per_pack)
        at_left = 2 * total + pack
        at_right = 2 * total + packs + pack
        from_left = column(above[at_left], left[pack], below[at_left])
        from_right = column(above[at_right], right[pack], below[at_right])
        shift = HALO * place
        after = pltpu.roll(from_right, lax.rem(LANES - shift, LANES), 1)
        before = pltpu.roll(from_left, lax.rem(2 * LANES - HALO - shift, LANES), 1)
        edge = jnp.where(edge_lane < HALO, after, jnp.where(edge_lane >= LANES - HALO, before, 0.0))
        return jnp.concatenate([own, edge], axis=1)

    def smooth(value):
        value = pltpu.roll(value, 1, 0) + (value + value) + pltpu.roll(value, tall - 1, 0)
        return pltpu.roll(value, 1, 1) + (value + value) + pltpu.roll(value, 2 * LANES - 1, 1)

    def one(at, carry):
        layer = table[lax.div(at, held) * depth + depth - held + lax.rem(at, held)]
        hole_layer = is_hole_layer(layer, spacing[0], anchor[0])

        @pl.when(hole_layer)
        def _():
            value = extended(v_in, at, at)
            weight = extended(w_in, at, total + at)
            hole = flat_f > 0.5
            inverse = 1.0 / jnp.where(hole, smooth(weight), 1.0)
            for _ in range(3):
                value = jnp.where(hole, smooth(weight * value) * inverse, value)
            result[at] = value[8 : 8 + rows, :LANES]

        @pl.when(jnp.logical_not(hole_layer))
        def _():
            result[at] = v_in[at]

        return carry

    lax.fori_loop(0, total, one, 0)
    for k in range(groups):
        outs[k][...] = result[pl.ds((me ^ k) * held, held)]


def fill(spacing, anchor, reach, v, w, left, right, above, below, groups, held, depth, full):
    rows = v.shape[1]
    return pl.pallas_call(
        functools.partial(fill_kernel, (groups, depth, held) + full),
        out_shape=[jax.ShapeDtypeStruct((held, rows, LANES), jnp.float32)] * groups,
        in_specs=[SMEM] * 3 + [VMEM] * 6,
        out_specs=[VMEM] * groups,
        scratch_shapes=[
            pltpu.SMEM((groups * depth,), jnp.int32),
            pltpu.VMEM((groups * held, rows, LANES), jnp.float32),
        ],
        compiler_params=params(),
        name="fill",
    )(spacing, anchor, reach, v, w, left, right, above, below)


def dot3(a_high, a_low, b_high, b_low, dims):
    def dot(a, b):
        return lax.dot_general(a, b, (dims, ((), ())), preferred_element_type=jnp.float32)

    return dot(a_high, b_high) + (dot(a_high, b_low) + dot(a_low, b_high))


def x_kernel(sizes, c_high, c_low, *rest):
    groups, parts, step = sizes
    pieces, outs = rest[:groups], rest[groups : groups + parts]
    b_high, b_low, acc = rest[groups + parts :]
    count, rows, _ = pieces[0].shape
    out_rows = outs[0].shape[1]
    me = lax.axis_index("gx")
    row = lax.axis_index("gy")
    tile = pl.program_id(0)

    @pl.when(tile == 0)
    def _():
        for k in range(groups):
            at = pl.ds(pl.multiple_of((me ^ k) * rows, rows), rows)
            for layer in range(count):
                high, low = split(pieces[k][layer])
                cols = pl.ds(layer * LANES, LANES)
                b_high[at, cols] = high
                b_low[at, cols] = low

    at = pl.ds(pl.multiple_of(tile * step, step), step)
    acc[at] = dot3(c_high[...], c_low[...], b_high[...], b_low[...], ((1,), (0,)))

    @pl.when(tile == pl.num_programs(0) - 1)
    def _():
        for k in range(parts):
            at = pl.ds(pl.multiple_of((row ^ k) * out_rows, out_rows), out_rows)
            for layer in range(count):
                outs[k][layer] = acc[at, pl.ds(layer * LANES, LANES)]


def along_x(pieces, parts):
    groups = len(pieces)
    count, rows, _ = pieces[0].shape
    length = rows * groups
    step = min(512, length)
    high, low = cosine_split(length)
    whole = pl.BlockSpec(pieces[0].shape, lambda n: (0, 0, 0))
    out_tile = (count, length // parts, LANES)
    return pl.pallas_call(
        functools.partial(x_kernel, (groups, parts, step)),
        grid=(length // step,),
        out_shape=[jax.ShapeDtypeStruct(out_tile, jnp.float32)] * parts,
        in_specs=[pl.BlockSpec((step, length), lambda n: (n, 0))] * 2 + [whole] * groups,
        out_specs=[pl.BlockSpec(out_tile, lambda n: (0, 0, 0))] * parts,
        scratch_shapes=[
            pltpu.VMEM((length, count * LANES), jnp.bfloat16),
            pltpu.VMEM((length, count * LANES), jnp.bfloat16),
            pltpu.VMEM((length, count * LANES), jnp.float32),
        ],
        compiler_params=params(),
        name="along_x",
    )(high, low, *pieces)


def y_kernel(sizes, slot, chained, spacing, anchor, c_high, c_low, *rest):
    parts, depth, step = sizes
    pieces = rest[:parts]
    out, a_high, a_low, acc, table, sems = rest[parts + (1 if chained else 0) :]
    count, rows, _ = pieces[0].shape
    row = lax.axis_index("gy")
    tile = pl.program_id(0)

    @pl.when(tile == 0)
    def _():
        order_layers(table, 0, lax.axis_index("gx") * depth, depth, spacing[0], anchor[0])
        for k in range(parts):
            cols = pl.ds(pl.multiple_of((row ^ k) * LANES, LANES), LANES)
            for layer in range(count):
                high, low = split(pieces[k][layer])
                at = pl.ds(layer * rows, rows)
                a_high[at, cols] = high
                a_low[at, cols] = low

    acc[tile] = dot3(a_high[...], a_low[...], c_high[...], c_low[...], ((1,), (1,)))

    def copy(n, layer):
        here = table[slot + layer] - lax.axis_index("gx") * depth
        cols = pl.ds(pl.multiple_of(n * step, step), step)
        return pltpu.make_async_copy(
            acc.at[n, pl.ds(layer * rows, rows)], out.at[here, :, cols], sems.at[n, layer]
        )

    for layer in range(count):
        copy(tile, layer).start()

    @pl.when(tile == pl.num_programs(0) - 1)
    def _():
        for n in range(acc.shape[0]):
            for layer in range(count):
                copy(n, layer).wait()


def along_y(spacing, anchor, pieces, slot, depth, before):
    parts = len(pieces)
    count, rows, _ = pieces[0].shape
    length = parts * LANES
    step = min(256, length)
    steps = length // step
    high, low = cosine_split(length)
    whole = pl.BlockSpec(pieces[0].shape, lambda n: (0, 0, 0))
    chained = before is not None
    return pl.pallas_call(
        functools.partial(y_kernel, (parts, depth, step), slot, chained),
        grid=(steps,),
        out_shape=jax.ShapeDtypeStruct((depth, rows, length), jnp.float32),
        in_specs=[SMEM, SMEM]
        + [pl.BlockSpec((step, length), lambda n: (n, 0))] * 2
        + [whole] * parts
        + ([ANY] if chained else []),
        out_specs=ANY,
        scratch_shapes=[
            pltpu.VMEM((count * rows, length), jnp.bfloat16),
            pltpu.VMEM((count * rows, length), jnp.bfloat16),
            pltpu.VMEM((steps, count * rows, step), jnp.float32),
            pltpu.SMEM((depth,), jnp.int32),
            pltpu.SemaphoreType.DMA((steps, count)),
        ],
        input_output_aliases={4 + parts: 0} if chained else {},
        compiler_params=params(),
        name="along_y",
    )(spacing, anchor, high, low, *pieces, *([before] if chained else []))


def swap(value, axis, k):
    size = lax.axis_size(axis)
    return lax.ppermute(value, axis, [(i, i ^ k) for i in range(size)])


def exchange(pieces, axis):
    got = {k: swap(pieces[k], axis, k) for k in reversed(range(1, len(pieces)))}
    return [pieces[0]] + [got[k] for k in range(1, len(pieces))]


def shift(value, axis, by):
    size = lax.axis_size(axis)
    return lax.ppermute(value, axis, [(i, i + by) for i in range(size) if 0 <= i + by < size])


def per_device(intensity, weight, spacing, anchor, reach):
    layers, rows, _ = intensity.shape
    groups = lax.axis_size("gx")
    parts = lax.axis_size("gy")
    depth = layers // groups
    held = hole_slots(depth)
    full = (rows * groups, LANES * parts)

    chunks = []
    slot = 0
    for count in clean_chunks(depth - held):
        gathered = gather_clean(spacing, anchor, intensity, groups, slot, count)
        chunks.append((slot, exchange(gathered, "gx")))
        slot += count

    v, w, first, last = punch(spacing, anchor, reach, intensity, weight, groups, held)
    left = shift(last, "gy", 1)
    right = shift(first, "gy", -1)
    top, bottom = edges(v, w, left, right)
    above = shift(bottom, "gx", 1)
    below = shift(top, "gx", -1)
    filled = fill(spacing, anchor, reach, v, w, left, right, above, below, groups, held, depth, full)
    chunks.append((slot, exchange(filled, "gx")))

    moved = [(at, exchange(along_x(pieces, parts), "gy")) for at, pieces in chunks]
    out = None
    for at, pieces in moved:
        out = along_y(spacing, anchor, pieces, at, depth, out)
    return out


def solution(mesh):
    in_specs = (P(None, "gx", "gy"), P(None, "gx", "gy"), P(), P(), P())
    out_specs = P("gx", "gy", None)
    return jax.shard_map(per_device, mesh=mesh, in_specs=in_specs, out_specs=out_specs, check_vma=False)
```

profile of v0, /device:TPU:0, one launch (start us, length us, event | category | flops | bytes accessed | tf_op | source)
XLA Modules:
  0.0 112.6 jit_solution(51586141934729381)
XLA Ops:
  0.0 1.6 %copy-done.2 = f32[32,128,128]{2,1,0:T(8,128)S(1)} copy-done((f32[32,128,128]{2,1,0:T(8,128)S(1)}, f32[32,128,128]{2,1,0:T(8,128)}, u32[]{:S(2)}) %copy-start.2) | copy-done | bytes 2097176
  2.9 1.5 %gather_clean.3 = (f32[2,128,128]{2,1,0:T(8,128)S(1)}, f32[2,128,128]{2,1,0:T(8,128)S(1)}, f32[2,128,128]{2,1,0:T(8,128)S(1)}, f32[2,128,128]{2,1,0:T(8,128)S(1)}) custom-call(s32[3]{0:T(128)S(1)} %copy-done.7, s32[3]{0:T(128)S(1)} %copy-done.8, f32[32,128,128]{2,1,0:T(8,128)S(1)} %copy-done.2), custom_call_target="tpu_custom_call" | custom-call | tf_op jit(solution)/shard_map/gather_clean/pallas_call | solution.py:102
  4.9 2.6 %collective-permute-start.25 = (f32[2,128,128]{2,1,0:T(8,128)S(1)}, f32[2,128,128]{2,1,0:T(8,128)S(1)}, u32[]{:S(2)}, u32[]{:S(2)}) collective-permute-start(f32[2,128,128]{2,1,0:T(8,128)S(1)} %get-tuple-element.79), channel_id=1, source_target_pairs={{0,16},{8,24},{16,0},{24,8},{1,17},{9,25},{17,1},{25,9},{2,18},{10... | collective-permute-start | bytes 393224 | tf_op jit(solution)/shard_map/ppermute | solution.py:421
  8.2 3.9 %punch.1 = (f32[12,128,128]{2,1,0:T(8,128)S(1)}, f32[12,128,128]{2,1,0:T(8,128)S(1)}, f32[1,128,128]{2,1,0:T(8,128)S(1)}, f32[1,128,128]{2,1,0:T(8,128)S(1)}) custom-call(s32[3]{0:T(128)S(1)} %copy-done.7, s32[3]{0:T(128)S(1)} %copy-done.8, s32[1]{0:T(128)S(6)} %copy.14.reach, f32[32,128,128]{2,1,0:T(8,128)S(1)} %copy-done.2, f32[32,128,128]{2,1,0:T(8,128)S(1)} %copy-done.6), custom_call_target="tpu_custom_call" | custom-call | tf_op jit(solution)/shard_map/punch/pallas_call | solution.py:166
  12.2 3.8 %collective-permute-start = (f32[1,128,128]{2,1,0:T(8,128)S(1)}, f32[1,128,128]{2,1,0:T(8,128)S(1)}, u32[]{:S(2)}, u32[]{:S(2)}) collective-permute-start(f32[1,128,128]{2,1,0:T(8,128)S(1)} %get-tuple-element.49), channel_id=1, source_target_pairs={{0,1},{1,2},{2,3},{3,4},{4,5},{5,6},{6,7},{8,9},{9,10},{10,11},{11... | collective-permute-start | bytes 196616 | tf_op jit(solution)/shard_map/ppermute | solution.py:431
  17.9 4.3 %collective-permute-done.1.right = f32[1,128,128]{2,1,0:T(8,128)S(1)} collective-permute-done((f32[1,128,128]{2,1,0:T(8,128)S(1)}, f32[1,128,128]{2,1,0:T(8,128)S(1)}, u32[]{:S(2)}, u32[]{:S(2)}) %collective-permute-start.1) | collective-permute-done | bytes 65568 | tf_op jit(solution)/shard_map/ppermute | solution.py:431
  24.8 1.9 %gather_clean.2 = (f32[3,128,128]{2,1,0:T(8,128)S(1)}, f32[3,128,128]{2,1,0:T(8,128)S(1)}, f32[3,128,128]{2,1,0:T(8,128)S(1)}, f32[3,128,128]{2,1,0:T(8,128)S(1)}) custom-call(s32[3]{0:T(128)S(1)} %copy-done.7, s32[3]{0:T(128)S(1)} %copy-done.8, f32[32,128,128]{2,1,0:T(8,128)S(1)} %copy-done.3), custom_call_target="tpu_custom_call" | custom-call | tf_op jit(solution)/shard_map/gather_clean/pallas_call | solution.py:102
  26.6 2.9 %collective-permute-start.14 = (f32[3,128,128]{2,1,0:T(8,128)S(1)}, f32[3,128,128]{2,1,0:T(8,128)S(1)}, u32[]{:S(2)}, u32[]{:S(2)}) collective-permute-start(f32[3,128,128]{2,1,0:T(8,128)S(1)} %get-tuple-element.66), channel_id=1, source_target_pairs={{0,8},{8,0},{16,24},{24,16},{1,9},{9,1},{17,25},{25,17},{2,10},{10... | collective-permute-start | bytes 589832 | tf_op jit(solution)/shard_map/ppermute | solution.py:421
  30.3 2.5 %collective-permute-start.27 = (f32[2,64,128]{2,1,0:T(8,128)S(1)}, f32[2,64,128]{2,1,0:T(8,128)S(1)}, u32[]{:S(2)}, u32[]{:S(2)}) collective-permute-start(f32[2,64,128]{2,1,0:T(8,128)S(1)} %get-tuple-element.82), channel_id=1, source_target_pairs={{0,1},{1,0},{2,3},{3,2},{4,5},{5,4},{6,7},{7,6},{8,9},{9,8},{10,11... | collective-permute-start | bytes 196616 | tf_op jit(solution)/shard_map/ppermute | solution.py:421
  32.8 1.6 %collective-permute-start.28 = (f32[2,64,128]{2,1,0:T(8,128)S(1)}, f32[2,64,128]{2,1,0:T(8,128)S(1)}, u32[]{:S(2)}, u32[]{:S(2)}) collective-permute-start(f32[2,64,128]{2,1,0:T(8,128)S(1)} %get-tuple-element.83), channel_id=1, source_target_pairs={{0,2},{1,3},{2,0},{3,1},{4,6},{5,7},{6,4},{7,5},{8,10},{9,11},{10,... | collective-permute-start | bytes 196616 | tf_op jit(solution)/shard_map/ppermute | solution.py:421
  34.3 1.7 %collective-permute-start.15 = (f32[3,128,128]{2,1,0:T(8,128)S(1)}, f32[3,128,128]{2,1,0:T(8,128)S(1)}, u32[]{:S(2)}, u32[]{:S(2)}) collective-permute-start(f32[3,128,128]{2,1,0:T(8,128)S(1)} %get-tuple-element.67), channel_id=1, source_target_pairs={{0,16},{8,24},{16,0},{24,8},{1,17},{9,25},{17,1},{25,9},{2,18},{10... | collective-permute-start | bytes 589832 | tf_op jit(solution)/shard_map/ppermute | solution.py:421
  36.0 2.0 %collective-permute-start.29 = (f32[2,64,128]{2,1,0:T(8,128)S(1)}, f32[2,64,128]{2,1,0:T(8,128)S(1)}, u32[]{:S(2)}, u32[]{:S(2)}) collective-permute-start(f32[2,64,128]{2,1,0:T(8,128)S(1)} %get-tuple-element.84), channel_id=1, source_target_pairs={{0,3},{1,2},{2,1},{3,0},{4,7},{5,6},{6,5},{7,4},{8,11},{9,10},{10,... | collective-permute-start | bytes 196616 | tf_op jit(solution)/shard_map/ppermute | solution.py:421
  38.0 1.6 %collective-permute-start.30 = (f32[2,64,128]{2,1,0:T(8,128)S(1)}, f32[2,64,128]{2,1,0:T(8,128)S(1)}, u32[]{:S(2)}, u32[]{:S(2)}) collective-permute-start(f32[2,64,128]{2,1,0:T(8,128)S(1)} %get-tuple-element.85), channel_id=1, source_target_pairs={{0,4},{1,5},{2,6},{3,7},{4,0},{5,1},{6,2},{7,3},{8,12},{9,13},{10,... | collective-permute-start | bytes 196616 | tf_op jit(solution)/shard_map/ppermute | solution.py:421
  39.6 7.4 %fill.1 = (f32[3,128,128]{2,1,0:T(8,128)S(1)}, f32[3,128,128]{2,1,0:T(8,128)S(1)}, f32[3,128,128]{2,1,0:T(8,128)S(1)}, f32[3,128,128]{2,1,0:T(8,128)S(1)}) custom-call(s32[3]{0:T(128)S(1)} %copy-done.7, s32[3]{0:T(128)S(1)} %copy-done.8, s32[1]{0:T(128)S(6)} %copy.14.reach, f32[12,128,128]{2,1,0:T(8,128)S(1)} %get-tuple-element.47.v.v_in, ...), custom_call_target="tpu_custom_call" | custom-call | tf_op jit(solution)/shard_map/fill/pallas_call | solution.py:274
  47.2 1.7 %collective-permute-start.5 = (f32[3,128,128]{2,1,0:T(8,128)S(1)}, f32[3,128,128]{2,1,0:T(8,128)S(1)}, u32[]{:S(2)}, u32[]{:S(2)}) collective-permute-start(f32[3,128,128]{2,1,0:T(8,128)S(1)} %get-tuple-element.55), channel_id=1, source_target_pairs={{0,16},{8,24},{16,0},{24,8},{1,17},{9,25},{17,1},{25,9},{2,18},{10... | collective-permute-start | bytes 589832 | tf_op jit(solution)/shard_map/ppermute | solution.py:421
  50.3 2.5 %collective-permute-start.32 = (f32[2,64,128]{2,1,0:T(8,128)S(1)}, f32[2,64,128]{2,1,0:T(8,128)S(1)}, u32[]{:S(2)}, u32[]{:S(2)}) collective-permute-start(f32[2,64,128]{2,1,0:T(8,128)S(1)} %get-tuple-element.87), channel_id=1, source_target_pairs={{0,6},{1,7},{2,4},{3,5},{4,2},{5,3},{6,0},{7,1},{8,14},{9,15},{10,... | collective-permute-start | bytes 196616 | tf_op jit(solution)/shard_map/ppermute | solution.py:421
  53.9 4.6 %collective-permute-done.31.rest_5_ = f32[2,64,128]{2,1,0:T(8,128)S(1)} collective-permute-done((f32[2,64,128]{2,1,0:T(8,128)S(1)}, f32[2,64,128]{2,1,0:T(8,128)S(1)}, u32[]{:S(2)}, u32[]{:S(2)}) %collective-permute-start.31) | collective-permute-done | bytes 65568 | tf_op jit(solution)/shard_map/ppermute | solution.py:421
  59.5 2.6 %collective-permute-start.19 = (f32[3,64,128]{2,1,0:T(8,128)S(1)}, f32[3,64,128]{2,1,0:T(8,128)S(1)}, u32[]{:S(2)}, u32[]{:S(2)}) collective-permute-start(f32[3,64,128]{2,1,0:T(8,128)S(1)} %get-tuple-element.72), channel_id=1, source_target_pairs={{0,3},{1,2},{2,1},{3,0},{4,7},{5,6},{6,5},{7,4},{8,11},{9,10},{10,... | collective-permute-start | bytes 294920 | tf_op jit(solution)/shard_map/ppermute | solution.py:421
  62.0 2.7 %collective-permute-start.33 = (f32[2,64,128]{2,1,0:T(8,128)S(1)}, f32[2,64,128]{2,1,0:T(8,128)S(1)}, u32[]{:S(2)}, u32[]{:S(2)}) collective-permute-start(f32[2,64,128]{2,1,0:T(8,128)S(1)} %get-tuple-element.88), channel_id=1, source_target_pairs={{0,7},{1,6},{2,5},{3,4},{4,3},{5,2},{6,1},{7,0},{8,15},{9,14},{10,... | collective-permute-start | bytes 196616 | tf_op jit(solution)/shard_map/ppermute | solution.py:421
  65.9 3.4 %collective-permute-done.33.rest_7_ = f32[2,64,128]{2,1,0:T(8,128)S(1)} collective-permute-done((f32[2,64,128]{2,1,0:T(8,128)S(1)}, f32[2,64,128]{2,1,0:T(8,128)S(1)}, u32[]{:S(2)}, u32[]{:S(2)}) %collective-permute-start.33) | collective-permute-done | bytes 65568 | tf_op jit(solution)/shard_map/ppermute | solution.py:421
  69.3 3.5 %collective-permute-start.21 = (f32[3,64,128]{2,1,0:T(8,128)S(1)}, f32[3,64,128]{2,1,0:T(8,128)S(1)}, u32[]{:S(2)}, u32[]{:S(2)}) collective-permute-start(f32[3,64,128]{2,1,0:T(8,128)S(1)} %get-tuple-element.74), channel_id=1, source_target_pairs={{0,5},{1,4},{2,7},{3,6},{4,1},{5,0},{6,3},{7,2},{8,13},{9,12},{10,... | collective-permute-start | bytes 294920 | tf_op jit(solution)/shard_map/ppermute | solution.py:421
  72.8 1.7 %collective-permute-start.22 = (f32[3,64,128]{2,1,0:T(8,128)S(1)}, f32[3,64,128]{2,1,0:T(8,128)S(1)}, u32[]{:S(2)}, u32[]{:S(2)}) collective-permute-start(f32[3,64,128]{2,1,0:T(8,128)S(1)} %get-tuple-element.75), channel_id=1, source_target_pairs={{0,6},{1,7},{2,4},{3,5},{4,2},{5,3},{6,0},{7,1},{8,14},{9,15},{10,... | collective-permute-start | bytes 294920 | tf_op jit(solution)/shard_map/ppermute | solution.py:421
  74.5 2.3 %collective-permute-start.23 = (f32[3,64,128]{2,1,0:T(8,128)S(1)}, f32[3,64,128]{2,1,0:T(8,128)S(1)}, u32[]{:S(2)}, u32[]{:S(2)}) collective-permute-start(f32[3,64,128]{2,1,0:T(8,128)S(1)} %get-tuple-element.76), channel_id=1, source_target_pairs={{0,7},{1,6},{2,5},{3,4},{4,3},{5,2},{6,1},{7,0},{8,15},{9,14},{10,... | collective-permute-start | bytes 294920 | tf_op jit(solution)/shard_map/ppermute | solution.py:421
  76.8 3.7 %collective-permute-start.11 = (f32[3,64,128]{2,1,0:T(8,128)S(1)}, f32[3,64,128]{2,1,0:T(8,128)S(1)}, u32[]{:S(2)}, u32[]{:S(2)}) collective-permute-start(f32[3,64,128]{2,1,0:T(8,128)S(1)} %get-tuple-element.62), channel_id=1, source_target_pairs={{0,5},{1,4},{2,7},{3,6},{4,1},{5,0},{6,3},{7,2},{8,13},{9,12},{10,... | collective-permute-start | bytes 294920 | tf_op jit(solution)/shard_map/ppermute | solution.py:421
  80.5 8.7 %collective-permute-done.21.rest_5_ = f32[3,64,128]{2,1,0:T(8,128)S(1)} collective-permute-done((f32[3,64,128]{2,1,0:T(8,128)S(1)}, f32[3,64,128]{2,1,0:T(8,128)S(1)}, u32[]{:S(2)}, u32[]{:S(2)}) %collective-permute-start.21) | collective-permute-done | bytes 98336 | tf_op jit(solution)/shard_map/ppermute | solution.py:421
  89.2 2.1 %collective-permute-start.12 = (f32[3,64,128]{2,1,0:T(8,128)S(1)}, f32[3,64,128]{2,1,0:T(8,128)S(1)}, u32[]{:S(2)}, u32[]{:S(2)}) collective-permute-start(f32[3,64,128]{2,1,0:T(8,128)S(1)} %get-tuple-element.63), channel_id=1, source_target_pairs={{0,6},{1,7},{2,4},{3,5},{4,2},{5,3},{6,0},{7,1},{8,14},{9,15},{10,... | collective-permute-start | bytes 294920 | tf_op jit(solution)/shard_map/ppermute | solution.py:421
  91.3 1.6 %collective-permute-start.13 = (f32[3,64,128]{2,1,0:T(8,128)S(1)}, f32[3,64,128]{2,1,0:T(8,128)S(1)}, u32[]{:S(2)}, u32[]{:S(2)}) collective-permute-start(f32[3,64,128]{2,1,0:T(8,128)S(1)} %get-tuple-element.64), channel_id=1, source_target_pairs={{0,7},{1,6},{2,5},{3,4},{4,3},{5,2},{6,1},{7,0},{8,15},{9,14},{10,... | collective-permute-start | bytes 294920 | tf_op jit(solution)/shard_map/ppermute | solution.py:421
  92.9 1.6 %collective-permute-start.7 = (f32[3,64,128]{2,1,0:T(8,128)S(1)}, f32[3,64,128]{2,1,0:T(8,128)S(1)}, u32[]{:S(2)}, u32[]{:S(2)}) collective-permute-start(f32[3,64,128]{2,1,0:T(8,128)S(1)} %get-tuple-element.58), channel_id=1, source_target_pairs={{0,1},{1,0},{2,3},{3,2},{4,5},{5,4},{6,7},{7,6},{8,9},{9,8},{10,11... | collective-permute-start | bytes 294920 | tf_op jit(solution)/shard_map/ppermute | solution.py:421
  95.4 4.4 %collective-permute-done.11.rest_5_ = f32[3,64,128]{2,1,0:T(8,128)S(1)} collective-permute-done((f32[3,64,128]{2,1,0:T(8,128)S(1)}, f32[3,64,128]{2,1,0:T(8,128)S(1)}, u32[]{:S(2)}, u32[]{:S(2)}) %collective-permute-start.11) | collective-permute-done | bytes 98336 | tf_op jit(solution)/shard_map/ppermute | solution.py:421
  99.8 4.1 %along_y.3.rest_8_ = f32[8,64,1024]{2,1,0:T(8,128)} custom-call(s32[3]{0:T(128)S(1)} %copy-done.7, s32[3]{0:T(128)S(1)} %copy-done.8, bf16[1024,1024]{1,0:T(8,128)(2,1)S(1)} %copy-done, bf16[1024,1024]{1,0:T(8,128)(2,1)S(1)} %copy-done.1, f32[2,64,128]{2,1,0:T(8,128)S(1)} %get-tuple-element.81.rest_0_, f32[2,64,128]{2,1,0:T(8,128)S(1)} %collective-permute-done.27.rest_1_, ...), custom_call_target="tpu_custom_call" | custom-call | tf_op jit(solution)/shard_map/along_y/pallas_call | solution.py:397
  103.8 4.3 %along_y.4.rest_8_ = f32[8,64,1024]{2,1,0:T(8,128)} custom-call(s32[3]{0:T(128)S(1)} %copy-done.7, s32[3]{0:T(128)S(1)} %copy-done.8, bf16[1024,1024]{1,0:T(8,128)(2,1)S(1)} %copy-done, bf16[1024,1024]{1,0:T(8,128)(2,1)S(1)} %copy-done.1, f32[3,64,128]{2,1,0:T(8,128)S(1)} %get-tuple-element.69.rest_0_, ...), custom_call_target="tpu_custom_call", output_to_operand_aliasing={{}: (12, {})} | custom-call | tf_op jit(solution)/shard_map/along_y/pallas_call | solution.py:397
  108.2 4.3 %along_y.5 = f32[8,64,1024]{2,1,0:T(8,128)} custom-call(s32[3]{0:T(128)S(1)} %copy-done.7, s32[3]{0:T(128)S(1)} %copy-done.8, bf16[1024,1024]{1,0:T(8,128)(2,1)S(1)} %copy-done, bf16[1024,1024]{1,0:T(8,128)(2,1)S(1)} %copy-done.1, f32[3,64,128]{2,1,0:T(8,128)S(1)} %get-tuple-element.57.rest_0_, ...), custom_call_target="tpu_custom_call", output_to_operand_aliasing={{}: (12, {})} | custom-call | tf_op jit(solution)/shard_map/along_y/pallas_call | solution.py:397
  (65 shorter events, 12.8 us)
Async XLA Ops:
  4.4 22.3 %collective-permute-start.24 = (f32[2,128,128]{2,1,0:T(8,128)S(1)}, f32[2,128,128]{2,1,0:T(8,128)S(1)}, u32[]{:S(2)}, u32[]{:S(2)}) collective-permute-start(f32[2,128,128]{2,1,0:T(8,128)S(1)} %get-tuple-element.78), channel_id=1, source_target_pairs={{0,8},{8,0},{16,24},{24,16},{1,9},{9,1},{17,25},{25,17},{2,10},{10... | collective-permute-start | bytes 393224 | tf_op jit(solution)/shard_map/ppermute | solution.py:421
  4.9 24.7 %collective-permute-start.25 = (f32[2,128,128]{2,1,0:T(8,128)S(1)}, f32[2,128,128]{2,1,0:T(8,128)S(1)}, u32[]{:S(2)}, u32[]{:S(2)}) collective-permute-start(f32[2,128,128]{2,1,0:T(8,128)S(1)} %get-tuple-element.79), channel_id=1, source_target_pairs={{0,16},{8,24},{16,0},{24,8},{1,17},{9,25},{17,1},{25,9},{2,18},{10... | collective-permute-start | bytes 393224 | tf_op jit(solution)/shard_map/ppermute | solution.py:421
  7.5 22.1 %collective-permute-start.26 = (f32[2,128,128]{2,1,0:T(8,128)S(1)}, f32[2,128,128]{2,1,0:T(8,128)S(1)}, u32[]{:S(2)}, u32[]{:S(2)}) collective-permute-start(f32[2,128,128]{2,1,0:T(8,128)S(1)} %get-tuple-element.80), channel_id=1, source_target_pairs={{0,24},{8,16},{16,8},{24,0},{1,25},{9,17},{17,9},{25,1},{2,26},{10... | collective-permute-start | bytes 393224 | tf_op jit(solution)/shard_map/ppermute | solution.py:421
  16.0 6.2 %collective-permute-start.1 = (f32[1,128,128]{2,1,0:T(8,128)S(1)}, f32[1,128,128]{2,1,0:T(8,128)S(1)}, u32[]{:S(2)}, u32[]{:S(2)}) collective-permute-start(f32[1,128,128]{2,1,0:T(8,128)S(1)} %get-tuple-element.50), channel_id=1, source_target_pairs={{1,0},{2,1},{3,2},{4,3},{5,4},{6,5},{7,6},{9,8},{10,9},{11,10},{12... | collective-permute-start | bytes 196616 | tf_op jit(solution)/shard_map/ppermute | solution.py:431
  22.1 12.2 %collective-permute-start.2 = (f32[26,8,128]{2,1,0:T(8,128)S(1)}, f32[26,8,128]{2,1,0:T(8,128)S(1)}, u32[]{:S(2)}, u32[]{:S(2)}) collective-permute-start(f32[26,8,128]{2,1,0:T(8,128)S(1)} %get-tuple-element.51), channel_id=1, source_target_pairs={{0,8},{8,16},{16,24},{1,9},{9,17},{17,25},{2,10},{10,18},{18,26},{... | collective-permute-start | bytes 319496 | tf_op jit(solution)/shard_map/ppermute | solution.py:431
  23.5 12.5 %collective-permute-start.3 = (f32[26,8,128]{2,1,0:T(8,128)S(1)}, f32[26,8,128]{2,1,0:T(8,128)S(1)}, u32[]{:S(2)}, u32[]{:S(2)}) collective-permute-start(f32[26,8,128]{2,1,0:T(8,128)S(1)} %get-tuple-element.52), channel_id=1, source_target_pairs={{8,0},{16,8},{24,16},{9,1},{17,9},{25,17},{10,2},{18,10},{26,18},{... | collective-permute-start | bytes 319496 | tf_op jit(solution)/shard_map/ppermute | solution.py:431
  26.6 22.3 %collective-permute-start.14 = (f32[3,128,128]{2,1,0:T(8,128)S(1)}, f32[3,128,128]{2,1,0:T(8,128)S(1)}, u32[]{:S(2)}, u32[]{:S(2)}) collective-permute-start(f32[3,128,128]{2,1,0:T(8,128)S(1)} %get-tuple-element.66), channel_id=1, source_target_pairs={{0,8},{8,0},{16,24},{24,16},{1,9},{9,1},{17,25},{25,17},{2,10},{10... | collective-permute-start | bytes 589832 | tf_op jit(solution)/shard_map/ppermute | solution.py:421
  30.3 5.7 %collective-permute-start.27 = (f32[2,64,128]{2,1,0:T(8,128)S(1)}, f32[2,64,128]{2,1,0:T(8,128)S(1)}, u32[]{:S(2)}, u32[]{:S(2)}) collective-permute-start(f32[2,64,128]{2,1,0:T(8,128)S(1)} %get-tuple-element.82), channel_id=1, source_target_pairs={{0,1},{1,0},{2,3},{3,2},{4,5},{5,4},{6,7},{7,6},{8,9},{9,8},{10,11... | collective-permute-start | bytes 196616 | tf_op jit(solution)/shard_map/ppermute | solution.py:421
  34.3 14.7 %collective-permute-start.15 = (f32[3,128,128]{2,1,0:T(8,128)S(1)}, f32[3,128,128]{2,1,0:T(8,128)S(1)}, u32[]{:S(2)}, u32[]{:S(2)}) collective-permute-start(f32[3,128,128]{2,1,0:T(8,128)S(1)} %get-tuple-element.67), channel_id=1, source_target_pairs={{0,16},{8,24},{16,0},{24,8},{1,17},{9,25},{17,1},{25,9},{2,18},{10... | collective-permute-start | bytes 589832 | tf_op jit(solution)/shard_map/ppermute | solution.py:421
  36.0 14.3 %collective-permute-start.16 = (f32[3,128,128]{2,1,0:T(8,128)S(1)}, f32[3,128,128]{2,1,0:T(8,128)S(1)}, u32[]{:S(2)}, u32[]{:S(2)}) collective-permute-start(f32[3,128,128]{2,1,0:T(8,128)S(1)} %get-tuple-element.68), channel_id=1, source_target_pairs={{0,24},{8,16},{16,8},{24,0},{1,25},{9,17},{17,9},{25,1},{2,26},{10... | collective-permute-start | bytes 589832 | tf_op jit(solution)/shard_map/ppermute | solution.py:421
  36.0 11.1 %collective-permute-start.29 = (f32[2,64,128]{2,1,0:T(8,128)S(1)}, f32[2,64,128]{2,1,0:T(8,128)S(1)}, u32[]{:S(2)}, u32[]{:S(2)}) collective-permute-start(f32[2,64,128]{2,1,0:T(8,128)S(1)} %get-tuple-element.84), channel_id=1, source_target_pairs={{0,3},{1,2},{2,1},{3,0},{4,7},{5,6},{6,5},{7,4},{8,11},{9,10},{10,... | collective-permute-start | bytes 196616 | tf_op jit(solution)/shard_map/ppermute | solution.py:421
  38.0 9.1 %collective-permute-start.30 = (f32[2,64,128]{2,1,0:T(8,128)S(1)}, f32[2,64,128]{2,1,0:T(8,128)S(1)}, u32[]{:S(2)}, u32[]{:S(2)}) collective-permute-start(f32[2,64,128]{2,1,0:T(8,128)S(1)} %get-tuple-element.85), channel_id=1, source_target_pairs={{0,4},{1,5},{2,6},{3,7},{4,0},{5,1},{6,2},{7,3},{8,12},{9,13},{10,... | collective-permute-start | bytes 196616 | tf_op jit(solution)/shard_map/ppermute | solution.py:421
  47.1 12.4 %collective-permute-start.4 = (f32[3,128,128]{2,1,0:T(8,128)S(1)}, f32[3,128,128]{2,1,0:T(8,128)S(1)}, u32[]{:S(2)}, u32[]{:S(2)}) collective-permute-start(f32[3,128,128]{2,1,0:T(8,128)S(1)} %get-tuple-element.54), channel_id=1, source_target_pairs={{0,8},{8,0},{16,24},{24,16},{1,9},{9,1},{17,25},{25,17},{2,10},{10... | collective-permute-start | bytes 589832 | tf_op jit(solution)/shard_map/ppermute | solution.py:421
  47.2 14.9 %collective-permute-start.5 = (f32[3,128,128]{2,1,0:T(8,128)S(1)}, f32[3,128,128]{2,1,0:T(8,128)S(1)}, u32[]{:S(2)}, u32[]{:S(2)}) collective-permute-start(f32[3,128,128]{2,1,0:T(8,128)S(1)} %get-tuple-element.55), channel_id=1, source_target_pairs={{0,16},{8,24},{16,0},{24,8},{1,17},{9,25},{17,1},{25,9},{2,18},{10... | collective-permute-start | bytes 589832 | tf_op jit(solution)/shard_map/ppermute | solution.py:421
  48.9 13.2 %collective-permute-start.6 = (f32[3,128,128]{2,1,0:T(8,128)S(1)}, f32[3,128,128]{2,1,0:T(8,128)S(1)}, u32[]{:S(2)}, u32[]{:S(2)}) collective-permute-start(f32[3,128,128]{2,1,0:T(8,128)S(1)} %get-tuple-element.56), channel_id=1, source_target_pairs={{0,24},{8,16},{16,8},{24,0},{1,25},{9,17},{17,9},{25,1},{2,26},{10... | collective-permute-start | bytes 589832 | tf_op jit(solution)/shard_map/ppermute | solution.py:421
  49.0 9.5 %collective-permute-start.31 = (f32[2,64,128]{2,1,0:T(8,128)S(1)}, f32[2,64,128]{2,1,0:T(8,128)S(1)}, u32[]{:S(2)}, u32[]{:S(2)}) collective-permute-start(f32[2,64,128]{2,1,0:T(8,128)S(1)} %get-tuple-element.86), channel_id=1, source_target_pairs={{0,5},{1,4},{2,7},{3,6},{4,1},{5,0},{6,3},{7,2},{8,13},{9,12},{10,... | collective-permute-start | bytes 196616 | tf_op jit(solution)/shard_map/ppermute | solution.py:421
  50.3 8.9 %collective-permute-start.32 = (f32[2,64,128]{2,1,0:T(8,128)S(1)}, f32[2,64,128]{2,1,0:T(8,128)S(1)}, u32[]{:S(2)}, u32[]{:S(2)}) collective-permute-start(f32[2,64,128]{2,1,0:T(8,128)S(1)} %get-tuple-element.87), channel_id=1, source_target_pairs={{0,6},{1,7},{2,4},{3,5},{4,2},{5,3},{6,0},{7,1},{8,14},{9,15},{10,... | collective-permute-start | bytes 196616 | tf_op jit(solution)/shard_map/ppermute | solution.py:421
  58.5 14.3 %collective-permute-start.17 = (f32[3,64,128]{2,1,0:T(8,128)S(1)}, f32[3,64,128]{2,1,0:T(8,128)S(1)}, u32[]{:S(2)}, u32[]{:S(2)}) collective-permute-start(f32[3,64,128]{2,1,0:T(8,128)S(1)} %get-tuple-element.70), channel_id=1, source_target_pairs={{0,1},{1,0},{2,3},{3,2},{4,5},{5,4},{6,7},{7,6},{8,9},{9,8},{10,11... | collective-permute-start | bytes 294920 | tf_op jit(solution)/shard_map/ppermute | solution.py:421
  59.2 15.3 %collective-permute-start.18 = (f32[3,64,128]{2,1,0:T(8,128)S(1)}, f32[3,64,128]{2,1,0:T(8,128)S(1)}, u32[]{:S(2)}, u32[]{:S(2)}) collective-permute-start(f32[3,64,128]{2,1,0:T(8,128)S(1)} %get-tuple-element.71), channel_id=1, source_target_pairs={{0,2},{1,3},{2,0},{3,1},{4,6},{5,7},{6,4},{7,5},{8,10},{9,11},{10,... | collective-permute-start | bytes 294920 | tf_op jit(solution)/shard_map/ppermute | solution.py:421
  59.5 17.3 %collective-permute-start.19 = (f32[3,64,128]{2,1,0:T(8,128)S(1)}, f32[3,64,128]{2,1,0:T(8,128)S(1)}, u32[]{:S(2)}, u32[]{:S(2)}) collective-permute-start(f32[3,64,128]{2,1,0:T(8,128)S(1)} %get-tuple-element.72), channel_id=1, source_target_pairs={{0,3},{1,2},{2,1},{3,0},{4,7},{5,6},{6,5},{7,4},{8,11},{9,10},{10,... | collective-permute-start | bytes 294920 | tf_op jit(solution)/shard_map/ppermute | solution.py:421
  62.0 14.7 %collective-permute-start.20 = (f32[3,64,128]{2,1,0:T(8,128)S(1)}, f32[3,64,128]{2,1,0:T(8,128)S(1)}, u32[]{:S(2)}, u32[]{:S(2)}) collective-permute-start(f32[3,64,128]{2,1,0:T(8,128)S(1)} %get-tuple-element.73), channel_id=1, source_target_pairs={{0,4},{1,5},{2,6},{3,7},{4,0},{5,1},{6,2},{7,3},{8,12},{9,13},{10,... | collective-permute-start | bytes 294920 | tf_op jit(solution)/shard_map/ppermute | solution.py:421
  62.0 7.3 %collective-permute-start.33 = (f32[2,64,128]{2,1,0:T(8,128)S(1)}, f32[2,64,128]{2,1,0:T(8,128)S(1)}, u32[]{:S(2)}, u32[]{:S(2)}) collective-permute-start(f32[2,64,128]{2,1,0:T(8,128)S(1)} %get-tuple-element.88), channel_id=1, source_target_pairs={{0,7},{1,6},{2,5},{3,4},{4,3},{5,2},{6,1},{7,0},{8,15},{9,14},{10,... | collective-permute-start | bytes 196616 | tf_op jit(solution)/shard_map/ppermute | solution.py:421
  69.3 19.9 %collective-permute-start.21 = (f32[3,64,128]{2,1,0:T(8,128)S(1)}, f32[3,64,128]{2,1,0:T(8,128)S(1)}, u32[]{:S(2)}, u32[]{:S(2)}) collective-permute-start(f32[3,64,128]{2,1,0:T(8,128)S(1)} %get-tuple-element.74), channel_id=1, source_target_pairs={{0,5},{1,4},{2,7},{3,6},{4,1},{5,0},{6,3},{7,2},{8,13},{9,12},{10,... | collective-permute-start | bytes 294920 | tf_op jit(solution)/shard_map/ppermute | solution.py:421
  72.8 18.5 %collective-permute-start.22 = (f32[3,64,128]{2,1,0:T(8,128)S(1)}, f32[3,64,128]{2,1,0:T(8,128)S(1)}, u32[]{:S(2)}, u32[]{:S(2)}) collective-permute-start(f32[3,64,128]{2,1,0:T(8,128)S(1)} %get-tuple-element.75), channel_id=1, source_target_pairs={{0,6},{1,7},{2,4},{3,5},{4,2},{5,3},{6,0},{7,1},{8,14},{9,15},{10,... | collective-permute-start | bytes 294920 | tf_op jit(solution)/shard_map/ppermute | solution.py:421
  74.5 18.4 %collective-permute-start.23 = (f32[3,64,128]{2,1,0:T(8,128)S(1)}, f32[3,64,128]{2,1,0:T(8,128)S(1)}, u32[]{:S(2)}, u32[]{:S(2)}) collective-permute-start(f32[3,64,128]{2,1,0:T(8,128)S(1)} %get-tuple-element.76), channel_id=1, source_target_pairs={{0,7},{1,6},{2,5},{3,4},{4,3},{5,2},{6,1},{7,0},{8,15},{9,14},{10,... | collective-permute-start | bytes 294920 | tf_op jit(solution)/shard_map/ppermute | solution.py:421
  76.8 17.7 %collective-permute-start.10 = (f32[3,64,128]{2,1,0:T(8,128)S(1)}, f32[3,64,128]{2,1,0:T(8,128)S(1)}, u32[]{:S(2)}, u32[]{:S(2)}) collective-permute-start(f32[3,64,128]{2,1,0:T(8,128)S(1)} %get-tuple-element.61), channel_id=1, source_target_pairs={{0,4},{1,5},{2,6},{3,7},{4,0},{5,1},{6,2},{7,3},{8,12},{9,13},{10,... | collective-permute-start | bytes 294920 | tf_op jit(solution)/shard_map/ppermute | solution.py:421
  76.8 23.0 %collective-permute-start.11 = (f32[3,64,128]{2,1,0:T(8,128)S(1)}, f32[3,64,128]{2,1,0:T(8,128)S(1)}, u32[]{:S(2)}, u32[]{:S(2)}) collective-permute-start(f32[3,64,128]{2,1,0:T(8,128)S(1)} %get-tuple-element.62), channel_id=1, source_target_pairs={{0,5},{1,4},{2,7},{3,6},{4,1},{5,0},{6,3},{7,2},{8,13},{9,12},{10,... | collective-permute-start | bytes 294920 | tf_op jit(solution)/shard_map/ppermute | solution.py:421
  89.2 19.0 %collective-permute-start.12 = (f32[3,64,128]{2,1,0:T(8,128)S(1)}, f32[3,64,128]{2,1,0:T(8,128)S(1)}, u32[]{:S(2)}, u32[]{:S(2)}) collective-permute-start(f32[3,64,128]{2,1,0:T(8,128)S(1)} %get-tuple-element.63), channel_id=1, source_target_pairs={{0,6},{1,7},{2,4},{3,5},{4,2},{5,3},{6,0},{7,1},{8,14},{9,15},{10,... | collective-permute-start | bytes 294920 | tf_op jit(solution)/shard_map/ppermute | solution.py:421
  91.3 16.9 %collective-permute-start.13 = (f32[3,64,128]{2,1,0:T(8,128)S(1)}, f32[3,64,128]{2,1,0:T(8,128)S(1)}, u32[]{:S(2)}, u32[]{:S(2)}) collective-permute-start(f32[3,64,128]{2,1,0:T(8,128)S(1)} %get-tuple-element.64), channel_id=1, source_target_pairs={{0,7},{1,6},{2,5},{3,4},{4,3},{5,2},{6,1},{7,0},{8,15},{9,14},{10,... | collective-permute-start | bytes 294920 | tf_op jit(solution)/shard_map/ppermute | solution.py:421
  92.9 15.3 %collective-permute-start.7 = (f32[3,64,128]{2,1,0:T(8,128)S(1)}, f32[3,64,128]{2,1,0:T(8,128)S(1)}, u32[]{:S(2)}, u32[]{:S(2)}) collective-permute-start(f32[3,64,128]{2,1,0:T(8,128)S(1)} %get-tuple-element.58), channel_id=1, source_target_pairs={{0,1},{1,0},{2,3},{3,2},{4,5},{5,4},{6,7},{7,6},{8,9},{9,8},{10,11... | collective-permute-start | bytes 294920 | tf_op jit(solution)/shard_map/ppermute | solution.py:421
  94.5 13.8 %collective-permute-start.8 = (f32[3,64,128]{2,1,0:T(8,128)S(1)}, f32[3,64,128]{2,1,0:T(8,128)S(1)}, u32[]{:S(2)}, u32[]{:S(2)}) collective-permute-start(f32[3,64,128]{2,1,0:T(8,128)S(1)} %get-tuple-element.59), channel_id=1, source_target_pairs={{0,2},{1,3},{2,0},{3,1},{4,6},{5,7},{6,4},{7,5},{8,10},{9,11},{10,... | collective-permute-start | bytes 294920 | tf_op jit(solution)/shard_map/ppermute | solution.py:421
  99.7 8.5 %collective-permute-start.9 = (f32[3,64,128]{2,1,0:T(8,128)S(1)}, f32[3,64,128]{2,1,0:T(8,128)S(1)}, u32[]{:S(2)}, u32[]{:S(2)}) collective-permute-start(f32[3,64,128]{2,1,0:T(8,128)S(1)} %get-tuple-element.60), channel_id=1, source_target_pairs={{0,3},{1,2},{2,1},{3,0},{4,7},{5,6},{6,5},{7,4},{8,11},{9,10},{10,... | collective-permute-start | bytes 294920 | tf_op jit(solution)/shard_map/ppermute | solution.py:421
  (11 other events, 183.4 us)
where the time goes:
time: 112 us; the launch traced here: 113 us
  starting transfers between devices  52.3 us (47%)
  Pallas kernels  30.4 us (27%)
  waiting for transfers between devices  26 us (23%)
  local copies, waits for them, and re-layouts  2.93 us (3%)
    ppermute x30, starting transfers between devices, swap(): return lax.ppermute(value, axis, [(i, i ^ k) for i in range(size)])  44.6 us
    ppermute x30, waiting for transfers between devices, swap(): return lax.ppermute(value, axis, [(i, i ^ k) for i in range(size)])  21.2 us
    pallas_call x3, Pallas kernels, along_y(): pl.pallas_call(functools.partial(y_kernel, (parts, depth, step), slot, ch...  12.7 us
    ppermute x4, starting transfers between devices, shift(): lax.ppermute(value, axis, [(i, i + by) for i in range(size) if 0 <= i + b...  7.67 us
    pallas_call x1, Pallas kernels, fill(): pl.pallas_call(functools.partial(fill_kernel, (groups, depth, held) + ful...  7.42 us
    ppermute x4, waiting for transfers between devices, shift(): lax.ppermute(value, axis, [(i, i + by) for i in range(size) if 0 <= i + b...  4.86 us
    pallas_call x1, Pallas kernels, punch(): pl.pallas_call(functools.partial(punch_kernel, (groups, depth, held)), ou...  3.94 us
    pallas_call x2, Pallas kernels, gather_clean(): pl.pallas_call(functools.partial(gather_kernel, (groups, depth), slot, co...  3.31 us
  transfers between devices with their start and end apart: 34, of which 6 were waited for; matrix products, arithmetic and copies ran while one was open for 0% of the time, Pallas kernels for 22%

commit v1 on v0

--- a/solution.py
+++ b/solution.py
@@ -11,8 +11,9 @@
 
 MIN_SPACING = 10
 HALO = 3
+EARLY = 5
 LANES = 128
-VMEM_LIMIT = 40 * 1024 * 1024
+HBM = pl.BlockSpec(memory_space=pltpu.HBM)
 ANY = pl.BlockSpec(memory_space=pl.ANY)
 SMEM = pl.BlockSpec(memory_space=pltpu.SMEM)
 VMEM = pl.BlockSpec(memory_space=pltpu.VMEM)
@@ -21,11 +22,6 @@
 def hole_slots(depth):
     whole, left = divmod(depth, MIN_SPACING)
     return min(depth, 3 * whole + min(3, left))
-
-
-def clean_chunks(count):
-    first = min(2, count)
-    return [part for part in (first, count - first) if part]
 
 
 @functools.lru_cache(maxsize=None)
@@ -43,8 +39,23 @@
     return high, (value - high.astype(jnp.float32)).astype(jnp.bfloat16)
 
 
-def params(**more):
-    return pltpu.CompilerParams(vmem_limit_bytes=VMEM_LIMIT, **more)
+def params(length=0):
+    return pltpu.CompilerParams(vmem_limit_bytes=8 * 2**20 + 6 * length * length)
+
+
+def cost(micros):
+    return pl.CostEstimate(flops=0, bytes_accessed=int(micros * 3.6e6), transcendentals=0)
+
+
+TOKEN = jax.ShapeDtypeStruct((8, LANES), jnp.float32)
+
+
+def in_hbm(value):
+    return pltpu.with_memory_space_constraint(value, pltpu.HBM)
+
+
+def in_vmem(value):
+    return pltpu.with_memory_space_constraint(value, pltpu.VMEM)
 
 
 def floor_mod(value, by):
@@ -78,12 +89,9 @@
     return dist * dist
 
 
-def gather_kernel(sizes, slot, count, spacing, anchor, layers, *rest):
+def clean_copies(sizes, slot, count, table, layers, outs, sems):
     groups, depth = sizes
-    outs, (table, sems) = rest[:groups], rest[groups:]
     me = lax.axis_index("gx")
-    for group in range(groups):
-        order_layers(table, group * depth, group * depth, depth, spacing[0], anchor[0])
     copies = []
     for k in range(groups):
         for part in range(count):
@@ -91,6 +99,21 @@
             copies.append(
                 pltpu.make_async_copy(layers.at[layer], outs[k].at[part], sems.at[k * count + part])
             )
+    return copies
+
+
+def gather_kernel(sizes, slot, count, spacing_in, anchor_in, layers, *rest):
+    groups, depth = sizes
+    outs, (spacing, anchor, table, sems, small) = rest[:groups], rest[groups:]
+    first = pltpu.make_async_copy(spacing_in, spacing, small.at[0])
+    second = pltpu.make_async_copy(anchor_in, anchor, small.at[1])
+    first.start()
+    second.start()
+    first.wait()
+    second.wait()
+    for group in range(groups):
+        order_layers(table, group * depth, group * depth, depth, spacing[0], anchor[0])
+    copies = clean_copies(sizes, slot, count, table, layers, outs, sems)
     for copy in copies:
         copy.start()
     for copy in copies:
@@ -102,19 +125,25 @@
     return pl.pallas_call(
         functools.partial(gather_kernel, (groups, depth), slot, count),
         out_shape=[jax.ShapeDtypeStruct((count,) + layers.shape[1:], jnp.float32)] * groups,
-        in_specs=[SMEM, SMEM, ANY],
-        out_specs=[ANY] * groups,
+        in_specs=[HBM] * 3,
+        out_specs=[VMEM] * groups,
         scratch_shapes=[
+            pltpu.SMEM(spacing.shape, jnp.int32),
+            pltpu.SMEM(anchor.shape, jnp.int32),
             pltpu.SMEM((groups * depth,), jnp.int32),
             pltpu.SemaphoreType.DMA((groups * count,)),
+            pltpu.SemaphoreType.DMA((2,)),
         ],
         compiler_params=params(),
+        cost_estimate=cost(1.5),
         name="gather_clean",
-    )(spacing, anchor, layers)
-
-
-def punch_kernel(sizes, spacing, anchor, reach, layers, weights, v_out, w_out, first_out, last_out, table, sems):
+    )(in_hbm(spacing), in_hbm(anchor), in_hbm(layers))
+
+
+def punch_kernel(sizes, slot, count, spacing, anchor, reach, layers, weights, v_out, w_out, first_out, last_out, *rest):
     groups, depth, held = sizes
+    outs, (token, table, sems, more) = rest[: groups if count else 0], rest[-4:]
+    token[...] = jnp.zeros(token.shape, jnp.float32)
     rows = v_out.shape[1]
     total = groups * held
     x_start = lax.axis_index("gx") * rows
@@ -127,6 +156,9 @@
         copies.append(pltpu.make_async_copy(layers.at[layer], v_out.at[at], sems.at[at]))
         copies.append(pltpu.make_async_copy(weights.at[layer], w_out.at[at], sems.at[total + at]))
     for copy in copies:
+        copy.start()
+    others = clean_copies((groups, depth), slot, count, table, layers, outs, more) if count else []
+    for copy in others:
         copy.start()
     shape = (rows, LANES)
     x_at = x_start + lax.broadcasted_iota(jnp.int32, shape, 0)
@@ -156,28 +188,37 @@
         if place == per_pack - 1 or at == 2 * total - 1:
             first_out[at // per_pack] = first
             last_out[at // per_pack] = last
-
-
-def punch(spacing, anchor, reach, layers, weights, groups, held):
+    for copy in others:
+        copy.wait()
+
+
+def punch(spacing, anchor, reach, layers, weights, groups, held, slot, count):
     depth = layers.shape[0] // groups
     total = groups * held
     packs = -(-2 * total // (LANES // HALO))
     tile = layers.shape[1:]
     return pl.pallas_call(
-        functools.partial(punch_kernel, (groups, depth, held)),
-        out_shape=[jax.ShapeDtypeStruct((count,) + tile, jnp.float32) for count in (total, total, packs, packs)],
-        in_specs=[SMEM, SMEM, SMEM, ANY, ANY],
-        out_specs=[VMEM] * 4,
+        functools.partial(punch_kernel, (groups, depth, held), slot, count),
+        out_shape=[
+            pltpu.VMEM((size,) + tile, jnp.float32)
+            for size in [total, total, packs, packs] + ([count] * groups if count else [])
+        ]
+        + [TOKEN],
+        in_specs=[SMEM, SMEM, SMEM, HBM, HBM],
+        out_specs=[VMEM] * (5 + (groups if count else 0)),
         scratch_shapes=[
             pltpu.SMEM((groups * depth,), jnp.int32),
             pltpu.SemaphoreType.DMA((2 * total,)),
+            pltpu.SemaphoreType.DMA((groups * max(1, count),)),
         ],
         compiler_params=params(),
+        cost_estimate=cost(3.5),
         name="punch",
-    )(spacing, anchor, reach, layers, weights)
-
-
-def edge_kernel(v, w, left, right, top, bottom):
+    )(spacing, anchor, reach, in_hbm(layers), in_hbm(weights))
+
+
+def edge_kernel(v, w, left, right, *rest):
+    top, bottom = rest[-2:]
     rows = v.shape[1]
     at = 0
     for ref in (v, w, left, right):
@@ -187,21 +228,23 @@
         at += count
 
 
-def edges(v, w, left, right):
+def edges(v, w, left, right, after):
     count = 2 * (v.shape[0] + left.shape[0])
     return pl.pallas_call(
         edge_kernel,
         out_shape=[jax.ShapeDtypeStruct((count, 8, LANES), jnp.float32)] * 2,
-        in_specs=[VMEM] * 4,
+        in_specs=[VMEM] * 4 + [ANY] * len(after),
         out_specs=[VMEM] * 2,
         compiler_params=params(),
+        cost_estimate=cost(0.3),
         name="edges",
-    )(v, w, left, right)
+    )(in_vmem(v), in_vmem(w), left, right, *after)
 
 
 def fill_kernel(sizes, spacing, anchor, reach, v_in, w_in, left, right, above, below, *rest):
     groups, depth, held, full_x, full_y = sizes
-    outs, (table, result) = rest[:groups], rest[groups:]
+    outs, (token, table, result) = rest[-groups - 3 : -3], rest[-3:]
+    token[...] = jnp.zeros(token.shape, jnp.float32)
     total = groups * held
     packs = left.shape[0]
     rows = v_in.shape[1]
@@ -269,20 +312,21 @@
         outs[k][...] = result[pl.ds((me ^ k) * held, held)]
 
 
-def fill(spacing, anchor, reach, v, w, left, right, above, below, groups, held, depth, full):
+def fill(spacing, anchor, reach, v, w, left, right, above, below, groups, held, depth, full, after):
     rows = v.shape[1]
     return pl.pallas_call(
         functools.partial(fill_kernel, (groups, depth, held) + full),
-        out_shape=[jax.ShapeDtypeStruct((held, rows, LANES), jnp.float32)] * groups,
-        in_specs=[SMEM] * 3 + [VMEM] * 6,
-        out_specs=[VMEM] * groups,
+        out_shape=[jax.ShapeDtypeStruct((held, rows, LANES), jnp.float32)] * groups + [TOKEN],
+        in_specs=[SMEM] * 3 + [VMEM] * 6 + [ANY] * len(after),
+        out_specs=[VMEM] * (groups + 1),
         scratch_shapes=[
             pltpu.SMEM((groups * depth,), jnp.int32),
             pltpu.VMEM((groups * held, rows, LANES), jnp.float32),
         ],
         compiler_params=params(),
+        cost_estimate=cost(8.5),
         name="fill",
-    )(spacing, anchor, reach, v, w, left, right, above, below)
+    )(spacing, anchor, reach, in_vmem(v), in_vmem(w), left, right, above, below, *after)
 
 
 def dot3(a_high, a_low, b_high, b_low, dims):
@@ -292,117 +336,103 @@
     return dot(a_high, b_high) + (dot(a_high, b_low) + dot(a_low, b_high))
 
 
-def x_kernel(sizes, c_high, c_low, *rest):
-    groups, parts, step = sizes
-    pieces, outs = rest[:groups], rest[groups : groups + parts]
-    b_high, b_low, acc = rest[groups + parts :]
+def x_kernel(groups, step, c_high, c_low, *rest):
+    pieces, (out, token, b_high, b_low) = rest[:groups], rest[-4:]
+    token[...] = jnp.zeros(token.shape, jnp.float32)
     count, rows, _ = pieces[0].shape
-    out_rows = outs[0].shape[1]
+    parts, _, out_rows, _ = out.shape
     me = lax.axis_index("gx")
-    row = lax.axis_index("gy")
-    tile = pl.program_id(0)
-
-    @pl.when(tile == 0)
-    def _():
-        for k in range(groups):
-            at = pl.ds(pl.multiple_of((me ^ k) * rows, rows), rows)
+    for k in range(groups):
+        at = pl.ds(pl.multiple_of((me ^ k) * rows, rows), rows)
+        for layer in range(count):
+            high, low = split(pieces[k][layer])
+            cols = pl.ds(layer * LANES, LANES)
+            b_high[at, cols] = high
+            b_low[at, cols] = low
+    each = step // out_rows
+
+    def some(tile, carry):
+        at = pl.ds(pl.multiple_of(tile * step, step), step)
+        acc = dot3(c_high[at], c_low[at], b_high[...], b_low[...], ((1,), (0,)))
+        for part in range(each):
             for layer in range(count):
-                high, low = split(pieces[k][layer])
-                cols = pl.ds(layer * LANES, LANES)
-                b_high[at, cols] = high
-                b_low[at, cols] = low
-
-    at = pl.ds(pl.multiple_of(tile * step, step), step)
-    acc[at] = dot3(c_high[...], c_low[...], b_high[...], b_low[...], ((1,), (0,)))
-
-    @pl.when(tile == pl.num_programs(0) - 1)
-    def _():
-        for k in range(parts):
-            at = pl.ds(pl.multiple_of((row ^ k) * out_rows, out_rows), out_rows)
-            for layer in range(count):
-                outs[k][layer] = acc[at, pl.ds(layer * LANES, LANES)]
-
-
-def along_x(pieces, parts):
+                out[tile * each + part, layer] = acc[
+                    part * out_rows : (part + 1) * out_rows, layer * LANES : (layer + 1) * LANES
+                ]
+        return carry
+
+    lax.fori_loop(0, parts // each, some, 0)
+
+
+def along_x(pieces, parts, after):
     groups = len(pieces)
     count, rows, _ = pieces[0].shape
     length = rows * groups
     step = min(512, length)
     high, low = cosine_split(length)
-    whole = pl.BlockSpec(pieces[0].shape, lambda n: (0, 0, 0))
-    out_tile = (count, length // parts, LANES)
     return pl.pallas_call(
-        functools.partial(x_kernel, (groups, parts, step)),
-        grid=(length // step,),
-        out_shape=[jax.ShapeDtypeStruct(out_tile, jnp.float32)] * parts,
-        in_specs=[pl.BlockSpec((step, length), lambda n: (n, 0))] * 2 + [whole] * groups,
-        out_specs=[pl.BlockSpec(out_tile, lambda n: (0, 0, 0))] * parts,
+        functools.partial(x_kernel, groups, step),
+        out_shape=[pltpu.HBM((parts, count, length // parts, LANES), jnp.float32), TOKEN],
+        in_specs=[VMEM] * (2 + groups) + [ANY] * len(after),
+        out_specs=[VMEM, VMEM],
         scratch_shapes=[
             pltpu.VMEM((length, count * LANES), jnp.bfloat16),
             pltpu.VMEM((length, count * LANES), jnp.bfloat16),
-            pltpu.VMEM((length, count * LANES), jnp.float32),
         ],
-        compiler_params=params(),
+        compiler_params=params(length),
+        cost_estimate=cost(0.4 * count),
         name="along_x",
-    )(high, low, *pieces)
-
-
-def y_kernel(sizes, slot, chained, spacing, anchor, c_high, c_low, *rest):
-    parts, depth, step = sizes
-    pieces = rest[:parts]
-    out, a_high, a_low, acc, table, sems = rest[parts + (1 if chained else 0) :]
-    count, rows, _ = pieces[0].shape
-    row = lax.axis_index("gy")
-    tile = pl.program_id(0)
-
-    @pl.when(tile == 0)
-    def _():
-        order_layers(table, 0, lax.axis_index("gx") * depth, depth, spacing[0], anchor[0])
-        for k in range(parts):
-            cols = pl.ds(pl.multiple_of((row ^ k) * LANES, LANES), LANES)
-            for layer in range(count):
-                high, low = split(pieces[k][layer])
-                at = pl.ds(layer * rows, rows)
-                a_high[at, cols] = high
-                a_low[at, cols] = low
-
-    acc[tile] = dot3(a_high[...], a_low[...], c_high[...], c_low[...], ((1,), (1,)))
-
-    def copy(n, layer):
-        here = table[slot + layer] - lax.axis_index("gx") * depth
-        cols = pl.ds(pl.multiple_of(n * step, step), step)
+    )(high, low, *pieces, *after)
+
+
+def y_kernel(slot, step, chained, spacing, anchor, c_high, c_low, pieces, *rest):
+    out, token, a_high, a_low, acc, table, sems = rest[-7:]
+    token[...] = jnp.zeros(token.shape, jnp.float32)
+    parts, count, rows, _ = pieces.shape
+    depth = out.shape[0]
+    first = lax.axis_index("gx") * depth
+    order_layers(table, 0, first, depth, spacing[0], anchor[0])
+    for part in range(parts):
+        cols = pl.ds(part * LANES, LANES)
+        for layer in range(count):
+            high, low = split(pieces[part, layer])
+            at = pl.ds(layer * rows, rows)
+            a_high[at, cols] = high
+            a_low[at, cols] = low
+
+    def copy(tile, layer):
+        cols = pl.ds(pl.multiple_of(tile * step, step), step)
         return pltpu.make_async_copy(
-            acc.at[n, pl.ds(layer * rows, rows)], out.at[here, :, cols], sems.at[n, layer]
+            acc.at[tile, pl.ds(layer * rows, rows)],
+            out.at[table[slot + layer] - first, :, cols],
+            sems.at[tile, layer],
         )
 
-    for layer in range(count):
-        copy(tile, layer).start()
-
-    @pl.when(tile == pl.num_programs(0) - 1)
-    def _():
-        for n in range(acc.shape[0]):
-            for layer in range(count):
-                copy(n, layer).wait()
-
-
-def along_y(spacing, anchor, pieces, slot, depth, before):
-    parts = len(pieces)
-    count, rows, _ = pieces[0].shape
+    def some(tile, carry):
+        at = pl.ds(pl.multiple_of(tile * step, step), step)
+        acc[tile] = dot3(a_high[...], a_low[...], c_high[at], c_low[at], ((1,), (1,)))
+        for layer in range(count):
+            copy(tile, layer).start()
+        return carry
+
+    lax.fori_loop(0, acc.shape[0], some, 0)
+    for tile in range(acc.shape[0]):
+        for layer in range(count):
+            copy(tile, layer).wait()
+
+
+def along_y(spacing, anchor, pieces, slot, depth, before, after):
+    parts, count, rows, _ = pieces.shape
     length = parts * LANES
     step = min(256, length)
     steps = length // step
     high, low = cosine_split(length)
-    whole = pl.BlockSpec(pieces[0].shape, lambda n: (0, 0, 0))
     chained = before is not None
     return pl.pallas_call(
-        functools.partial(y_kernel, (parts, depth, step), slot, chained),
-        grid=(steps,),
-        out_shape=jax.ShapeDtypeStruct((depth, rows, length), jnp.float32),
-        in_specs=[SMEM, SMEM]
-        + [pl.BlockSpec((step, length), lambda n: (n, 0))] * 2
-        + [whole] * parts
-        + ([ANY] if chained else []),
-        out_specs=ANY,
+        functools.partial(y_kernel, slot, step, chained),
+        out_shape=[jax.ShapeDtypeStruct((depth, rows, length), jnp.float32), TOKEN],
+        in_specs=[SMEM, SMEM, VMEM, VMEM, VMEM] + ([HBM] if chained else []) + [ANY] * len(after),
+        out_specs=[HBM, VMEM],
         scratch_shapes=[
             pltpu.VMEM((count * rows, length), jnp.bfloat16),
             pltpu.VMEM((count * rows, length), jnp.bfloat16),
@@ -410,10 +440,11 @@
             pltpu.SMEM((depth,), jnp.int32),
             pltpu.SemaphoreType.DMA((steps, count)),
         ],
-        input_output_aliases={4 + parts: 0} if chained else {},
-        compiler_params=params(),
+        input_output_aliases={5: 0} if chained else {},
+        compiler_params=params(length),
+        cost_estimate=cost(1.0 * count),
         name="along_y",
-    )(spacing, anchor, high, low, *pieces, *([before] if chained else []))
+    )(spacing, anchor, high, low, pieces, *([before] if chained else []), *after)
 
 
 def swap(value, axis, k):
@@ -439,26 +470,42 @@
     held = hole_slots(depth)
     full = (rows * groups, LANES * parts)
 
+    clean = depth - held
+    early = min(EARLY, clean)
+    late = clean - early
+
+    def to_rows(value):
+        return lax.all_to_all(value, "gy", split_axis=0, concat_axis=0, tiled=True)
+
     chunks = []
-    slot = 0
-    for count in clean_chunks(depth - held):
-        gathered = gather_clean(spacing, anchor, intensity, groups, slot, count)
-        chunks.append((slot, exchange(gathered, "gx")))
-        slot += count
-
-    v, w, first, last = punch(spacing, anchor, reach, intensity, weight, groups, held)
+    if early:
+        gathered = gather_clean(spacing, anchor, intensity, groups, 0, early)
+        first_pieces = exchange(gathered, "gx")
+    v, w, first, last, *gathered, token = punch(
+        spacing, anchor, reach, intensity, weight, groups, held, early, late
+    )
     left = shift(last, "gy", 1)
     right = shift(first, "gy", -1)
-    top, bottom = edges(v, w, left, right)
+    if late:
+        late_pieces = exchange(gathered, "gx")
+    if early:
+        spectrum, token = along_x(first_pieces, parts, [left, right])
+        chunks.append((0, to_rows(spectrum)))
+    top, bottom = edges(v, w, left, right, [token])
     above = shift(bottom, "gx", 1)
     below = shift(top, "gx", -1)
-    filled = fill(spacing, anchor, reach, v, w, left, right, above, below, groups, held, depth, full)
-    chunks.append((slot, exchange(filled, "gx")))
-
-    moved = [(at, exchange(along_x(pieces, parts), "gy")) for at, pieces in chunks]
+    if late:
+        spectrum, token = along_x(late_pieces, parts, [token])
+        chunks.append((early, to_rows(spectrum)))
+    *filled, token = fill(
+        spacing, anchor, reach, v, w, left, right, above, below, groups, held, depth, full, [token]
+    )
+    pieces = exchange(filled, "gx")
+    spectrum, token = along_x(pieces, parts, [token])
+    chunks.append((clean, to_rows(spectrum)))
     out = None
-    for at, pieces in moved:
-        out = along_y(spacing, anchor, pieces, at, depth, out)
+    for slot, pieces in chunks:
+        out, token = along_y(spacing, anchor, pieces, slot, depth, out, [token])
     return out
 
 

time: 112 us -> 93.9 us (0.84); the launches traced: 113 us -> 93.3 us
  starting transfers between devices: 52.3 us -> 26.7 us
  waiting for transfers between devices: 26 us -> 34.4 us
  Pallas kernels: 30.4 us -> 28.2 us
    ppermute x30 -> x6, starting transfers between devices: 44.6 us -> 8.26 us  [swap(): return lax.ppermute(value, axis, [(i, i ^ k) for i in range(size)])]
    all_to_all x0 -> x2, waiting for transfers between devices: none -> 16.9 us  [to_rows(): return lax.all_to_all(value, 'gy', split_axis=0, concat_axis=0, tiled=True)]
    ppermute x30 -> x6, waiting for transfers between devices: 21.2 us -> 9.58 us  [swap(): return lax.ppermute(value, axis, [(i, i ^ k) for i in range(size)])]
    all_to_all x0 -> x2, starting transfers between devices: none -> 10.1 us  [to_rows(): return lax.all_to_all(value, 'gy', split_axis=0, concat_axis=0, tiled=True)]
    ppermute x4, waiting for transfers between devices: 4.86 us -> 7.87 us  [shift(): lax.ppermute(value, axis, [(i, i + by) for i in range(size) if 0 <= i + b...]
    pallas_call x7 -> x5, Pallas kernels: 19.7 us -> 18.4 us  [the longest x2 10 us: along_y(): pl.pallas_call(functools.partial(y_kernel, slot, step, chained), out_shap...]
    pallas_call x2 -> x1, Pallas kernels: 3.31 us -> 2.47 us  [gather_clean(): pl.pallas_call(functools.partial(gather_kernel, (groups, depth), slot, co...]
  transfers between devices with their start and end apart: 34 -> 12, of which waited for: 6 -> 8; matrix products, arithmetic and copies ran while one was open for 0% -> 0% of each run, Pallas kernels for 22% -> 19%
where the time goes in v1:
time: 93.9 us; the launch traced here: 93.3 us
  waiting for transfers between devices  34.4 us (37%)
  Pallas kernels  28.2 us (30%)
  starting transfers between devices  26.7 us (28%)
  local copies, waits for them, and re-layouts  3.22 us (3%)
    all_to_all x2, waiting for transfers between devices, to_rows(): return lax.all_to_all(value, 'gy', split_axis=0, concat_axis=0, tiled=True)  16.9 us
    all_to_all x2, starting transfers between devices, to_rows(): return lax.all_to_all(value, 'gy', split_axis=0, concat_axis=0, tiled=True)  10.1 us
    pallas_call x2, Pallas kernels, along_y(): pl.pallas_call(functools.partial(y_kernel, slot, step, chained), out_shap...  10 us
    ppermute x6, waiting for transfers between devices, swap(): return lax.ppermute(value, axis, [(i, i ^ k) for i in range(size)])  9.58 us
    ppermute x4, starting transfers between devices, shift(): lax.ppermute(value, axis, [(i, i + by) for i in range(size) if 0 <= i + b...  8.28 us
    ppermute x6, starting transfers between devices, swap(): return lax.ppermute(value, axis, [(i, i ^ k) for i in range(size)])  8.26 us
    ppermute x4, waiting for transfers between devices, shift(): lax.ppermute(value, axis, [(i, i + by) for i in range(size) if 0 <= i + b...  7.87 us
    pallas_call x1, Pallas kernels, fill(): pl.pallas_call(functools.partial(fill_kernel, (groups, depth, held) + ful...  7.36 us
  transfers between devices with their start and end apart: 12, of which 8 were waited for; matrix products, arithmetic and copies ran while one was open for 0% of the time, Pallas kernels for 19%

profile of v1, /device:TPU:0, one launch (start us, length us, event | category | flops | bytes accessed | tf_op | source)
XLA Modules:
  0.0 93.3 jit_solution(18373794963184280481)
XLA Ops:
  0.0 2.5 %gather_clean.1 = (f32[5,128,128]{2,1,0:T(8,128)S(1)}, f32[5,128,128]{2,1,0:T(8,128)S(1)}, f32[5,128,128]{2,1,0:T(8,128)S(1)}, f32[5,128,128]{2,1,0:T(8,128)S(1)}) custom-call(s32[3]{0:T(128)} %spacing.7, s32[3]{0:T(128)} %anchor.7, f32[32,128,128]{2,1,0:T(8,128)} %layers.3), custom_call_target="tpu_custom_call" | custom-call | bytes 5400000 | tf_op jit(solution)/shard_map/gather_clean/pallas_call | solution.py:125
  2.5 0.5 collective-permute-start.2
  3.0 2.6 %collective-permute-start.3 = (f32[5,128,128]{2,1,0:T(8,128)S(1)}, f32[5,128,128]{2,1,0:T(8,128)S(1)}, u32[]{:S(2)}, u32[]{:S(2)}) collective-permute-start(f32[5,128,128]{2,1,0:T(8,128)S(1)} %get-tuple-element.33), channel_id=1, source_target_pairs={{0,16},{8,24},{16,0},{24,8},{1,17},{9,25},{17,1},{25,9},{2,18},{10... | collective-permute-start | bytes 983048 | tf_op jit(solution)/shard_map/ppermute | solution.py:452
  5.6 0.1 collective-permute-start.4
  6.3 0.0 copy-start.3
  6.3 0.0 copy-start.5
  6.3 3.7 %punch.1 = (f32[12,128,128]{2,1,0:T(8,128)S(1)}, f32[12,128,128]{2,1,0:T(8,128)S(1)}, f32[1,128,128]{2,1,0:T(8,128)S(1)}, f32[1,128,128]{2,1,0:T(8,128)S(1)}, f32[8,128]{1,0:T(8,128)}) custom-call(s32[3]{0:T(128)S(1)} %copy-done.7, s32[3]{0:T(128)S(1)} %copy-done.8, s32[1]{0:T(128)S(6)} %copy.12.reach, f32[32,128,128]{2,1,0:T(8,128)} %layers.3, ...), custom_call_target="tpu_custom_call" | custom-call | bytes 12600000 | tf_op jit(solution)/shard_map/punch/pallas_call | solution.py:200
  10.0 3.7 %collective-permute-start = (f32[1,128,128]{2,1,0:T(8,128)S(1)}, f32[1,128,128]{2,1,0:T(8,128)S(1)}, u32[]{:S(2)}, u32[]{:S(2)}) collective-permute-start(f32[1,128,128]{2,1,0:T(8,128)S(1)} %get-tuple-element.29), channel_id=1, source_target_pairs={{0,1},{1,2},{2,3},{3,4},{4,5},{5,6},{6,7},{8,9},{9,10},{10,11},{11... | collective-permute-start | bytes 196616 | tf_op jit(solution)/shard_map/ppermute | solution.py:462
  13.7 1.3 %collective-permute-start.1 = (f32[1,128,128]{2,1,0:T(8,128)S(1)}, f32[1,128,128]{2,1,0:T(8,128)S(1)}, u32[]{:S(2)}, u32[]{:S(2)}) collective-permute-start(f32[1,128,128]{2,1,0:T(8,128)S(1)} %get-tuple-element.30), channel_id=1, source_target_pairs={{1,0},{2,1},{3,2},{4,3},{5,4},{6,5},{7,6},{9,8},{10,9},{11,10},{12... | collective-permute-start | bytes 196616 | tf_op jit(solution)/shard_map/ppermute | solution.py:462
  15.0 0.6 collective-permute-done.rest_4_.left
  15.6 4.3 %collective-permute-done.1.rest_5_.right = f32[1,128,128]{2,1,0:T(8,128)S(1)} collective-permute-done((f32[1,128,128]{2,1,0:T(8,128)S(1)}, f32[1,128,128]{2,1,0:T(8,128)S(1)}, u32[]{:S(2)}, u32[]{:S(2)}) %collective-permute-start.1) | collective-permute-done | bytes 65568 | tf_op jit(solution)/shard_map/ppermute | solution.py:462
  19.8 0.8 collective-permute-done.4.rest_3_
  20.6 2.6 %along_x.2 = (f32[8,5,64,128]{3,2,1,0:T(8,128)}, f32[8,128]{1,0:T(8,128)S(1)}) custom-call(bf16[512,512]{1,0:T(8,128)(2,1)S(1)} %copy-done.5, bf16[512,512]{1,0:T(8,128)(2,1)S(1)} %copy-done.3, f32[5,128,128]{2,1,0:T(8,128)S(1)} %get-tuple-element.31.rest_0_, f32[5,128,128]{2,1,0:T(8,128)S(1)} %collective-permute-done.2.rest_1_, ...), custom_call_target="tpu_custom_call" | custom-call | bytes 7200000 | tf_op jit(solution)/shard_map/along_x/pallas_call | solution.py:373
  23.3 5.9 %all-to-all-start.1 = ((f32[8,5,64,128]{3,2,1,0:T(8,128)}), f32[8,5,64,128]{3,2,1,0:T(8,128)S(1)}, u32[]{:S(2)}, u32[]{:S(2)}) async-start(f32[8,5,64,128]{3,2,1,0:T(8,128)} %get-tuple-element.44), calls=%async_computation.1 | async-start | bytes 2621440 | tf_op jit(solution)/shard_map/all_to_all | solution.py:478
  29.2 0.0 copy-start.6
  29.2 2.0 %collective-permute-start.5 = (f32[26,8,128]{2,1,0:T(8,128)S(1)}, f32[26,8,128]{2,1,0:T(8,128)S(1)}, u32[]{:S(2)}, u32[]{:S(2)}) collective-permute-start(f32[26,8,128]{2,1,0:T(8,128)S(1)} %get-tuple-element.36), channel_id=1, source_target_pairs={{0,8},{8,16},{16,24},{1,9},{9,17},{17,25},{2,10},{10,18},{18,26},{... | collective-permute-start | bytes 319496 | tf_op jit(solution)/shard_map/ppermute | solution.py:462
  31.3 1.3 %collective-permute-start.6 = (f32[26,8,128]{2,1,0:T(8,128)S(1)}, f32[26,8,128]{2,1,0:T(8,128)S(1)}, u32[]{:S(2)}, u32[]{:S(2)}) collective-permute-start(f32[26,8,128]{2,1,0:T(8,128)S(1)} %get-tuple-element.37), channel_id=1, source_target_pairs={{8,0},{16,8},{24,16},{9,1},{17,9},{25,17},{10,2},{18,10},{26,18},{... | collective-permute-start | bytes 319496 | tf_op jit(solution)/shard_map/ppermute | solution.py:462
  32.6 3.0 %collective-permute-done.6.below = f32[26,8,128]{2,1,0:T(8,128)S(1)} collective-permute-done((f32[26,8,128]{2,1,0:T(8,128)S(1)}, f32[26,8,128]{2,1,0:T(8,128)S(1)}, u32[]{:S(2)}, u32[]{:S(2)}) %collective-permute-start.6) | collective-permute-done | bytes 106528 | tf_op jit(solution)/shard_map/ppermute | solution.py:462
  35.6 7.4 %fill.1 = (f32[3,128,128]{2,1,0:T(8,128)S(1)}, f32[3,128,128]{2,1,0:T(8,128)S(1)}, f32[3,128,128]{2,1,0:T(8,128)S(1)}, f32[3,128,128]{2,1,0:T(8,128)S(1)}, f32[8,128]{1,0:T(8,128)S(1)}) custom-call(s32[3]{0:T(128)S(1)} %copy-done.7, s32[3]{0:T(128)S(1)} %copy-done.8, s32[1]{0:T(128)S(6)} %copy.12.reach, f32[12,128,128]{2,1,0:T(8,128)S(1)} %get-tuple-element.27.v.v_in, ...), custom_call_target="tpu_custom_call" | custom-call | bytes 30600000 | tf_op jit(solution)/shard_map/fill/pallas_call | solution.py:317
  43.0 3.7 %collective-permute-start.7 = (f32[3,128,128]{2,1,0:T(8,128)S(1)}, f32[3,128,128]{2,1,0:T(8,128)S(1)}, u32[]{:S(2)}, u32[]{:S(2)}) collective-permute-start(f32[3,128,128]{2,1,0:T(8,128)S(1)} %get-tuple-element.39), channel_id=1, source_target_pairs={{0,8},{8,0},{16,24},{24,16},{1,9},{9,1},{17,25},{25,17},{2,10},{10... | collective-permute-start | bytes 589832 | tf_op jit(solution)/shard_map/ppermute | solution.py:452
  46.6 1.4 %collective-permute-start.9 = (f32[3,128,128]{2,1,0:T(8,128)S(1)}, f32[3,128,128]{2,1,0:T(8,128)S(1)}, u32[]{:S(2)}, u32[]{:S(2)}) collective-permute-start(f32[3,128,128]{2,1,0:T(8,128)S(1)} %get-tuple-element.41), channel_id=1, source_target_pairs={{0,24},{8,16},{16,8},{24,0},{1,25},{9,17},{17,9},{25,1},{2,26},{10... | collective-permute-start | bytes 589832 | tf_op jit(solution)/shard_map/ppermute | solution.py:452
  48.1 6.3 %collective-permute-done.8.rest_2_ = f32[3,128,128]{2,1,0:T(8,128)S(1)} collective-permute-done((f32[3,128,128]{2,1,0:T(8,128)S(1)}, f32[3,128,128]{2,1,0:T(8,128)S(1)}, u32[]{:S(2)}, u32[]{:S(2)}) %collective-permute-start.8) | collective-permute-done | bytes 196640 | tf_op jit(solution)/shard_map/ppermute | solution.py:452
  54.4 2.5 %collective-permute-done.9.rest_3_ = f32[3,128,128]{2,1,0:T(8,128)S(1)} collective-permute-done((f32[3,128,128]{2,1,0:T(8,128)S(1)}, f32[3,128,128]{2,1,0:T(8,128)S(1)}, u32[]{:S(2)}, u32[]{:S(2)}) %collective-permute-start.9) | collective-permute-done | bytes 196640 | tf_op jit(solution)/shard_map/ppermute | solution.py:452
  56.9 2.0 %along_x.3 = (f32[8,3,64,128]{3,2,1,0:T(8,128)}, f32[8,128]{1,0:T(8,128)S(1)}) custom-call(bf16[512,512]{1,0:T(8,128)(2,1)S(1)} %copy-done.6, bf16[512,512]{1,0:T(8,128)(2,1)S(1)} %copy-done.4, f32[3,128,128]{2,1,0:T(8,128)S(1)} %get-tuple-element.38.rest_0_, f32[3,128,128]{2,1,0:T(8,128)S(1)} %collective-permute-done.7.rest_1_, ...), custom_call_target="tpu_custom_call" | custom-call | bytes 4320000 | tf_op jit(solution)/shard_map/along_x/pallas_call | solution.py:373
  58.9 2.1 %all-to-all-done.1.pieces = f32[8,5,64,128]{3,2,1,0:T(8,128)S(1)} async-done(((f32[8,5,64,128]{3,2,1,0:T(8,128)}), f32[8,5,64,128]{3,2,1,0:T(8,128)S(1)}, u32[]{:S(2)}, u32[]{:S(2)}) %all-to-all-start.1) | async-done | bytes 1310752 | tf_op jit(solution)/shard_map/all_to_all | solution.py:478
  61.0 4.2 %all-to-all-start = ((f32[8,3,64,128]{3,2,1,0:T(8,128)}), f32[8,3,64,128]{3,2,1,0:T(8,128)}, u32[]{:S(2)}, u32[]{:S(2)}) async-start(f32[8,3,64,128]{3,2,1,0:T(8,128)} %get-tuple-element.43), calls=%async_computation | async-start | bytes 1572864 | tf_op jit(solution)/shard_map/all_to_all | solution.py:478
  65.2 0.0 copy-start.1
  65.3 1.6 %copy-done.1 = bf16[1024,1024]{1,0:T(8,128)(2,1)S(1)} copy-done((bf16[1024,1024]{1,0:T(8,128)(2,1)S(1)}, bf16[1024,1024]{1,0:T(8,128)(2,1)}, u32[]{:S(2)}) %copy-start.1) | copy-done | bytes 2097176
  66.8 4.6 %along_y.2 = (f32[8,64,1024]{2,1,0:T(8,128)}, f32[8,128]{1,0:T(8,128)S(1)}) custom-call(s32[3]{0:T(128)S(1)} %copy-done.7, s32[3]{0:T(128)S(1)} %copy-done.8, bf16[1024,1024]{1,0:T(8,128)(2,1)S(1)} %copy-done.1, bf16[1024,1024]{1,0:T(8,128)(2,1)S(1)} %copy-done, f32[8,5,64,128]{3,2,1,0:T(8,128)S(1)} %all-to-all-done.1.pieces, ...), custom_call_target="tpu_custom_call" | custom-call | bytes 18000000 | tf_op jit(solution)/shard_map/along_y/pallas_call | solution.py:431
  71.5 14.8 %all-to-all-done.pieces = f32[8,3,64,128]{3,2,1,0:T(8,128)} async-done(((f32[8,3,64,128]{3,2,1,0:T(8,128)}), f32[8,3,64,128]{3,2,1,0:T(8,128)}, u32[]{:S(2)}, u32[]{:S(2)}) %all-to-all-start) | async-done | bytes 786464 | tf_op jit(solution)/shard_map/all_to_all | solution.py:478
  86.3 1.6 %copy-done.2 = bf16[1024,1024]{1,0:T(8,128)(2,1)S(1)} copy-done((bf16[1024,1024]{1,0:T(8,128)(2,1)S(1)}, bf16[1024,1024]{1,0:T(8,128)(2,1)}, u32[]{:S(2)}) %copy-start.2) | copy-done | bytes 2097176
  87.9 5.4 %along_y.3 = (f32[8,64,1024]{2,1,0:T(8,128)}, f32[8,128]{1,0:T(8,128)}) custom-call(s32[3]{0:T(128)S(1)} %copy-done.7, s32[3]{0:T(128)S(1)} %copy-done.8, bf16[1024,1024]{1,0:T(8,128)(2,1)S(1)} %copy-done.2, bf16[1024,1024]{1,0:T(8,128)(2,1)S(1)} %copy-done, f32[8,3,64,128]{3,2,1,0:T(8,128)} %all-to-all-done.pieces, ...), custom_call_target="tpu_custom_call", output_to_operand_aliasing={{0}: (5, {})} | custom-call | bytes 10800000 | tf_op jit(solution)/shard_map/along_y/pallas_call | solution.py:431
  (18 shorter events, 0.1 us)
Async XLA Ops:
  0.0 6.3 %copy-start.8 = (s32[3]{0:T(128)S(1)}, s32[3]{0:T(128)}, u32[]{:S(2)}) copy-start(s32[3]{0:T(128)} %anchor.7) | copy-start | bytes 40
  0.0 6.3 %copy-start.7 = (s32[3]{0:T(128)S(1)}, s32[3]{0:T(128)}, u32[]{:S(2)}) copy-start(s32[3]{0:T(128)} %spacing.7) | copy-start | bytes 40
  2.5 17.4 %collective-permute-start.2 = (f32[5,128,128]{2,1,0:T(8,128)S(1)}, f32[5,128,128]{2,1,0:T(8,128)S(1)}, u32[]{:S(2)}, u32[]{:S(2)}) collective-permute-start(f32[5,128,128]{2,1,0:T(8,128)S(1)} %get-tuple-element.32), channel_id=1, source_target_pairs={{0,8},{8,0},{16,24},{24,16},{1,9},{9,1},{17,25},{25,17},{2,10},{10... | collective-permute-start | bytes 983048 | tf_op jit(solution)/shard_map/ppermute | solution.py:452
  3.0 16.8 %collective-permute-start.3 = (f32[5,128,128]{2,1,0:T(8,128)S(1)}, f32[5,128,128]{2,1,0:T(8,128)S(1)}, u32[]{:S(2)}, u32[]{:S(2)}) collective-permute-start(f32[5,128,128]{2,1,0:T(8,128)S(1)} %get-tuple-element.33), channel_id=1, source_target_pairs={{0,16},{8,24},{16,0},{24,8},{1,17},{9,25},{17,1},{25,9},{2,18},{10... | collective-permute-start | bytes 983048 | tf_op jit(solution)/shard_map/ppermute | solution.py:452
  5.6 15.1 %collective-permute-start.4 = (f32[5,128,128]{2,1,0:T(8,128)S(1)}, f32[5,128,128]{2,1,0:T(8,128)S(1)}, u32[]{:S(2)}, u32[]{:S(2)}) collective-permute-start(f32[5,128,128]{2,1,0:T(8,128)S(1)} %get-tuple-element.34), channel_id=1, source_target_pairs={{0,24},{8,16},{16,8},{24,0},{1,25},{9,17},{17,9},{25,1},{2,26},{10... | collective-permute-start | bytes 983048 | tf_op jit(solution)/shard_map/ppermute | solution.py:452
  6.3 14.3 %copy-start.3 = (bf16[512,512]{1,0:T(8,128)(2,1)S(1)}, bf16[512,512]{1,0:T(8,128)(2,1)}, u32[]{:S(2)}) copy-start(bf16[512,512]{1,0:T(8,128)(2,1)} %constant.9.clone.c_low) | copy-start | bytes 1572868
  6.3 14.3 %copy-start.5 = (bf16[512,512]{1,0:T(8,128)(2,1)S(1)}, bf16[512,512]{1,0:T(8,128)(2,1)}, u32[]{:S(2)}) copy-start(bf16[512,512]{1,0:T(8,128)(2,1)} %constant.8.clone.c_high) | copy-start | bytes 1572868
  10.0 5.6 %collective-permute-start = (f32[1,128,128]{2,1,0:T(8,128)S(1)}, f32[1,128,128]{2,1,0:T(8,128)S(1)}, u32[]{:S(2)}, u32[]{:S(2)}) collective-permute-start(f32[1,128,128]{2,1,0:T(8,128)S(1)} %get-tuple-element.29), channel_id=1, source_target_pairs={{0,1},{1,2},{2,3},{3,4},{4,5},{5,6},{6,7},{8,9},{9,10},{10,11},{11... | collective-permute-start | bytes 196616 | tf_op jit(solution)/shard_map/ppermute | solution.py:462
  13.7 6.2 %collective-permute-start.1 = (f32[1,128,128]{2,1,0:T(8,128)S(1)}, f32[1,128,128]{2,1,0:T(8,128)S(1)}, u32[]{:S(2)}, u32[]{:S(2)}) collective-permute-start(f32[1,128,128]{2,1,0:T(8,128)S(1)} %get-tuple-element.30), channel_id=1, source_target_pairs={{1,0},{2,1},{3,2},{4,3},{5,4},{6,5},{7,6},{9,8},{10,9},{11,10},{12... | collective-permute-start | bytes 196616 | tf_op jit(solution)/shard_map/ppermute | solution.py:462
  23.3 37.7 %all-to-all-start.1 = ((f32[8,5,64,128]{3,2,1,0:T(8,128)}), f32[8,5,64,128]{3,2,1,0:T(8,128)S(1)}, u32[]{:S(2)}, u32[]{:S(2)}) async-start(f32[8,5,64,128]{3,2,1,0:T(8,128)} %get-tuple-element.44), calls=%async_computation.1 | async-start | bytes 2621440 | tf_op jit(solution)/shard_map/all_to_all | solution.py:478
  29.2 27.7 %copy-start.4 = (bf16[512,512]{1,0:T(8,128)(2,1)S(1)}, bf16[512,512]{1,0:T(8,128)(2,1)}, u32[]{:S(2)}) copy-start(bf16[512,512]{1,0:T(8,128)(2,1)} %constant.9.clone.c_low) | copy-start | bytes 1572868
  29.2 27.7 %copy-start.6 = (bf16[512,512]{1,0:T(8,128)(2,1)S(1)}, bf16[512,512]{1,0:T(8,128)(2,1)}, u32[]{:S(2)}) copy-start(bf16[512,512]{1,0:T(8,128)(2,1)} %constant.8.clone.c_high) | copy-start | bytes 1572868
  29.2 3.3 %collective-permute-start.5 = (f32[26,8,128]{2,1,0:T(8,128)S(1)}, f32[26,8,128]{2,1,0:T(8,128)S(1)}, u32[]{:S(2)}, u32[]{:S(2)}) collective-permute-start(f32[26,8,128]{2,1,0:T(8,128)S(1)} %get-tuple-element.36), channel_id=1, source_target_pairs={{0,8},{8,16},{16,24},{1,9},{9,17},{17,25},{2,10},{10,18},{18,26},{... | collective-permute-start | bytes 319496 | tf_op jit(solution)/shard_map/ppermute | solution.py:462
  31.3 4.3 %collective-permute-start.6 = (f32[26,8,128]{2,1,0:T(8,128)S(1)}, f32[26,8,128]{2,1,0:T(8,128)S(1)}, u32[]{:S(2)}, u32[]{:S(2)}) collective-permute-start(f32[26,8,128]{2,1,0:T(8,128)S(1)} %get-tuple-element.37), channel_id=1, source_target_pairs={{8,0},{16,8},{24,16},{9,1},{17,9},{25,17},{10,2},{18,10},{26,18},{... | collective-permute-start | bytes 319496 | tf_op jit(solution)/shard_map/ppermute | solution.py:462
  42.9 22.3 %copy-start = (bf16[1024,1024]{1,0:T(8,128)(2,1)S(1)}, bf16[1024,1024]{1,0:T(8,128)(2,1)}, u32[]{:S(2)}) copy-start(bf16[1024,1024]{1,0:T(8,128)(2,1)} %constant.11.clone.c_low) | copy-start | bytes 6291460
  43.0 5.1 %collective-permute-start.7 = (f32[3,128,128]{2,1,0:T(8,128)S(1)}, f32[3,128,128]{2,1,0:T(8,128)S(1)}, u32[]{:S(2)}, u32[]{:S(2)}) collective-permute-start(f32[3,128,128]{2,1,0:T(8,128)S(1)} %get-tuple-element.39), channel_id=1, source_target_pairs={{0,8},{8,0},{16,24},{24,16},{1,9},{9,1},{17,25},{25,17},{2,10},{10... | collective-permute-start | bytes 589832 | tf_op jit(solution)/shard_map/ppermute | solution.py:452
  46.6 7.8 %collective-permute-start.8 = (f32[3,128,128]{2,1,0:T(8,128)S(1)}, f32[3,128,128]{2,1,0:T(8,128)S(1)}, u32[]{:S(2)}, u32[]{:S(2)}) collective-permute-start(f32[3,128,128]{2,1,0:T(8,128)S(1)} %get-tuple-element.40), channel_id=1, source_target_pairs={{0,16},{8,24},{16,0},{24,8},{1,17},{9,25},{17,1},{25,9},{2,18},{10... | collective-permute-start | bytes 589832 | tf_op jit(solution)/shard_map/ppermute | solution.py:452
  46.6 10.2 %collective-permute-start.9 = (f32[3,128,128]{2,1,0:T(8,128)S(1)}, f32[3,128,128]{2,1,0:T(8,128)S(1)}, u32[]{:S(2)}, u32[]{:S(2)}) collective-permute-start(f32[3,128,128]{2,1,0:T(8,128)S(1)} %get-tuple-element.41), channel_id=1, source_target_pairs={{0,24},{8,16},{16,8},{24,0},{1,25},{9,17},{17,9},{25,1},{2,26},{10... | collective-permute-start | bytes 589832 | tf_op jit(solution)/shard_map/ppermute | solution.py:452
  61.0 25.3 %all-to-all-start = ((f32[8,3,64,128]{3,2,1,0:T(8,128)}), f32[8,3,64,128]{3,2,1,0:T(8,128)}, u32[]{:S(2)}, u32[]{:S(2)}) async-start(f32[8,3,64,128]{3,2,1,0:T(8,128)} %get-tuple-element.43), calls=%async_computation | async-start | bytes 1572864 | tf_op jit(solution)/shard_map/all_to_all | solution.py:478
  65.2 1.6 %copy-start.1 = (bf16[1024,1024]{1,0:T(8,128)(2,1)S(1)}, bf16[1024,1024]{1,0:T(8,128)(2,1)}, u32[]{:S(2)}) copy-start(bf16[1024,1024]{1,0:T(8,128)(2,1)} %constant.10.clone.c_high) | copy-start | bytes 6291460
  86.3 1.6 %copy-start.2 = (bf16[1024,1024]{1,0:T(8,128)(2,1)S(1)}, bf16[1024,1024]{1,0:T(8,128)(2,1)}, u32[]{:S(2)}) copy-start(bf16[1024,1024]{1,0:T(8,128)(2,1)} %constant.10.clone.c_high) | copy-start | bytes 6291460

commit v2 on v1

v2 whole, which is shorter than its diff:
```python
import functools
import math

import jax
import jax.numpy as jnp
import numpy as np
from jax import lax
from jax.experimental import pallas as pl
from jax.experimental.pallas import tpu as pltpu
from jax.sharding import PartitionSpec as P

MIN_SPACING = 10
HALO = 3
LANES = 128
PACK = LANES // (2 * HALO)
FIRST_APART = False
LAST_APART = True
EARLY = 5
HBM = pl.BlockSpec(memory_space=pltpu.HBM)
ANY = pl.BlockSpec(memory_space=pl.ANY)
SMEM = pl.BlockSpec(memory_space=pltpu.SMEM)
VMEM = pl.BlockSpec(memory_space=pltpu.VMEM)


def hole_slots(depth):
    whole, left = divmod(depth, MIN_SPACING)
    return min(depth, 3 * whole + min(3, left))


@functools.lru_cache(maxsize=None)
def cosine_split(length):
    freq = np.arange(length, dtype=np.int64)
    phase = (freq[:, None] * (2 * freq[None, :] + 1)) % (4 * length)
    matrix = np.cos(phase * (math.pi / (2 * length))) * math.sqrt(2.0 / length)
    high = matrix.astype(jnp.bfloat16)
    low = (matrix - high.astype(np.float64)).astype(jnp.bfloat16)
    return high, low


def split(value):
    high = value.astype(jnp.bfloat16)
    return high, (value - high.astype(jnp.float32)).astype(jnp.bfloat16)


def params(length=0):
    return pltpu.CompilerParams(vmem_limit_bytes=8 * 2**20 + 6 * length * length)


def cost(micros):
    return pl.CostEstimate(flops=0, bytes_accessed=int(micros * 3.6e6), transcendentals=0)


TOKEN = jax.ShapeDtypeStruct((8, LANES), jnp.float32)


def partner(n, size):
    return n if n < 3 else size + 2 - n


def in_hbm(value):
    return pltpu.with_memory_space_constraint(value, pltpu.HBM)


def in_vmem(value):
    return pltpu.with_memory_space_constraint(value, pltpu.VMEM)


def floor_mod(value, by):
    rest = lax.rem(value, by)
    return jnp.where(rest < 0, rest + by, rest)


def order_layers(table, at, first, depth, spacing, anchor):
    phase = floor_mod(first - anchor, spacing)
    front = jnp.int32(0)
    back = jnp.int32(depth - 1)
    for step in range(depth):
        hole = (phase <= 1) | (phase == spacing - 1)
        table[at + jnp.where(hole, back, front)] = first + step
        front = jnp.where(hole, front, front + 1)
        back = jnp.where(hole, back - 1, back)
        phase = jnp.where(phase + 1 == spacing, 0, phase + 1)


def is_hole_layer(layer, spacing, anchor):
    phase = floor_mod(layer - anchor, spacing)
    return (phase <= 1) | (phase == spacing - 1)


def squared_dist(position, spacing, anchor):
    step = spacing.astype(jnp.float32)
    from_anchor = (position - anchor).astype(jnp.float32)
    turns = jnp.floor((from_anchor + 0.5) / step)
    offset = from_anchor - turns * step
    dist = jnp.minimum(offset, step - offset)
    return dist * dist


def clean_copies(sizes, slot, count, table, layers, outs, sems):
    groups, depth = sizes
    me = lax.axis_index("gx")
    copies = []
    for k in range(groups):
        for part in range(count):
            layer = table[(me ^ partner(k, groups)) * depth + slot + part]
            copies.append(
                pltpu.make_async_copy(layers.at[layer], outs[k].at[part], sems.at[k * count + part])
            )
    return copies


def gather_kernel(sizes, slot, count, spacing_in, anchor_in, layers, *rest):
    groups, depth = sizes
    outs, (spacing, anchor, table, sems, small) = rest[:groups], rest[groups:]
    first = pltpu.make_async_copy(spacing_in, spacing, small.at[0])
    second = pltpu.make_async_copy(anchor_in, anchor, small.at[1])
    first.start()
    second.start()
    first.wait()
    second.wait()
    for group in range(groups):
        order_layers(table, group * depth, group * depth, depth, spacing[0], anchor[0])
    copies = clean_copies(sizes, slot, count, table, layers, outs, sems)
    for copy in copies:
        copy.start()
    for copy in copies:
        copy.wait()


def gather_clean(spacing, anchor, layers, groups, slot, count):
    depth = layers.shape[0] // groups
    return pl.pallas_call(
        functools.partial(gather_kernel, (groups, depth), slot, count),
        out_shape=[jax.ShapeDtypeStruct((count,) + layers.shape[1:], jnp.float32)] * groups,
        in_specs=[HBM] * 3,
        out_specs=[VMEM] * groups,
        scratch_shapes=[
            pltpu.SMEM(spacing.shape, jnp.int32),
            pltpu.SMEM(anchor.shape, jnp.int32),
            pltpu.SMEM((groups * depth,), jnp.int32),
            pltpu.SemaphoreType.DMA((groups * count,)),
            pltpu.SemaphoreType.DMA((2,)),
        ],
        compiler_params=params(),
        cost_estimate=cost(1.5),
        name="gather_clean",
    )(in_hbm(spacing), in_hbm(anchor), in_hbm(layers))


def punch_kernel(sizes, slot, count, spacing, anchor, reach, layers, weights, v_out, w_out, sides_out, *rest):
    groups, depth, held = sizes
    outs, (token, table, sems, more) = rest[: groups if count else 0], rest[-4:]
    token[...] = jnp.zeros(token.shape, jnp.float32)
    rows = v_out.shape[1]
    total = groups * held
    x_start = lax.axis_index("gx") * rows
    y_start = lax.axis_index("gy") * LANES
    for group in range(groups):
        order_layers(table, group * depth, group * depth, depth, spacing[0], anchor[0])
    copies = []
    for at in range(total):
        layer = table[(at // held) * depth + depth - held + at % held]
        copies.append(pltpu.make_async_copy(layers.at[layer], v_out.at[at], sems.at[at]))
        copies.append(pltpu.make_async_copy(weights.at[layer], w_out.at[at], sems.at[total + at]))
    for copy in copies:
        copy.start()
    others = clean_copies((groups, depth), slot, count, table, layers, outs, more) if count else []
    for copy in others:
        copy.start()
    shape = (rows, LANES)
    x_at = x_start + lax.broadcasted_iota(jnp.int32, shape, 0)
    lane = lax.broadcasted_iota(jnp.int32, shape, 1)
    plane = squared_dist(x_at, spacing[1], anchor[1]) + squared_dist(y_start + lane, spacing[2], anchor[2])
    flat = plane <= reach[0].astype(jnp.float32)
    for copy in copies:
        copy.wait()
    for at in range(total):
        layer = table[(at // held) * depth + depth - held + at % held]
        tall = jnp.where(is_hole_layer(layer, spacing[0], anchor[0]), 1.0, 0.0)
        v_out[at] = jnp.where(flat & (jnp.full(shape, tall) > 0.5), 0.0, v_out[at])
    for pack in range(sides_out.shape[1]):
        for kind, ref in enumerate((v_out, w_out)):
            tile = jnp.zeros(shape, jnp.float32)
            for at in range(pack * PACK, min(total, (pack + 1) * PACK)):
                place = 2 * HALO * (at % PACK)
                here = (lane >= place) & (lane < place + 2 * HALO)
                tile = jnp.where(here, pltpu.roll(ref[at], place + HALO, 1), tile)
            sides_out[kind, pack] = tile
    for copy in others:
        copy.wait()


def punch(spacing, anchor, reach, layers, weights, groups, held, slot, count):
    depth = layers.shape[0] // groups
    total = groups * held
    packs = -(-total // PACK)
    tile = layers.shape[1:]
    return pl.pallas_call(
        functools.partial(punch_kernel, (groups, depth, held), slot, count),
        out_shape=[
            pltpu.VMEM(size + tile, jnp.float32)
            for size in [(total,), (total,), (2, packs)] + ([(count,)] * groups if count else [])
        ]
        + [TOKEN],
        in_specs=[SMEM, SMEM, SMEM, HBM, HBM],
        out_specs=[VMEM] * (4 + (groups if count else 0)),
        scratch_shapes=[
            pltpu.SMEM((groups * depth,), jnp.int32),
            pltpu.SemaphoreType.DMA((2 * total,)),
            pltpu.SemaphoreType.DMA((groups * max(1, count),)),
        ],
        compiler_params=params(),
        cost_estimate=cost(3.5),
        name="punch",
    )(spacing, anchor, reach, in_hbm(layers), in_hbm(weights))


def edge_kernel(v, w, left, own, right, *rest):
    top, bottom = rest[-2:]
    rows = v.shape[1]
    at = 0
    for ref in (v, w, left, own, right):
        for array in [ref] if len(ref.shape) == 3 else [ref.at[0], ref.at[1]]:
            count = array.shape[0]
            top[at : at + count] = array[:, :8]
            bottom[at : at + count] = array[:, rows - 8 :]
            at += count


def edges(v, w, left, own, right, after):
    count = 2 * v.shape[0] + 6 * own.shape[1]
    return pl.pallas_call(
        edge_kernel,
        out_shape=[jax.ShapeDtypeStruct((count, 8, LANES), jnp.float32)] * 2,
        in_specs=[VMEM] * 5 + [ANY] * len(after),
        out_specs=[VMEM] * 2,
        compiler_params=params(),
        cost_estimate=cost(0.3),
        name="edges",
    )(in_vmem(v), in_vmem(w), left, own, right, *after)


def fill_kernel(sizes, spacing, anchor, reach, v_in, w_in, left, own, right, above, below, *rest):
    groups, depth, held, full_x, full_y = sizes
    outs, (token, table, result, beside) = rest[-groups - 4 : -4], rest[-4:]
    token[...] = jnp.zeros(token.shape, jnp.float32)
    total = groups * held
    packs = own.shape[1]
    rows = v_in.shape[1]
    me = lax.axis_index("gx")
    x_start = me * rows
    y_start = lax.axis_index("gy") * LANES
    for group in range(groups):
        order_layers(table, group * depth, group * depth, depth, spacing[0], anchor[0])
    tall = rows + 16
    shape = (tall, LANES)
    lane = lax.broadcasted_iota(jnp.int32, shape, 1)
    x_at = x_start - 8 + lax.broadcasted_iota(jnp.int32, shape, 0)
    x_dist = squared_dist(x_at, spacing[1], anchor[1])
    x_inside = (x_at >= 0) & (x_at < full_x)
    turn = jnp.floor((lane.astype(jnp.float32) + 0.5) * (0.5 / HALO))
    column = lane - 2 * HALO * turn.astype(jnp.int32)

    def holes_at(y_at):
        plane = x_dist + squared_dist(y_at, spacing[2], anchor[2])
        return (plane <= reach[0].astype(jnp.float32)) & x_inside & (y_at >= 0) & (y_at < full_y)

    def extended(ref, at, array):
        return jnp.concatenate([above[array], ref[at], below[array]], axis=0)

    def down_rows(value):
        return pltpu.roll(value, 1, 0) + (value + value) + pltpu.roll(value, tall - 1, 0)

    def lanes(value, by):
        return pltpu.roll(value, by % LANES, 1)

    def inverse_of(hole, total_weight):
        return 1.0 / jnp.where(hole, total_weight, 1.0)

    def across(value):
        return lanes(value, 1) + (value + value) + lanes(value, -1)

    inner = column < HALO
    for pack in range(packs):
        found = []
        for low, high, start in ((left, own, -HALO), (own, right, LANES - HALO)):
            tiles = []
            for kind in range(2):
                places = [
                    2 * total + (2 * {id(left): 0, id(own): 1, id(right): 2}[id(ref)] + kind) * packs + pack
                    for ref in (low, high)
                ]
                tiles.append(
                    jnp.where(
                        inner,
                        extended(low, (kind, pack), places[0]),
                        extended(high, (kind, pack), places[1]),
                    )
                )
            value, weight = tiles
            hole = holes_at(y_start + start + column)
            sums = down_rows(weight)
            kept = [sums]
            inverse = inverse_of(hole, across(sums))
            for sweep in range(3):
                sums = down_rows(weight * value)
                kept.append(sums)
                if sweep < 2:
                    value = jnp.where(hole, across(sums) * inverse, value)
            found.append(kept)
        for n in range(4):
            beside[pack, n] = jnp.where(column == HALO - 2, lanes(found[1][n], -2), found[0][n])

    flat = holes_at(y_start + lane)
    flat_f = jnp.where(flat, 1.0, 0.0)

    def one(index, carry):
        group = me ^ index
        values, weights, holes, edges_at = [], [], [], []
        for slot in range(held):
            at = group * held + slot
            layer = table[group * depth + depth - held + slot]
            swept = jnp.where(is_hole_layer(layer, spacing[0], anchor[0]), 1.0, 0.0)
            values.append(extended(v_in, at, at))
            weights.append(extended(w_in, at, total + at))
            holes.append(flat_f * swept > 0.5)
            to_edge = 2 * LANES - (2 * HALO * lax.rem(at, PACK) + HALO - 1)
            edges_at.append((lax.div(at, PACK), jnp.where(to_edge >= LANES, to_edge - LANES, to_edge)))

        def smooth(arrays, n):
            arrays = [down_rows(array) for array in arrays]
            edges = [pltpu.roll(beside[pack, n], to_edge, 1) for pack, to_edge in edges_at]
            before = [jnp.where(lane == 0, edge, lanes(array, 1)) for edge, array in zip(edges, arrays)]
            after = [jnp.where(lane == LANES - 1, edge, lanes(array, -1)) for edge, array in zip(edges, arrays)]
            return [low + (array + array) + high for low, array, high in zip(before, arrays, after)]

        inverses = [inverse_of(hole, value) for hole, value in zip(holes, smooth(weights, 0))]
        for sweep in range(3):
            sums = smooth([weight * value for weight, value in zip(weights, values)], sweep + 1)
            values = [
                jnp.where(hole, value * inverse, old)
                for hole, value, inverse, old in zip(holes, sums, inverses, values)
            ]
        for slot in range(held):
            result[index * held + slot] = values[slot][8 : 8 + rows]
        return carry

    lax.fori_loop(0, groups, one, 0)
    for n in range(groups):
        outs[n][...] = result[n * held : (n + 1) * held]


def fill(spacing, anchor, reach, v, w, sides, above, below, groups, held, depth, full, after):
    rows = v.shape[1]
    return pl.pallas_call(
        functools.partial(fill_kernel, (groups, depth, held) + full),
        out_shape=[jax.ShapeDtypeStruct((held, rows, LANES), jnp.float32)] * groups + [TOKEN],
        in_specs=[SMEM] * 3 + [VMEM] * 7 + [ANY] * len(after),
        out_specs=[VMEM] * (groups + 1),
        scratch_shapes=[
            pltpu.SMEM((groups * depth,), jnp.int32),
            pltpu.VMEM((groups * held, rows, LANES), jnp.float32),
            pltpu.VMEM((sides[0].shape[1], 4, rows + 16, LANES), jnp.float32),
        ],
        compiler_params=params(),
        cost_estimate=cost(7.0),
        name="fill",
    )(spacing, anchor, reach, in_vmem(v), in_vmem(w), *sides, above, below, *after)


def dot3(a_high, a_low, b_high, b_low, dims):
    def dot(a, b):
        return lax.dot_general(a, b, (dims, ((), ())), preferred_element_type=jnp.float32)

    return dot(a_high, b_high) + (dot(a_high, b_low) + dot(a_low, b_high))


def x_kernel(groups, made, step, c_high, c_low, *rest):
    pieces = rest[:groups]
    outs, (token, b_high, b_low, acc) = rest[-4 - made : -4], rest[-4:]
    token[...] = jnp.zeros(token.shape, jnp.float32)
    apart = len(outs) > 1
    count, rows, _ = pieces[0].shape
    out_rows = outs[0].shape[-2]
    length = c_high.shape[0]
    parts = length // out_rows
    me = lax.axis_index("gx")
    for k in range(groups):
        at = pl.ds(pl.multiple_of((me ^ partner(k, groups)) * rows, rows), rows)
        for layer in range(count):
            high, low = split(pieces[k][layer])
            cols = pl.ds(layer * LANES, LANES)
            b_high[at, cols] = high
            b_low[at, cols] = low
    each = step // out_rows

    def some(tile, carry):
        at = pl.ds(pl.multiple_of(tile * step, step), step)
        value = dot3(c_high[at], c_low[at], b_high[...], b_low[...], ((1,), (0,)))
        if apart:
            acc[at] = value
        else:
            for part in range(each):
                for layer in range(count):
                    outs[0][tile * each + part, layer] = value[
                        part * out_rows : (part + 1) * out_rows, layer * LANES : (layer + 1) * LANES
                    ]
        return carry

    lax.fori_loop(0, parts // each, some, 0)
    if apart:
        row = lax.axis_index("gy")
        for k in range(parts):
            at = pl.ds(pl.multiple_of((row ^ partner(k, parts)) * out_rows, out_rows), out_rows)
            for layer in range(count):
                outs[k][layer] = acc[at, pl.ds(layer * LANES, LANES)]


def along_x(pieces, parts, apart, after):
    groups = len(pieces)
    count, rows, _ = pieces[0].shape
    length = rows * groups
    step = min(512, length)
    high, low = cosine_split(length)
    tile = (count, length // parts, LANES)
    if apart:
        shapes = [jax.ShapeDtypeStruct(tile, jnp.float32)] * parts
    else:
        shapes = [pltpu.HBM((parts,) + tile, jnp.float32)]
    return pl.pallas_call(
        functools.partial(x_kernel, groups, len(shapes), step),
        out_shape=shapes + [TOKEN],
        in_specs=[VMEM] * (2 + groups) + [ANY] * len(after),
        out_specs=[VMEM] * (len(shapes) + 1),
        scratch_shapes=[
            pltpu.VMEM((length, count * LANES), jnp.bfloat16),
            pltpu.VMEM((length, count * LANES), jnp.bfloat16),
            pltpu.VMEM((length if apart else 8, count * LANES), jnp.float32),
        ],
        compiler_params=params(length),
        cost_estimate=cost(0.4 * count),
        name="along_x",
    )(high, low, *pieces, *after)


def column_tiles(length, step):
    return [part.T.reshape(length, -1, step).swapaxes(0, 1) for part in cosine_split(length)]


def keep_kernel(source, *rest):
    kept, token, sems = rest[-3:]
    token[...] = jnp.zeros(token.shape, jnp.float32)
    copies = [pltpu.make_async_copy(source.at[n], kept.at[n], sems.at[n]) for n in range(source.shape[0])]
    for copy in copies:
        copy.start()
    for copy in copies:
        copy.wait()


def kept_tiles(length, after):
    tiles = jnp.asarray(np.concatenate(column_tiles(length, min(256, length))))
    return pl.pallas_call(
        keep_kernel,
        out_shape=[pltpu.VMEM(tiles.shape, jnp.bfloat16), TOKEN],
        in_specs=[HBM] + [ANY] * len(after),
        out_specs=[VMEM, VMEM],
        scratch_shapes=[pltpu.SemaphoreType.DMA((tiles.shape[0],))],
        compiler_params=params(length),
        cost_estimate=cost(2.0),
        name="keep_tiles",
    )(in_hbm(tiles), *after)


def y_kernel(slot, chained, apart, spacing, anchor, cosines, *rest):
    out, token, a_high, a_low, acc, near, table, sems, more = rest[-9:]
    _, length, step = cosines.shape
    steps = length // step
    parts = length // LANES
    pieces = rest[: parts if apart else 1]
    token[...] = jnp.zeros(token.shape, jnp.float32)
    count, rows, _ = pieces[0].shape[-3:]
    depth = out.shape[0]
    if not apart:
        arrivals = [pltpu.make_async_copy(pieces[0].at[n], near.at[n], more.at[n]) for n in range(parts)]
        for arrival in arrivals:
            arrival.start()
    first = lax.axis_index("gx") * depth
    order_layers(table, 0, first, depth, spacing[0], anchor[0])
    row = lax.axis_index("gy")
    for part in range(parts):
        if apart:
            piece = pieces[part]
            cols = pl.ds(pl.multiple_of((row ^ partner(part, parts)) * LANES, LANES), LANES)
        else:
            arrivals[part].wait()
            piece = near.at[part]
            cols = pl.ds(part * LANES, LANES)
        for layer in range(count):
            high, low = split(piece[layer])
            at = pl.ds(layer * rows, rows)
            a_high[at, cols] = high
            a_low[at, cols] = low

    copies = []
    for tile in range(steps):
        acc[tile] = dot3(a_high[...], a_low[...], cosines[tile], cosines[steps + tile], ((1,), (0,)))
        for layer in range(count):
            copies.append(
                pltpu.make_async_copy(
                    acc.at[tile, pl.ds(layer * rows, rows)],
                    out.at[table[slot + layer] - first, :, pl.ds(tile * step, step)],
                    sems.at[tile, layer],
                )
            )
            copies[-1].start()
    for copy in copies:
        copy.wait()


def along_y(tiles, spacing, anchor, pieces, slot, depth, before, parts, after):
    apart = len(pieces) > 1
    count, rows, _ = pieces[0].shape[-3:]
    length = parts * LANES
    step = min(256, length)
    steps = length // step
    chained = before is not None
    near = (1, 8, LANES) if apart else pieces[0].shape[1:]
    pieces = pieces if apart else [in_hbm(pieces[0])]
    return pl.pallas_call(
        functools.partial(y_kernel, slot, chained, apart),
        out_shape=[jax.ShapeDtypeStruct((depth, rows, length), jnp.float32), TOKEN],
        in_specs=[SMEM, SMEM, VMEM]
        + [VMEM if apart else HBM] * len(pieces)
        + ([HBM] if chained else [])
        + [ANY] * len(after),
        out_specs=[HBM, VMEM],
        scratch_shapes=[
            pltpu.VMEM((count * rows, length), jnp.bfloat16),
            pltpu.VMEM((count * rows, length), jnp.bfloat16),
            pltpu.VMEM((steps, count * rows, step), jnp.float32),
            pltpu.VMEM((1 if apart else parts,) + near, jnp.float32),
            pltpu.SMEM((depth,), jnp.int32),
            pltpu.SemaphoreType.DMA((steps, count)),
            pltpu.SemaphoreType.DMA((parts,)),
        ],
        input_output_aliases={3 + len(pieces): 0} if chained else {},
        compiler_params=params(length),
        cost_estimate=cost(1.0 * count),
        name="along_y",
    )(spacing, anchor, in_vmem(tiles), *pieces, *([before] if chained else []), *after)


def swap(value, axis, k):
    size = lax.axis_size(axis)
    return lax.ppermute(value, axis, [(i, i ^ k) for i in range(size)])


def exchange(pieces, axis):
    size = len(pieces)
    return [pieces[0]] + [swap(pieces[n], axis, partner(n, size)) for n in range(1, size)]


def shift(value, axis, by):
    size = lax.axis_size(axis)
    return lax.ppermute(value, axis, [(i, i + by) for i in range(size) if 0 <= i + by < size])


def per_device(intensity, weight, spacing, anchor, reach):
    layers, rows, _ = intensity.shape
    groups = lax.axis_size("gx")
    parts = lax.axis_size("gy")
    depth = layers // groups
    held = hole_slots(depth)
    full = (rows * groups, LANES * parts)

    clean = depth - held
    early = min(EARLY, clean)
    late = clean - early

    def to_rows(spectrum, apart):
        if apart:
            return exchange(spectrum, "gy")
        return [lax.all_to_all(spectrum[0], "gy", split_axis=0, concat_axis=0, tiled=True)]

    chunks = []
    if early:
        gathered = gather_clean(spacing, anchor, intensity, groups, 0, early)
        first_pieces = exchange(gathered, "gx")
    v, w, own, *gathered, token = punch(
        spacing, anchor, reach, intensity, weight, groups, held, early, late
    )
    left = shift(own, "gy", 1)
    right = shift(own, "gy", -1)
    if late:
        late_pieces = exchange(gathered, "gx")
    if early:
        *spectrum, token = along_x(first_pieces, parts, FIRST_APART, [left, right])
        chunks.append((0, to_rows(spectrum, FIRST_APART)))
    top, bottom = edges(v, w, left, own, right, [token])
    above = shift(bottom, "gx", 1)
    below = shift(top, "gx", -1)
    *filled, token = fill(
        spacing, anchor, reach, v, w, (left, own, right), above, below, groups, held, depth, full, [token]
    )
    tiles, token = kept_tiles(full[1], [token])
    pieces = exchange([filled[partner(n, groups)] for n in range(groups)], "gx")
    *spectrum, token = along_x(pieces, parts, LAST_APART, [token])
    chunks.append((clean, to_rows(spectrum, LAST_APART)))
    out = None
    for slot, pieces in chunks:
        out, token = along_y(tiles, spacing, anchor, pieces, slot, depth, out, parts, [token])
    return out


def solution(mesh):
    in_specs = (P(None, "gx", "gy"), P(None, "gx", "gy"), P(), P(), P())
    out_specs = P("gx", "gy", None)
    return jax.shard_map(per_device, mesh=mesh, in_specs=in_specs, out_specs=out_specs, check_vma=False)
```

time: 93.9 us -> 83.8 us (0.89)
  waiting for transfers between devices: 34.4 us -> 18.4 us
  starting transfers between devices: 26.7 us -> 34.7 us
  Pallas kernels: 28.2 us -> 25.2 us
    all_to_all x2 -> x1, waiting for transfers between devices: 16.9 us -> 0.01 us  [to_rows(): lax.all_to_all(spectrum[0], 'gy', split_axis=0, concat_axis=0, tiled=True)]
    ppermute x6 -> x13, starting transfers between devices: 8.26 us -> 19.7 us  [swap(): return lax.ppermute(value, axis, [(i, i ^ k) for i in range(size)])]
    all_to_all x2 -> x1, starting transfers between devices: 10.1 us -> 5.91 us  [to_rows(): lax.all_to_all(spectrum[0], 'gy', split_axis=0, concat_axis=0, tiled=True)]
    pallas_call x1, Pallas kernels: 7.36 us -> 4.71 us  [fill(): pl.pallas_call(functools.partial(fill_kernel, (groups, depth, held) + ful...]
    ppermute x6 -> x13, waiting for transfers between devices: 9.58 us -> 10.6 us  [swap(): return lax.ppermute(value, axis, [(i, i ^ k) for i in range(size)])]
    unnamed x18 -> x12, local copies, waits for them, and re-layouts: 3.22 us -> 4.15 us
    pallas_call x4 -> x5, Pallas kernels: 14.7 us -> 14.9 us  [the longest x2 8.94 us: along_y(): pl.pallas_call(functools.partial(y_kernel, slot, chained, apart), out_sha...]
  transfers between devices with their start and end apart: 12 -> 18, of which waited for: 8 -> 8; matrix products, arithmetic and copies ran while one was open for 0% -> 0% of each run, Pallas kernels for 19% -> 20%
where the time goes in v2:
time: 83.8 us; the launch traced here: 83.3 us
  starting transfers between devices  34.7 us (41%)
  Pallas kernels  25.2 us (30%)
  waiting for transfers between devices  18.4 us (22%)
  local copies, waits for them, and re-layouts  4.15 us (5%)
    ppermute x13, starting transfers between devices, swap(): return lax.ppermute(value, axis, [(i, i ^ k) for i in range(size)])  19.7 us
    ppermute x13, waiting for transfers between devices, swap(): return lax.ppermute(value, axis, [(i, i ^ k) for i in range(size)])  10.6 us
    ppermute x4, starting transfers between devices, shift(): lax.ppermute(value, axis, [(i, i + by) for i in range(size) if 0 <= i + b...  9.04 us
    pallas_call x2, Pallas kernels, along_y(): pl.pallas_call(functools.partial(y_kernel, slot, chained, apart), out_sha...  8.94 us
    ppermute x4, waiting for transfers between devices, shift(): lax.ppermute(value, axis, [(i, i + by) for i in range(size) if 0 <= i + b...  7.79 us
    all_to_all x1, starting transfers between devices, to_rows(): lax.all_to_all(spectrum[0], 'gy', split_axis=0, concat_axis=0, tiled=True)  5.91 us
    pallas_call x1, Pallas kernels, fill(): pl.pallas_call(functools.partial(fill_kernel, (groups, depth, held) + ful...  4.71 us
    unnamed x12, local copies, waits for them, and re-layouts  4.15 us
  transfers between devices with their start and end apart: 18, of which 8 were waited for; matrix products, arithmetic and copies ran while one was open for 0% of the time, Pallas kernels for 20%

profile of v2, /device:TPU:0, one launch (start us, length us, event | category | flops | bytes accessed | tf_op | source)
XLA Modules:
  0.0 83.3 jit_solution(469069554085408123)
XLA Ops:
  0.0 2.5 %gather_clean.1 = (f32[5,128,128]{2,1,0:T(8,128)S(1)}, f32[5,128,128]{2,1,0:T(8,128)S(1)}, f32[5,128,128]{2,1,0:T(8,128)S(1)}, f32[5,128,128]{2,1,0:T(8,128)S(1)}) custom-call(s32[3]{0:T(128)} %spacing.7, s32[3]{0:T(128)} %anchor.7, f32[32,128,128]{2,1,0:T(8,128)} %layers.3), custom_call_target="tpu_custom_call" | custom-call | bytes 5400000 | tf_op jit(solution)/shard_map/gather_clean/pallas_call | solution.py:132
  3.0 2.6 %collective-permute-start.3 = (f32[5,128,128]{2,1,0:T(8,128)S(1)}, f32[5,128,128]{2,1,0:T(8,128)S(1)}, u32[]{:S(2)}, u32[]{:S(2)}) collective-permute-start(f32[5,128,128]{2,1,0:T(8,128)S(1)} %get-tuple-element.40), channel_id=1, source_target_pairs={{0,16},{8,24},{16,0},{24,8},{1,17},{9,25},{17,1},{25,9},{2,18},{10... | collective-permute-start | bytes 983048 | tf_op jit(solution)/shard_map/ppermute | solution.py:555
  6.3 3.1 %punch.1 = (f32[12,128,128]{2,1,0:T(8,128)S(1)}, f32[12,128,128]{2,1,0:T(8,128)S(1)}, f32[2,1,128,128]{3,2,1,0:T(8,128)S(1)}, f32[8,128]{1,0:T(8,128)}) custom-call(s32[3]{0:T(128)S(1)} %copy-done.4, s32[3]{0:T(128)S(1)} %copy-done.5, s32[1]{0:T(128)S(6)} %copy.11.reach, f32[32,128,128]{2,1,0:T(8,128)} %layers.3, f32[32,128,128]{2,1,0:T(8,128)} %weights.1), custom_call_target="tpu_custom_call" | custom-call | bytes 12600000 | tf_op jit(solution)/shard_map/punch/pallas_call | solution.py:198
  9.5 1.3 %collective-permute-start.1 = (f32[2,1,128,128]{3,2,1,0:T(8,128)S(1)}, f32[2,1,128,128]{3,2,1,0:T(8,128)S(1)}, u32[]{:S(2)}, u32[]{:S(2)}) collective-permute-start(f32[2,1,128,128]{3,2,1,0:T(8,128)S(1)} %get-tuple-element.37.own), channel_id=1, source_target_pairs={{1,0},{2,1},{3,2},{4,3},{5,4},{6,5},{7,6},{9,8},{10,9},{11,10},{12... | collective-permute-start | bytes 393224 | tf_op jit(solution)/shard_map/ppermute | solution.py:565
  10.8 4.6 %collective-permute-start = (f32[2,1,128,128]{3,2,1,0:T(8,128)S(1)}, f32[2,1,128,128]{3,2,1,0:T(8,128)S(1)}, u32[]{:S(2)}, u32[]{:S(2)}) collective-permute-start(f32[2,1,128,128]{3,2,1,0:T(8,128)S(1)} %get-tuple-element.37.own), channel_id=1, source_target_pairs={{0,1},{1,2},{2,3},{3,4},{4,5},{5,6},{6,7},{8,9},{9,10},{10,11},{11... | collective-permute-start | bytes 393224 | tf_op jit(solution)/shard_map/ppermute | solution.py:565
  15.3 1.8 %collective-permute-done.1.rest_5_.right = f32[2,1,128,128]{3,2,1,0:T(8,128)S(1)} collective-permute-done((f32[2,1,128,128]{3,2,1,0:T(8,128)S(1)}, f32[2,1,128,128]{3,2,1,0:T(8,128)S(1)}, u32[]{:S(2)}, u32[]{:S(2)}) %collective-permute-start.1) | collective-permute-done | bytes 131104 | tf_op jit(solution)/shard_map/ppermute | solution.py:565
  17.1 3.0 %collective-permute-done.rest_4_.left = f32[2,1,128,128]{3,2,1,0:T(8,128)S(1)} collective-permute-done((f32[2,1,128,128]{3,2,1,0:T(8,128)S(1)}, f32[2,1,128,128]{3,2,1,0:T(8,128)S(1)}, u32[]{:S(2)}, u32[]{:S(2)}) %collective-permute-start) | collective-permute-done | bytes 131104 | tf_op jit(solution)/shard_map/ppermute | solution.py:565
  20.1 0.5 collective-permute-done.4.rest_3_
  20.6 2.6 %along_x.2 = (f32[8,5,64,128]{3,2,1,0:T(8,128)}, f32[8,128]{1,0:T(8,128)S(1)}) custom-call(bf16[512,512]{1,0:T(8,128)(2,1)S(1)} %copy-done.3, bf16[512,512]{1,0:T(8,128)(2,1)S(1)} %copy-done.2, f32[5,128,128]{2,1,0:T(8,128)S(1)} %get-tuple-element.38.rest_0_, f32[5,128,128]{2,1,0:T(8,128)S(1)} %collective-permute-done.2.rest_1_, ...), custom_call_target="tpu_custom_call" | custom-call | bytes 7200000 | tf_op jit(solution)/shard_map/along_x/pallas_call | solution.py:430
  23.3 5.9 %all-to-all-start = ((f32[8,5,64,128]{3,2,1,0:T(8,128)}), f32[8,5,64,128]{3,2,1,0:T(8,128)}, u32[]{:S(2)}, u32[]{:S(2)}) async-start(f32[8,5,64,128]{3,2,1,0:T(8,128)} %get-tuple-element.60), calls=%async_computation | async-start | bytes 2621440 | tf_op jit(solution)/shard_map/all_to_all | solution.py:583
  29.2 1.9 %collective-permute-start.5 = (f32[30,8,128]{2,1,0:T(8,128)S(1)}, f32[30,8,128]{2,1,0:T(8,128)S(1)}, u32[]{:S(2)}, u32[]{:S(2)}) collective-permute-start(f32[30,8,128]{2,1,0:T(8,128)S(1)} %get-tuple-element.43), channel_id=1, source_target_pairs={{0,8},{8,16},{16,24},{1,9},{9,17},{17,25},{2,10},{10,18},{18,26},{... | collective-permute-start | bytes 368648 | tf_op jit(solution)/shard_map/ppermute | solution.py:565
  31.1 1.3 %collective-permute-start.6 = (f32[30,8,128]{2,1,0:T(8,128)S(1)}, f32[30,8,128]{2,1,0:T(8,128)S(1)}, u32[]{:S(2)}, u32[]{:S(2)}) collective-permute-start(f32[30,8,128]{2,1,0:T(8,128)S(1)} %get-tuple-element.44), channel_id=1, source_target_pairs={{8,0},{16,8},{24,16},{9,1},{17,9},{25,17},{10,2},{18,10},{26,18},{... | collective-permute-start | bytes 368648 | tf_op jit(solution)/shard_map/ppermute | solution.py:565
  32.4 3.0 %collective-permute-done.6.below = f32[30,8,128]{2,1,0:T(8,128)S(1)} collective-permute-done((f32[30,8,128]{2,1,0:T(8,128)S(1)}, f32[30,8,128]{2,1,0:T(8,128)S(1)}, u32[]{:S(2)}, u32[]{:S(2)}) %collective-permute-start.6) | collective-permute-done | bytes 122912 | tf_op jit(solution)/shard_map/ppermute | solution.py:565
  35.4 4.7 %fill.1 = (f32[3,128,128]{2,1,0:T(8,128)S(1)}, f32[3,128,128]{2,1,0:T(8,128)S(1)}, f32[3,128,128]{2,1,0:T(8,128)S(1)}, f32[3,128,128]{2,1,0:T(8,128)S(1)}, f32[8,128]{1,0:T(8,128)S(1)}) custom-call(s32[3]{0:T(128)S(1)} %copy-done.4, s32[3]{0:T(128)S(1)} %copy-done.5, s32[1]{0:T(128)S(6)} %copy.11.reach, f32[12,128,128]{2,1,0:T(8,128)S(1)} %get-tuple-element.35.v.v_in, ...), custom_call_target="tpu_custom_call" | custom-call | bytes 25200000 | tf_op jit(solution)/shard_map/fill/pallas_call | solution.py:355
  40.2 3.9 %collective-permute-start.7 = (f32[3,128,128]{2,1,0:T(8,128)S(1)}, f32[3,128,128]{2,1,0:T(8,128)S(1)}, u32[]{:S(2)}, u32[]{:S(2)}) collective-permute-start(f32[3,128,128]{2,1,0:T(8,128)S(1)} %get-tuple-element.48), channel_id=1, source_target_pairs={{0,8},{8,0},{16,24},{24,16},{1,9},{9,1},{17,25},{25,17},{2,10},{10... | collective-permute-start | bytes 589832 | tf_op jit(solution)/shard_map/ppermute | solution.py:555
  44.1 1.4 %collective-permute-start.9 = (f32[3,128,128]{2,1,0:T(8,128)S(1)}, f32[3,128,128]{2,1,0:T(8,128)S(1)}, u32[]{:S(2)}, u32[]{:S(2)}) collective-permute-start(f32[3,128,128]{2,1,0:T(8,128)S(1)} %get-tuple-element.50), channel_id=1, source_target_pairs={{0,24},{8,16},{16,8},{24,0},{1,25},{9,17},{17,9},{25,1},{2,26},{10... | collective-permute-start | bytes 589832 | tf_op jit(solution)/shard_map/ppermute | solution.py:555
  45.5 2.2 %keep_tiles.1 = (bf16[8,1024,256]{2,1,0:T(8,128)(2,1)S(1)}, f32[8,128]{1,0:T(8,128)S(1)}) custom-call(bf16[8,1024,256]{2,1,0:T(8,128)(2,1)} %constant.8.clone.source, f32[8,128]{1,0:T(8,128)S(1)} %get-tuple-element.45.rest_0_), custom_call_target="tpu_custom_call" | custom-call | bytes 7200000 | tf_op jit(solution)/shard_map/keep_tiles/pallas_call | solution.py:462
  47.8 1.9 %copy-done = bf16[8,1024,256]{2,1,0:T(8,128)(2,1)} copy-done((bf16[8,1024,256]{2,1,0:T(8,128)(2,1)}, bf16[8,1024,256]{2,1,0:T(8,128)(2,1)S(1)}, u32[]{:S(2)}) %copy-start) | copy-done | bytes 4194328
  49.7 2.1 %collective-permute-done.8.rest_2_ = f32[3,128,128]{2,1,0:T(8,128)S(1)} collective-permute-done((f32[3,128,128]{2,1,0:T(8,128)S(1)}, f32[3,128,128]{2,1,0:T(8,128)S(1)}, u32[]{:S(2)}, u32[]{:S(2)}) %collective-permute-start.8) | collective-permute-done | bytes 196640 | tf_op jit(solution)/shard_map/ppermute | solution.py:555
  51.9 2.5 %collective-permute-done.9.rest_3_ = f32[3,128,128]{2,1,0:T(8,128)S(1)} collective-permute-done((f32[3,128,128]{2,1,0:T(8,128)S(1)}, f32[3,128,128]{2,1,0:T(8,128)S(1)}, u32[]{:S(2)}, u32[]{:S(2)}) %collective-permute-start.9) | collective-permute-done | bytes 196640 | tf_op jit(solution)/shard_map/ppermute | solution.py:555
  54.3 1.1 %along_x.3 = (f32[3,64,128]{2,1,0:T(8,128)S(1)}, f32[3,64,128]{2,1,0:T(8,128)S(1)}, f32[3,64,128]{2,1,0:T(8,128)S(1)}, f32[3,64,128]{2,1,0:T(8,128)S(1)}, f32[3,...) custom-call(bf16[512,512]{1,0:T(8,128)(2,1)S(1)} %copy-done.3, ...), custom_call_target="tpu_custom_call" | custom-call | bytes 4320000 | tf_op jit(solution)/shard_map/along_x/pallas_call | solution.py:430
  55.5 2.1 %collective-permute-start.10 = (f32[3,64,128]{2,1,0:T(8,128)S(1)}, f32[3,64,128]{2,1,0:T(8,128)S(1)}, u32[]{:S(2)}, u32[]{:S(2)}) collective-permute-start(f32[3,64,128]{2,1,0:T(8,128)S(1)} %get-tuple-element.53), channel_id=1, source_target_pairs={{0,1},{1,0},{2,3},{3,2},{4,5},{5,4},{6,7},{7,6},{8,9},{9,8},{10,11... | collective-permute-start | bytes 294920 | tf_op jit(solution)/shard_map/ppermute | solution.py:555
  57.6 1.5 %collective-permute-start.11 = (f32[3,64,128]{2,1,0:T(8,128)S(1)}, f32[3,64,128]{2,1,0:T(8,128)S(1)}, u32[]{:S(2)}, u32[]{:S(2)}) collective-permute-start(f32[3,64,128]{2,1,0:T(8,128)S(1)} %get-tuple-element.54), channel_id=1, source_target_pairs={{0,2},{1,3},{2,0},{3,1},{4,6},{5,7},{6,4},{7,5},{8,10},{9,11},{10,... | collective-permute-start | bytes 294920 | tf_op jit(solution)/shard_map/ppermute | solution.py:555
  59.0 2.0 %collective-permute-start.12 = (f32[3,64,128]{2,1,0:T(8,128)S(1)}, f32[3,64,128]{2,1,0:T(8,128)S(1)}, u32[]{:S(2)}, u32[]{:S(2)}) collective-permute-start(f32[3,64,128]{2,1,0:T(8,128)S(1)} %get-tuple-element.55), channel_id=1, source_target_pairs={{0,7},{1,6},{2,5},{3,4},{4,3},{5,2},{6,1},{7,0},{8,15},{9,14},{10,... | collective-permute-start | bytes 294920 | tf_op jit(solution)/shard_map/ppermute | solution.py:555
  61.0 1.9 %collective-permute-start.13 = (f32[3,64,128]{2,1,0:T(8,128)S(1)}, f32[3,64,128]{2,1,0:T(8,128)S(1)}, u32[]{:S(2)}, u32[]{:S(2)}) collective-permute-start(f32[3,64,128]{2,1,0:T(8,128)S(1)} %get-tuple-element.56), channel_id=1, source_target_pairs={{0,6},{1,7},{2,4},{3,5},{4,2},{5,3},{6,0},{7,1},{8,14},{9,15},{10,... | collective-permute-start | bytes 294920 | tf_op jit(solution)/shard_map/ppermute | solution.py:555
  62.8 1.5 %collective-permute-start.14 = (f32[3,64,128]{2,1,0:T(8,128)S(1)}, f32[3,64,128]{2,1,0:T(8,128)S(1)}, u32[]{:S(2)}, u32[]{:S(2)}) collective-permute-start(f32[3,64,128]{2,1,0:T(8,128)S(1)} %get-tuple-element.57), channel_id=1, source_target_pairs={{0,5},{1,4},{2,7},{3,6},{4,1},{5,0},{6,3},{7,2},{8,13},{9,12},{10,... | collective-permute-start | bytes 294920 | tf_op jit(solution)/shard_map/ppermute | solution.py:555
  64.3 2.4 %collective-permute-start.15 = (f32[3,64,128]{2,1,0:T(8,128)S(1)}, f32[3,64,128]{2,1,0:T(8,128)S(1)}, u32[]{:S(2)}, u32[]{:S(2)}) collective-permute-start(f32[3,64,128]{2,1,0:T(8,128)S(1)} %get-tuple-element.58), channel_id=1, source_target_pairs={{0,4},{1,5},{2,6},{3,7},{4,0},{5,1},{6,2},{7,3},{8,12},{9,13},{10,... | collective-permute-start | bytes 294920 | tf_op jit(solution)/shard_map/ppermute | solution.py:555
  66.7 2.2 %copy-done.1 = bf16[8,1024,256]{2,1,0:T(8,128)(2,1)S(1)} copy-done((bf16[8,1024,256]{2,1,0:T(8,128)(2,1)S(1)}, bf16[8,1024,256]{2,1,0:T(8,128)(2,1)}, u32[]{:S(2)}) %copy-start.1) | copy-done | bytes 4194328
  68.9 5.3 %along_y.2 = (f32[8,64,1024]{2,1,0:T(8,128)}, f32[8,128]{1,0:T(8,128)S(1)}) custom-call(s32[3]{0:T(128)S(1)} %copy-done.4, s32[3]{0:T(128)S(1)} %copy-done.5, bf16[8,1024,256]{2,1,0:T(8,128)(2,1)S(1)} %copy-done.1, f32[8,5,64,128]{3,2,1,0:T(8,128)} %all-to-all-done.rest_0_, f32[8,128]{1,0:T(8,128)S(1)} %get-tuple-element.61.rest_1_), custom_call_target="tpu_custom_call" | custom-call | bytes 18000000 | tf_op jit(solution)/shard_map/along_y/pallas_call | solution.py:529
  74.2 4.0 %collective-permute-done.14.rest_5_ = f32[3,64,128]{2,1,0:T(8,128)S(1)} collective-permute-done((f32[3,64,128]{2,1,0:T(8,128)S(1)}, f32[3,64,128]{2,1,0:T(8,128)S(1)}, u32[]{:S(2)}, u32[]{:S(2)}) %collective-permute-start.14) | collective-permute-done | bytes 98336 | tf_op jit(solution)/shard_map/ppermute | solution.py:555
  78.1 1.5 %collective-permute-done.15.rest_6_ = f32[3,64,128]{2,1,0:T(8,128)S(1)} collective-permute-done((f32[3,64,128]{2,1,0:T(8,128)S(1)}, f32[3,64,128]{2,1,0:T(8,128)S(1)}, u32[]{:S(2)}, u32[]{:S(2)}) %collective-permute-start.15) | collective-permute-done | bytes 98336 | tf_op jit(solution)/shard_map/ppermute | solution.py:555
  79.6 3.7 %along_y.3 = (f32[8,64,1024]{2,1,0:T(8,128)}, f32[8,128]{1,0:T(8,128)}) custom-call(s32[3]{0:T(128)S(1)} %copy-done.4, s32[3]{0:T(128)S(1)} %copy-done.5, bf16[8,1024,256]{2,1,0:T(8,128)(2,1)S(1)} %copy-done.1, f32[3,64,128]{2,1,0:T(8,128)S(1)} %get-tuple-element.52.rest_0_, ...), custom_call_target="tpu_custom_call", output_to_operand_aliasing={{0}: (11, {})} | custom-call | bytes 10800000 | tf_op jit(solution)/shard_map/along_y/pallas_call | solution.py:529
  (25 shorter events, 0.7 us)
Async XLA Ops:
  0.0 6.3 %copy-start.5 = (s32[3]{0:T(128)S(1)}, s32[3]{0:T(128)}, u32[]{:S(2)}) copy-start(s32[3]{0:T(128)} %anchor.7) | copy-start | bytes 40
  0.0 6.3 %copy-start.4 = (s32[3]{0:T(128)S(1)}, s32[3]{0:T(128)}, u32[]{:S(2)}) copy-start(s32[3]{0:T(128)} %spacing.7) | copy-start | bytes 40
  2.5 17.6 %collective-permute-start.2 = (f32[5,128,128]{2,1,0:T(8,128)S(1)}, f32[5,128,128]{2,1,0:T(8,128)S(1)}, u32[]{:S(2)}, u32[]{:S(2)}) collective-permute-start(f32[5,128,128]{2,1,0:T(8,128)S(1)} %get-tuple-element.39), channel_id=1, source_target_pairs={{0,8},{8,0},{16,24},{24,16},{1,9},{9,1},{17,25},{25,17},{2,10},{10... | collective-permute-start | bytes 983048 | tf_op jit(solution)/shard_map/ppermute | solution.py:555
  3.0 17.1 %collective-permute-start.3 = (f32[5,128,128]{2,1,0:T(8,128)S(1)}, f32[5,128,128]{2,1,0:T(8,128)S(1)}, u32[]{:S(2)}, u32[]{:S(2)}) collective-permute-start(f32[5,128,128]{2,1,0:T(8,128)S(1)} %get-tuple-element.40), channel_id=1, source_target_pairs={{0,16},{8,24},{16,0},{24,8},{1,17},{9,25},{17,1},{25,9},{2,18},{10... | collective-permute-start | bytes 983048 | tf_op jit(solution)/shard_map/ppermute | solution.py:555
  5.6 15.1 %collective-permute-start.4 = (f32[5,128,128]{2,1,0:T(8,128)S(1)}, f32[5,128,128]{2,1,0:T(8,128)S(1)}, u32[]{:S(2)}, u32[]{:S(2)}) collective-permute-start(f32[5,128,128]{2,1,0:T(8,128)S(1)} %get-tuple-element.41), channel_id=1, source_target_pairs={{0,24},{8,16},{16,8},{24,0},{1,25},{9,17},{17,9},{25,1},{2,26},{10... | collective-permute-start | bytes 983048 | tf_op jit(solution)/shard_map/ppermute | solution.py:555
  6.3 14.3 %copy-start.2 = (bf16[512,512]{1,0:T(8,128)(2,1)S(1)}, bf16[512,512]{1,0:T(8,128)(2,1)}, u32[]{:S(2)}) copy-start(bf16[512,512]{1,0:T(8,128)(2,1)} %constant.7.clone.c_low) | copy-start | bytes 1572868
  6.3 14.3 %copy-start.3 = (bf16[512,512]{1,0:T(8,128)(2,1)S(1)}, bf16[512,512]{1,0:T(8,128)(2,1)}, u32[]{:S(2)}) copy-start(bf16[512,512]{1,0:T(8,128)(2,1)} %constant.6.clone.c_high) | copy-start | bytes 1572868
  9.5 7.7 %collective-permute-start.1 = (f32[2,1,128,128]{3,2,1,0:T(8,128)S(1)}, f32[2,1,128,128]{3,2,1,0:T(8,128)S(1)}, u32[]{:S(2)}, u32[]{:S(2)}) collective-permute-start(f32[2,1,128,128]{3,2,1,0:T(8,128)S(1)} %get-tuple-element.37.own), channel_id=1, source_target_pairs={{1,0},{2,1},{3,2},{4,3},{5,4},{6,5},{7,6},{9,8},{10,9},{11,10},{12... | collective-permute-start | bytes 393224 | tf_op jit(solution)/shard_map/ppermute | solution.py:565
  10.8 9.3 %collective-permute-start = (f32[2,1,128,128]{3,2,1,0:T(8,128)S(1)}, f32[2,1,128,128]{3,2,1,0:T(8,128)S(1)}, u32[]{:S(2)}, u32[]{:S(2)}) collective-permute-start(f32[2,1,128,128]{3,2,1,0:T(8,128)S(1)} %get-tuple-element.37.own), channel_id=1, source_target_pairs={{0,1},{1,2},{2,3},{3,4},{4,5},{5,6},{6,7},{8,9},{9,10},{10,11},{11... | collective-permute-start | bytes 393224 | tf_op jit(solution)/shard_map/ppermute | solution.py:565
  23.3 43.4 %all-to-all-start = ((f32[8,5,64,128]{3,2,1,0:T(8,128)}), f32[8,5,64,128]{3,2,1,0:T(8,128)}, u32[]{:S(2)}, u32[]{:S(2)}) async-start(f32[8,5,64,128]{3,2,1,0:T(8,128)} %get-tuple-element.60), calls=%async_computation | async-start | bytes 2621440 | tf_op jit(solution)/shard_map/all_to_all | solution.py:583
  29.2 3.2 %collective-permute-start.5 = (f32[30,8,128]{2,1,0:T(8,128)S(1)}, f32[30,8,128]{2,1,0:T(8,128)S(1)}, u32[]{:S(2)}, u32[]{:S(2)}) collective-permute-start(f32[30,8,128]{2,1,0:T(8,128)S(1)} %get-tuple-element.43), channel_id=1, source_target_pairs={{0,8},{8,16},{16,24},{1,9},{9,17},{17,25},{2,10},{10,18},{18,26},{... | collective-permute-start | bytes 368648 | tf_op jit(solution)/shard_map/ppermute | solution.py:565
  31.1 4.3 %collective-permute-start.6 = (f32[30,8,128]{2,1,0:T(8,128)S(1)}, f32[30,8,128]{2,1,0:T(8,128)S(1)}, u32[]{:S(2)}, u32[]{:S(2)}) collective-permute-start(f32[30,8,128]{2,1,0:T(8,128)S(1)} %get-tuple-element.44), channel_id=1, source_target_pairs={{8,0},{16,8},{24,16},{9,1},{17,9},{25,17},{10,2},{18,10},{26,18},{... | collective-permute-start | bytes 368648 | tf_op jit(solution)/shard_map/ppermute | solution.py:565
  40.2 9.5 %collective-permute-start.7 = (f32[3,128,128]{2,1,0:T(8,128)S(1)}, f32[3,128,128]{2,1,0:T(8,128)S(1)}, u32[]{:S(2)}, u32[]{:S(2)}) collective-permute-start(f32[3,128,128]{2,1,0:T(8,128)S(1)} %get-tuple-element.48), channel_id=1, source_target_pairs={{0,8},{8,0},{16,24},{24,16},{1,9},{9,1},{17,25},{25,17},{2,10},{10... | collective-permute-start | bytes 589832 | tf_op jit(solution)/shard_map/ppermute | solution.py:555
  44.1 7.8 %collective-permute-start.8 = (f32[3,128,128]{2,1,0:T(8,128)S(1)}, f32[3,128,128]{2,1,0:T(8,128)S(1)}, u32[]{:S(2)}, u32[]{:S(2)}) collective-permute-start(f32[3,128,128]{2,1,0:T(8,128)S(1)} %get-tuple-element.49), channel_id=1, source_target_pairs={{0,16},{8,24},{16,0},{24,8},{1,17},{9,25},{17,1},{25,9},{2,18},{10... | collective-permute-start | bytes 589832 | tf_op jit(solution)/shard_map/ppermute | solution.py:555
  44.1 10.2 %collective-permute-start.9 = (f32[3,128,128]{2,1,0:T(8,128)S(1)}, f32[3,128,128]{2,1,0:T(8,128)S(1)}, u32[]{:S(2)}, u32[]{:S(2)}) collective-permute-start(f32[3,128,128]{2,1,0:T(8,128)S(1)} %get-tuple-element.50), channel_id=1, source_target_pairs={{0,24},{8,16},{16,8},{24,0},{1,25},{9,17},{17,9},{25,1},{2,26},{10... | collective-permute-start | bytes 589832 | tf_op jit(solution)/shard_map/ppermute | solution.py:555
  47.7 2.0 %copy-start = (bf16[8,1024,256]{2,1,0:T(8,128)(2,1)}, bf16[8,1024,256]{2,1,0:T(8,128)(2,1)S(1)}, u32[]{:S(2)}) copy-start(bf16[8,1024,256]{2,1,0:T(8,128)(2,1)S(1)} %get-tuple-element.46.cosines) | copy-start | bytes 12582916
  55.5 8.8 %collective-permute-start.10 = (f32[3,64,128]{2,1,0:T(8,128)S(1)}, f32[3,64,128]{2,1,0:T(8,128)S(1)}, u32[]{:S(2)}, u32[]{:S(2)}) collective-permute-start(f32[3,64,128]{2,1,0:T(8,128)S(1)} %get-tuple-element.53), channel_id=1, source_target_pairs={{0,1},{1,0},{2,3},{3,2},{4,5},{5,4},{6,7},{7,6},{8,9},{9,8},{10,11... | collective-permute-start | bytes 294920 | tf_op jit(solution)/shard_map/ppermute | solution.py:555
  57.6 9.1 %collective-permute-start.11 = (f32[3,64,128]{2,1,0:T(8,128)S(1)}, f32[3,64,128]{2,1,0:T(8,128)S(1)}, u32[]{:S(2)}, u32[]{:S(2)}) collective-permute-start(f32[3,64,128]{2,1,0:T(8,128)S(1)} %get-tuple-element.54), channel_id=1, source_target_pairs={{0,2},{1,3},{2,0},{3,1},{4,6},{5,7},{6,4},{7,5},{8,10},{9,11},{10,... | collective-permute-start | bytes 294920 | tf_op jit(solution)/shard_map/ppermute | solution.py:555
  59.0 15.1 %collective-permute-start.12 = (f32[3,64,128]{2,1,0:T(8,128)S(1)}, f32[3,64,128]{2,1,0:T(8,128)S(1)}, u32[]{:S(2)}, u32[]{:S(2)}) collective-permute-start(f32[3,64,128]{2,1,0:T(8,128)S(1)} %get-tuple-element.55), channel_id=1, source_target_pairs={{0,7},{1,6},{2,5},{3,4},{4,3},{5,2},{6,1},{7,0},{8,15},{9,14},{10,... | collective-permute-start | bytes 294920 | tf_op jit(solution)/shard_map/ppermute | solution.py:555
  61.0 13.2 %collective-permute-start.13 = (f32[3,64,128]{2,1,0:T(8,128)S(1)}, f32[3,64,128]{2,1,0:T(8,128)S(1)}, u32[]{:S(2)}, u32[]{:S(2)}) collective-permute-start(f32[3,64,128]{2,1,0:T(8,128)S(1)} %get-tuple-element.56), channel_id=1, source_target_pairs={{0,6},{1,7},{2,4},{3,5},{4,2},{5,3},{6,0},{7,1},{8,14},{9,15},{10,... | collective-permute-start | bytes 294920 | tf_op jit(solution)/shard_map/ppermute | solution.py:555
  62.8 15.3 %collective-permute-start.14 = (f32[3,64,128]{2,1,0:T(8,128)S(1)}, f32[3,64,128]{2,1,0:T(8,128)S(1)}, u32[]{:S(2)}, u32[]{:S(2)}) collective-permute-start(f32[3,64,128]{2,1,0:T(8,128)S(1)} %get-tuple-element.57), channel_id=1, source_target_pairs={{0,5},{1,4},{2,7},{3,6},{4,1},{5,0},{6,3},{7,2},{8,13},{9,12},{10,... | collective-permute-start | bytes 294920 | tf_op jit(solution)/shard_map/ppermute | solution.py:555
  64.3 15.3 %collective-permute-start.15 = (f32[3,64,128]{2,1,0:T(8,128)S(1)}, f32[3,64,128]{2,1,0:T(8,128)S(1)}, u32[]{:S(2)}, u32[]{:S(2)}) collective-permute-start(f32[3,64,128]{2,1,0:T(8,128)S(1)} %get-tuple-element.58), channel_id=1, source_target_pairs={{0,4},{1,5},{2,6},{3,7},{4,0},{5,1},{6,2},{7,3},{8,12},{9,13},{10,... | collective-permute-start | bytes 294920 | tf_op jit(solution)/shard_map/ppermute | solution.py:555
  66.7 13.0 %collective-permute-start.16 = (f32[3,64,128]{2,1,0:T(8,128)S(1)}, f32[3,64,128]{2,1,0:T(8,128)S(1)}, u32[]{:S(2)}, u32[]{:S(2)}) collective-permute-start(f32[3,64,128]{2,1,0:T(8,128)S(1)} %get-tuple-element.59), channel_id=1, source_target_pairs={{0,3},{1,2},{2,1},{3,0},{4,7},{5,6},{6,5},{7,4},{8,11},{9,10},{10,... | collective-permute-start | bytes 294920 | tf_op jit(solution)/shard_map/ppermute | solution.py:555
  66.7 2.2 %copy-start.1 = (bf16[8,1024,256]{2,1,0:T(8,128)(2,1)S(1)}, bf16[8,1024,256]{2,1,0:T(8,128)(2,1)}, u32[]{:S(2)}) copy-start(bf16[8,1024,256]{2,1,0:T(8,128)(2,1)} %copy-done) | copy-start | bytes 12582916

commit v3 on v2

--- a/solution.py
+++ b/solution.py
@@ -57,6 +57,19 @@
     return n if n < 3 else size + 2 - n
 
 
+def column_of(lane):
+    turn = jnp.floor((lane.astype(jnp.float32) + 0.5) * (0.5 / HALO))
+    return lane - 2 * HALO * turn.astype(jnp.int32)
+
+
+def is_even(axis, shape):
+    return jnp.full(shape, lax.rem(lax.axis_index(axis), 2)) == 0
+
+
+def partners(size):
+    return [partner(n, size) for n in range(1, size)]
+
+
 def in_hbm(value):
     return pltpu.with_memory_space_constraint(value, pltpu.HBM)
 
@@ -96,22 +109,21 @@
     return dist * dist
 
 
-def clean_copies(sizes, slot, count, table, layers, outs, sems):
-    groups, depth = sizes
+def clean_copies(depth, some, slot, count, table, layers, outs, sems):
     me = lax.axis_index("gx")
     copies = []
-    for k in range(groups):
+    for n, k in enumerate(some):
         for part in range(count):
-            layer = table[(me ^ partner(k, groups)) * depth + slot + part]
+            layer = table[(me ^ k) * depth + slot + part]
             copies.append(
-                pltpu.make_async_copy(layers.at[layer], outs[k].at[part], sems.at[k * count + part])
+                pltpu.make_async_copy(layers.at[layer], outs[n].at[part], sems.at[n * count + part])
             )
     return copies
 
 
 def gather_kernel(sizes, slot, count, spacing_in, anchor_in, layers, *rest):
     groups, depth = sizes
-    outs, (spacing, anchor, table, sems, small) = rest[:groups], rest[groups:]
+    outs, (spacing, anchor, table, sems, small) = rest[:-5], rest[-5:]
     first = pltpu.make_async_copy(spacing_in, spacing, small.at[0])
     second = pltpu.make_async_copy(anchor_in, anchor, small.at[1])
     first.start()
@@ -120,7 +132,7 @@
     second.wait()
     for group in range(groups):
         order_layers(table, group * depth, group * depth, depth, spacing[0], anchor[0])
-    copies = clean_copies(sizes, slot, count, table, layers, outs, sems)
+    copies = clean_copies(depth, partners(groups), slot, count, table, layers, outs, sems)
     for copy in copies:
         copy.start()
     for copy in copies:
@@ -131,9 +143,9 @@
     depth = layers.shape[0] // groups
     return pl.pallas_call(
         functools.partial(gather_kernel, (groups, depth), slot, count),
-        out_shape=[jax.ShapeDtypeStruct((count,) + layers.shape[1:], jnp.float32)] * groups,
+        out_shape=[jax.ShapeDtypeStruct((count,) + layers.shape[1:], jnp.float32)] * (groups - 1),
         in_specs=[HBM] * 3,
-        out_specs=[VMEM] * groups,
+        out_specs=[VMEM] * (groups - 1),
         scratch_shapes=[
             pltpu.SMEM(spacing.shape, jnp.int32),
             pltpu.SMEM(anchor.shape, jnp.int32),
@@ -147,9 +159,9 @@
     )(in_hbm(spacing), in_hbm(anchor), in_hbm(layers))
 
 
-def punch_kernel(sizes, slot, count, spacing, anchor, reach, layers, weights, v_out, w_out, sides_out, *rest):
+def punch_kernel(sizes, early, late, spacing, anchor, reach, layers, weights, v_out, w_out, sides_out, one_out, other_out, *rest):
     groups, depth, held = sizes
-    outs, (token, table, sems, more) = rest[: groups if count else 0], rest[-4:]
+    outs, (token, table, sems, more, own_sems) = rest[:-5], rest[-5:]
     token[...] = jnp.zeros(token.shape, jnp.float32)
     rows = v_out.shape[1]
     total = groups * held
@@ -164,7 +176,12 @@
         copies.append(pltpu.make_async_copy(weights.at[layer], w_out.at[at], sems.at[total + at]))
     for copy in copies:
         copy.start()
-    others = clean_copies((groups, depth), slot, count, table, layers, outs, more) if count else []
+    others = []
+    if early:
+        others += clean_copies(depth, [0], 0, early, table, layers, outs[:1], own_sems)
+        outs = outs[1:]
+    if late:
+        others += clean_copies(depth, range(groups), early, late, table, layers, outs, more)
     for copy in others:
         copy.start()
     shape = (rows, LANES)
@@ -186,28 +203,37 @@
                 here = (lane >= place) & (lane < place + 2 * HALO)
                 tile = jnp.where(here, pltpu.roll(ref[at], place + HALO, 1), tile)
             sides_out[kind, pack] = tile
+        inner = column_of(lane) < HALO
+        value, weight = sides_out[0, pack], sides_out[1, pack]
+        to_right = jnp.where(inner, value, pltpu.roll(weight, HALO, 1))
+        to_left = jnp.where(inner, pltpu.roll(weight, LANES - HALO, 1), value)
+        even = is_even("gy", shape)
+        one_out[pack] = jnp.where(even, to_right, to_left)
+        other_out[pack] = jnp.where(even, to_left, to_right)
     for copy in others:
         copy.wait()
 
 
-def punch(spacing, anchor, reach, layers, weights, groups, held, slot, count):
+def punch(spacing, anchor, reach, layers, weights, groups, held, early, late):
     depth = layers.shape[0] // groups
     total = groups * held
     packs = -(-total // PACK)
     tile = layers.shape[1:]
+    clean = ([(early,)] if early else []) + ([(late,)] * groups if late else [])
     return pl.pallas_call(
-        functools.partial(punch_kernel, (groups, depth, held), slot, count),
+        functools.partial(punch_kernel, (groups, depth, held), early, late),
         out_shape=[
             pltpu.VMEM(size + tile, jnp.float32)
-            for size in [(total,), (total,), (2, packs)] + ([(count,)] * groups if count else [])
+            for size in [(total,), (total,), (2, packs), (packs,), (packs,)] + clean
         ]
         + [TOKEN],
         in_specs=[SMEM, SMEM, SMEM, HBM, HBM],
-        out_specs=[VMEM] * (4 + (groups if count else 0)),
+        out_specs=[VMEM] * (6 + len(clean)),
         scratch_shapes=[
             pltpu.SMEM((groups * depth,), jnp.int32),
             pltpu.SemaphoreType.DMA((2 * total,)),
-            pltpu.SemaphoreType.DMA((groups * max(1, count),)),
+            pltpu.SemaphoreType.DMA((groups * max(1, late),)),
+            pltpu.SemaphoreType.DMA((max(1, early),)),
         ],
         compiler_params=params(),
         cost_estimate=cost(3.5),
@@ -215,20 +241,26 @@
     )(spacing, anchor, reach, in_hbm(layers), in_hbm(weights))
 
 
-def edge_kernel(v, w, left, own, right, *rest):
-    top, bottom = rest[-2:]
+def edge_kernel(v, w, own, one, other, *rest):
+    outs = rest[-2:]
     rows = v.shape[1]
-    at = 0
-    for ref in (v, w, left, own, right):
-        for array in [ref] if len(ref.shape) == 3 else [ref.at[0], ref.at[1]]:
-            count = array.shape[0]
-            top[at : at + count] = array[:, :8]
-            bottom[at : at + count] = array[:, rows - 8 :]
-            at += count
-
-
-def edges(v, w, left, own, right, after):
-    count = 2 * v.shape[0] + 6 * own.shape[1]
+    even = lax.rem(lax.axis_index("gx"), 2)
+    for parity in range(2):
+
+        @pl.when(even == parity)
+        def _():
+            bottom, top = outs if parity == 0 else outs[::-1]
+            at = 0
+            for ref in (v, w, own, one, other):
+                for array in [ref] if len(ref.shape) == 3 else [ref.at[0], ref.at[1]]:
+                    count = array.shape[0]
+                    top[at : at + count] = array[:, :8]
+                    bottom[at : at + count] = array[:, rows - 8 :]
+                    at += count
+
+
+def edges(v, w, own, one, other, after):
+    count = 2 * v.shape[0] + 4 * own.shape[1]
     return pl.pallas_call(
         edge_kernel,
         out_shape=[jax.ShapeDtypeStruct((count, 8, LANES), jnp.float32)] * 2,
@@ -237,12 +269,13 @@
         compiler_params=params(),
         cost_estimate=cost(0.3),
         name="edges",
-    )(in_vmem(v), in_vmem(w), left, own, right, *after)
-
-
-def fill_kernel(sizes, spacing, anchor, reach, v_in, w_in, left, own, right, above, below, *rest):
-    groups, depth, held, full_x, full_y = sizes
+    )(in_vmem(v), in_vmem(w), own, one, other, *after)
+
+
+def fill_kernel(sizes, spacing, anchor, reach, v_in, w_in, own, one_side, other_side, one_end, other_end, *rest):
+    groups, depth, held, late, full_x, full_y = sizes
     outs, (token, table, result, beside) = rest[-groups - 4 : -4], rest[-4:]
+    more = rest[:groups]
     token[...] = jnp.zeros(token.shape, jnp.float32)
     total = groups * held
     packs = own.shape[1]
@@ -258,15 +291,20 @@
     x_at = x_start - 8 + lax.broadcasted_iota(jnp.int32, shape, 0)
     x_dist = squared_dist(x_at, spacing[1], anchor[1])
     x_inside = (x_at >= 0) & (x_at < full_x)
-    turn = jnp.floor((lane.astype(jnp.float32) + 0.5) * (0.5 / HALO))
-    column = lane - 2 * HALO * turn.astype(jnp.int32)
+    column = column_of(lane)
 
     def holes_at(y_at):
         plane = x_dist + squared_dist(y_at, spacing[2], anchor[2])
         return (plane <= reach[0].astype(jnp.float32)) & x_inside & (y_at >= 0) & (y_at < full_y)
 
+    even_x = is_even("gx", (8, LANES))
+    even_y = is_even("gy", shape)
+
     def extended(ref, at, array):
-        return jnp.concatenate([above[array], ref[at], below[array]], axis=0)
+        one, other = one_end[array], other_end[array]
+        above = jnp.where(even_x, other, one)
+        below = jnp.where(even_x, one, other)
+        return jnp.concatenate([above, ref[at], below], axis=0)
 
     def down_rows(value):
         return pltpu.roll(value, 1, 0) + (value + value) + pltpu.roll(value, tall - 1, 0)
@@ -282,21 +320,16 @@
 
     inner = column < HALO
     for pack in range(packs):
+        at_end = 2 * total + pack
+        mine = [extended(own, (kind, pack), at_end + kind * packs) for kind in range(2)]
+        one_from = extended(one_side, pack, at_end + 2 * packs)
+        other_from = extended(other_side, pack, at_end + 3 * packs)
+        left = jnp.where(even_y, other_from, one_from)
+        right = jnp.where(even_y, one_from, other_from)
+        left, right = (left, lanes(left, -HALO)), (right, lanes(right, HALO))
         found = []
-        for low, high, start in ((left, own, -HALO), (own, right, LANES - HALO)):
-            tiles = []
-            for kind in range(2):
-                places = [
-                    2 * total + (2 * {id(left): 0, id(own): 1, id(right): 2}[id(ref)] + kind) * packs + pack
-                    for ref in (low, high)
-                ]
-                tiles.append(
-                    jnp.where(
-                        inner,
-                        extended(low, (kind, pack), places[0]),
-                        extended(high, (kind, pack), places[1]),
-                    )
-                )
+        for low, high, start in ((left, mine, -HALO), (mine, right, LANES - HALO)):
+            tiles = [jnp.where(inner, one, other) for one, other in zip(low, high)]
             value, weight = tiles
             hole = holes_at(y_start + start + column)
             sums = down_rows(weight)
@@ -347,15 +380,18 @@
 
     lax.fori_loop(0, groups, one, 0)
     for n in range(groups):
-        outs[n][...] = result[n * held : (n + 1) * held]
-
-
-def fill(spacing, anchor, reach, v, w, sides, above, below, groups, held, depth, full, after):
+        if late:
+            outs[n][:late] = more[n][...]
+        outs[n][late:] = result[n * held : (n + 1) * held]
+
+
+def fill(spacing, anchor, reach, v, w, sides, ends, late, groups, held, depth, full, after):
+    count = late[0].shape[0] if late else 0
     rows = v.shape[1]
     return pl.pallas_call(
-        functools.partial(fill_kernel, (groups, depth, held) + full),
-        out_shape=[jax.ShapeDtypeStruct((held, rows, LANES), jnp.float32)] * groups + [TOKEN],
-        in_specs=[SMEM] * 3 + [VMEM] * 7 + [ANY] * len(after),
+        functools.partial(fill_kernel, (groups, depth, held, count) + full),
+        out_shape=[jax.ShapeDtypeStruct((count + held, rows, LANES), jnp.float32)] * groups + [TOKEN],
+        in_specs=[SMEM] * 3 + [VMEM] * (7 + len(late)) + [ANY] * len(after),
         out_specs=[VMEM] * (groups + 1),
         scratch_shapes=[
             pltpu.SMEM((groups * depth,), jnp.int32),
@@ -365,7 +401,7 @@
         compiler_params=params(),
         cost_estimate=cost(7.0),
         name="fill",
-    )(spacing, anchor, reach, in_vmem(v), in_vmem(w), *sides, above, below, *after)
+    )(spacing, anchor, reach, in_vmem(v), in_vmem(w), *sides, *ends, *late, *after)
 
 
 def dot3(a_high, a_low, b_high, b_low, dims):
@@ -377,7 +413,7 @@
 
 def x_kernel(groups, made, step, c_high, c_low, *rest):
     pieces = rest[:groups]
-    outs, (token, b_high, b_low, acc) = rest[-4 - made : -4], rest[-4:]
+    outs, (token, b_high, b_low, acc, sems) = rest[-5 - made : -5], rest[-5:]
     token[...] = jnp.zeros(token.shape, jnp.float32)
     apart = len(outs) > 1
     count, rows, _ = pieces[0].shape
@@ -393,21 +429,23 @@
             b_high[at, cols] = high
             b_low[at, cols] = low
     each = step // out_rows
-
-    def some(tile, carry):
-        at = pl.ds(pl.multiple_of(tile * step, step), step)
+    copies = []
+    for tile in range(length // step):
+        at = pl.ds(tile * step, step)
         value = dot3(c_high[at], c_low[at], b_high[...], b_low[...], ((1,), (0,)))
         if apart:
             acc[at] = value
-        else:
-            for part in range(each):
-                for layer in range(count):
-                    outs[0][tile * each + part, layer] = value[
-                        part * out_rows : (part + 1) * out_rows, layer * LANES : (layer + 1) * LANES
-                    ]
-        return carry
-
-    lax.fori_loop(0, parts // each, some, 0)
+            continue
+        for part in range(each):
+            for layer in range(count):
+                acc[tile * each + part, layer] = value[
+                    part * out_rows : (part + 1) * out_rows, layer * LANES : (layer + 1) * LANES
+                ]
+        some = pl.ds(tile * each, each)
+        copies.append(pltpu.make_async_copy(acc.at[some], outs[0].at[some], sems.at[tile]))
+        copies[-1].start()
+    for copy in copies:
+        copy.wait()
     if apart:
         row = lax.axis_index("gy")
         for k in range(parts):
@@ -420,7 +458,7 @@
     groups = len(pieces)
     count, rows, _ = pieces[0].shape
     length = rows * groups
-    step = min(512, length)
+    step = min(512 if apart else 256, length)
     high, low = cosine_split(length)
     tile = (count, length // parts, LANES)
     if apart:
@@ -431,11 +469,12 @@
         functools.partial(x_kernel, groups, len(shapes), step),
         out_shape=shapes + [TOKEN],
         in_specs=[VMEM] * (2 + groups) + [ANY] * len(after),
-        out_specs=[VMEM] * (len(shapes) + 1),
+        out_specs=[VMEM if apart else HBM] * len(shapes) + [VMEM],
         scratch_shapes=[
             pltpu.VMEM((length, count * LANES), jnp.bfloat16),
             pltpu.VMEM((length, count * LANES), jnp.bfloat16),
-            pltpu.VMEM((length if apart else 8, count * LANES), jnp.float32),
+            pltpu.VMEM((length, count * LANES) if apart else (parts,) + tile, jnp.float32),
+            pltpu.SemaphoreType.DMA((length // step,)),
         ],
         compiler_params=params(length),
         cost_estimate=cost(0.4 * count),
@@ -556,13 +595,16 @@
 
 
 def exchange(pieces, axis):
-    size = len(pieces)
-    return [pieces[0]] + [swap(pieces[n], axis, partner(n, size)) for n in range(1, size)]
-
-
-def shift(value, axis, by):
+    return [swap(piece, axis, k) for piece, k in zip(pieces, partners(len(pieces) + 1))]
+
+
+def swap_neighbours(first, second, axis):
     size = lax.axis_size(axis)
-    return lax.ppermute(value, axis, [(i, i + by) for i in range(size) if 0 <= i + by < size])
+    answers = []
+    for value, start in ((first, 0), (second, 1)):
+        pairs = [(i, i + 1) for i in range(start, size - 1, 2)]
+        answers.append(lax.ppermute(value, axis, pairs + [(j, i) for i, j in pairs]))
+    return answers
 
 
 def per_device(intensity, weight, spacing, anchor, reach):
@@ -579,33 +621,30 @@
 
     def to_rows(spectrum, apart):
         if apart:
-            return exchange(spectrum, "gy")
+            return spectrum[:1] + exchange(spectrum[1:], "gy")
         return [lax.all_to_all(spectrum[0], "gy", split_axis=0, concat_axis=0, tiled=True)]
 
     chunks = []
     if early:
         gathered = gather_clean(spacing, anchor, intensity, groups, 0, early)
         first_pieces = exchange(gathered, "gx")
-    v, w, own, *gathered, token = punch(
+    v, w, own, one, other, *mine, token = punch(
         spacing, anchor, reach, intensity, weight, groups, held, early, late
     )
-    left = shift(own, "gy", 1)
-    right = shift(own, "gy", -1)
-    if late:
-        late_pieces = exchange(gathered, "gx")
+    sides = swap_neighbours(one, other, "gy")
+    ends = swap_neighbours(*edges(v, w, own, *sides, []), "gx")
     if early:
-        *spectrum, token = along_x(first_pieces, parts, FIRST_APART, [left, right])
+        first_pieces = mine[:1] + first_pieces
+        mine = mine[1:]
+        *spectrum, token = along_x(first_pieces, parts, FIRST_APART, sides)
         chunks.append((0, to_rows(spectrum, FIRST_APART)))
-    top, bottom = edges(v, w, left, own, right, [token])
-    above = shift(bottom, "gx", 1)
-    below = shift(top, "gx", -1)
     *filled, token = fill(
-        spacing, anchor, reach, v, w, (left, own, right), above, below, groups, held, depth, full, [token]
+        spacing, anchor, reach, v, w, [own] + sides, ends, mine, groups, held, depth, full, [token]
     )
     tiles, token = kept_tiles(full[1], [token])
-    pieces = exchange([filled[partner(n, groups)] for n in range(groups)], "gx")
+    pieces = filled[:1] + exchange([filled[k] for k in partners(groups)], "gx")
     *spectrum, token = along_x(pieces, parts, LAST_APART, [token])
-    chunks.append((clean, to_rows(spectrum, LAST_APART)))
+    chunks.append((early, to_rows(spectrum, LAST_APART)))
     out = None
     for slot, pieces in chunks:
         out, token = along_y(tiles, spacing, anchor, pieces, slot, depth, out, parts, [token])

time: 83.8 us -> 81.9 us (0.977)
  starting transfers between devices: 34.7 us -> 30.7 us
  waiting for transfers between devices: 18.4 us -> 20.3 us
    ppermute x4, starting transfers between devices: 9.04 us -> 3.21 us  [swap_neighbours(): lax.ppermute(value, axis, pairs + [(j, i) for i, j in pairs])]
    ppermute x4, waiting for transfers between devices: 7.79 us -> 2.58 us  [swap_neighbours(): lax.ppermute(value, axis, pairs + [(j, i) for i, j in pairs])]
    ppermute x13, waiting for transfers between devices: 10.6 us -> 14.3 us  [swap(): return lax.ppermute(value, axis, [(i, i ^ k) for i in range(size)])]
    all_to_all x1, waiting for transfers between devices: 0.01 us -> 3.4 us  [to_rows(): lax.all_to_all(spectrum[0], 'gy', split_axis=0, concat_axis=0, tiled=True)]
    ppermute x13, starting transfers between devices: 19.7 us -> 21.5 us  [swap(): return lax.ppermute(value, axis, [(i, i ^ k) for i in range(size)])]
  transfers between devices with their start and end apart: 18 -> 18, of which waited for: 8 -> 7; matrix products, arithmetic and copies ran while one was open for 0% -> 0% of each run, Pallas kernels for 20% -> 21%
where the time goes in v3:
time: 81.9 us; the launch traced here: 81.5 us
  starting transfers between devices  30.7 us (37%)
  Pallas kernels  25.5 us (31%)
  waiting for transfers between devices  20.3 us (25%)
  local copies, waits for them, and re-layouts  4.16 us (5%)
  between operations  0.84 us (1%)
    ppermute x13, starting transfers between devices, swap(): return lax.ppermute(value, axis, [(i, i ^ k) for i in range(size)])  21.5 us
    ppermute x13, waiting for transfers between devices, swap(): return lax.ppermute(value, axis, [(i, i ^ k) for i in range(size)])  14.3 us
    pallas_call x2, Pallas kernels, along_y(): pl.pallas_call(functools.partial(y_kernel, slot, chained, apart), out_sha...  8.94 us
    all_to_all x1, starting transfers between devices, to_rows(): lax.all_to_all(spectrum[0], 'gy', split_axis=0, concat_axis=0, tiled=True)  5.92 us
    pallas_call x1, Pallas kernels, fill(): pl.pallas_call(functools.partial(fill_kernel, (groups, depth, held, count...  4.75 us
    unnamed x12, local copies, waits for them, and re-layouts  4.16 us
    pallas_call x2, Pallas kernels, along_x(): pl.pallas_call(functools.partial(x_kernel, groups, len(shapes), step), ou...  3.65 us
    pallas_call x1, Pallas kernels, punch(): pl.pallas_call(functools.partial(punch_kernel, (groups, depth, held), ear...  3.58 us
  transfers between devices with their start and end apart: 18, of which 7 were waited for; matrix products, arithmetic and copies ran while one was open for 0% of the time, Pallas kernels for 21%

profile of v3, /device:TPU:0, one launch (start us, length us, event | category | flops | bytes accessed | tf_op | source)
XLA Modules:
  0.0 81.5 jit_solution(181779229695106959)
XLA Ops:
  0.0 2.4 %gather_clean.1 = (f32[5,128,128]{2,1,0:T(8,128)S(1)}, f32[5,128,128]{2,1,0:T(8,128)S(1)}, f32[5,128,128]{2,1,0:T(8,128)S(1)}) custom-call(s32[3]{0:T(128)} %spacing.7, s32[3]{0:T(128)} %anchor.7, f32[32,128,128]{2,1,0:T(8,128)} %layers.3), custom_call_target="tpu_custom_call" | custom-call | bytes 5400000 | tf_op jit(solution)/shard_map/gather_clean/pallas_call | solution.py:144
  2.4 0.5 collective-permute-start.4
  2.9 2.6 %collective-permute-start.5 = (f32[5,128,128]{2,1,0:T(8,128)S(1)}, f32[5,128,128]{2,1,0:T(8,128)S(1)}, u32[]{:S(2)}, u32[]{:S(2)}) collective-permute-start(f32[5,128,128]{2,1,0:T(8,128)S(1)} %get-tuple-element.46), channel_id=1, source_target_pairs={{0,16},{8,24},{16,0},{24,8},{1,17},{9,25},{17,1},{25,9},{2,18},{10... | collective-permute-start | bytes 983048 | tf_op jit(solution)/shard_map/ppermute | solution.py:594
  6.2 3.6 %punch.1 = (f32[12,128,128]{2,1,0:T(8,128)S(1)}, f32[12,128,128]{2,1,0:T(8,128)S(1)}, f32[2,1,128,128]{3,2,1,0:T(8,128)S(1)}, f32[1,128,128]{2,1,0:T(8,128)S(1)}...) custom-call(s32[3]{0:T(128)S(1)} %copy-done.4, s32[3]{0:T(128)S(1)} %copy-done.5, ...), custom_call_target="tpu_custom_call" | custom-call | bytes 12600000 | tf_op jit(solution)/shard_map/punch/pallas_call | solution.py:223
  9.8 1.8 %collective-permute-start = (f32[1,128,128]{2,1,0:T(8,128)S(1)}, f32[1,128,128]{2,1,0:T(8,128)S(1)}, u32[]{:S(2)}, u32[]{:S(2)}) collective-permute-start(f32[1,128,128]{2,1,0:T(8,128)S(1)} %get-tuple-element.40), channel_id=1, source_target_pairs={{0,1},{2,3},{4,5},{6,7},{1,0},{3,2},{5,4},{7,6},{8,9},{10,11},{12,... | collective-permute-start | bytes 196616 | tf_op jit(solution)/shard_map/ppermute | solution.py:606
  11.6 0.7 collective-permute-start.1
  12.3 1.9 %collective-permute-done.one.rest_4_.one_side = f32[1,128,128]{2,1,0:T(8,128)S(1)} collective-permute-done((f32[1,128,128]{2,1,0:T(8,128)S(1)}, f32[1,128,128]{2,1,0:T(8,128)S(1)}, u32[]{:S(2)}, u32[]{:S(2)}) %collective-permute-start) | collective-permute-done | bytes 65568 | tf_op jit(solution)/shard_map/ppermute | solution.py:606
  14.3 6.3 %collective-permute-done.6.rest_3_ = f32[5,128,128]{2,1,0:T(8,128)S(1)} collective-permute-done((f32[5,128,128]{2,1,0:T(8,128)S(1)}, f32[5,128,128]{2,1,0:T(8,128)S(1)}, u32[]{:S(2)}, u32[]{:S(2)}) %collective-permute-start.6) | collective-permute-done | bytes 327712 | tf_op jit(solution)/shard_map/ppermute | solution.py:594
  20.5 2.5 %along_x.2 = (f32[8,5,64,128]{3,2,1,0:T(8,128)}, f32[8,128]{1,0:T(8,128)S(1)}) custom-call(bf16[512,512]{1,0:T(8,128)(2,1)S(1)} %copy-done.3, bf16[512,512]{1,0:T(8,128)(2,1)S(1)} %copy-done.2, f32[5,128,128]{2,1,0:T(8,128)S(1)} %get-tuple-element.44.rest_0_, f32[5,128,128]{2,1,0:T(8,128)S(1)} %collective-permute-done.4.rest_1_, ...), custom_call_target="tpu_custom_call" | custom-call | bytes 7200000 | tf_op jit(solution)/shard_map/along_x/pallas_call | solution.py:468
  23.0 5.9 %all-to-all-start = ((f32[8,5,64,128]{3,2,1,0:T(8,128)}), f32[8,5,64,128]{3,2,1,0:T(8,128)}, u32[]{:S(2)}, u32[]{:S(2)}) async-start(f32[8,5,64,128]{3,2,1,0:T(8,128)} %get-tuple-element.64), calls=%async_computation | async-start | bytes 2621440 | tf_op jit(solution)/shard_map/all_to_all | solution.py:625
  29.1 0.7 collective-permute-start.3
  29.7 0.6 collective-permute-done.2.one_end
  30.4 4.7 %fill.1 = (f32[3,128,128]{2,1,0:T(8,128)S(1)}, f32[3,128,128]{2,1,0:T(8,128)S(1)}, f32[3,128,128]{2,1,0:T(8,128)S(1)}, f32[3,128,128]{2,1,0:T(8,128)S(1)}, f32[8,128]{1,0:T(8,128)S(1)}) custom-call(s32[3]{0:T(128)S(1)} %copy-done.4, s32[3]{0:T(128)S(1)} %copy-done.5, s32[1]{0:T(128)S(6)} %copy.11.reach, f32[12,128,128]{2,1,0:T(8,128)S(1)} %get-tuple-element.37.v.v_in, ...), custom_call_target="tpu_custom_call" | custom-call | bytes 25200000 | tf_op jit(solution)/shard_map/fill/pallas_call | solution.py:391
  35.1 5.7 %collective-permute-start.7 = (f32[3,128,128]{2,1,0:T(8,128)S(1)}, f32[3,128,128]{2,1,0:T(8,128)S(1)}, u32[]{:S(2)}, u32[]{:S(2)}) collective-permute-start(f32[3,128,128]{2,1,0:T(8,128)S(1)} %get-tuple-element.52), channel_id=1, source_target_pairs={{0,8},{8,0},{16,24},{24,16},{1,9},{9,1},{17,25},{25,17},{2,10},{10... | collective-permute-start | bytes 589832 | tf_op jit(solution)/shard_map/ppermute | solution.py:594
  40.9 0.7 collective-permute-start.8
  41.6 0.7 collective-permute-start.9
  42.3 2.2 %keep_tiles.1 = (bf16[8,1024,256]{2,1,0:T(8,128)(2,1)S(1)}, f32[8,128]{1,0:T(8,128)S(1)}) custom-call(bf16[8,1024,256]{2,1,0:T(8,128)(2,1)} %constant.8.clone.source, f32[8,128]{1,0:T(8,128)S(1)} %get-tuple-element.49.rest_0_), custom_call_target="tpu_custom_call" | custom-call | bytes 7200000 | tf_op jit(solution)/shard_map/keep_tiles/pallas_call | solution.py:501
  44.5 1.9 %copy-done = bf16[8,1024,256]{2,1,0:T(8,128)(2,1)} copy-done((bf16[8,1024,256]{2,1,0:T(8,128)(2,1)}, bf16[8,1024,256]{2,1,0:T(8,128)(2,1)S(1)}, u32[]{:S(2)}) %copy-start) | copy-done | bytes 4194328
  46.5 2.1 %collective-permute-done.8.rest_2_ = f32[3,128,128]{2,1,0:T(8,128)S(1)} collective-permute-done((f32[3,128,128]{2,1,0:T(8,128)S(1)}, f32[3,128,128]{2,1,0:T(8,128)S(1)}, u32[]{:S(2)}, u32[]{:S(2)}) %collective-permute-start.8) | collective-permute-done | bytes 196640 | tf_op jit(solution)/shard_map/ppermute | solution.py:594
  48.6 2.5 %collective-permute-done.9.rest_3_ = f32[3,128,128]{2,1,0:T(8,128)S(1)} collective-permute-done((f32[3,128,128]{2,1,0:T(8,128)S(1)}, f32[3,128,128]{2,1,0:T(8,128)S(1)}, u32[]{:S(2)}, u32[]{:S(2)}) %collective-permute-start.9) | collective-permute-done | bytes 196640 | tf_op jit(solution)/shard_map/ppermute | solution.py:594
  51.1 1.2 %along_x.3 = (f32[3,64,128]{2,1,0:T(8,128)S(1)}, f32[3,64,128]{2,1,0:T(8,128)S(1)}, f32[3,64,128]{2,1,0:T(8,128)S(1)}, f32[3,64,128]{2,1,0:T(8,128)S(1)}, f32[3,...) custom-call(bf16[512,512]{1,0:T(8,128)(2,1)S(1)} %copy-done.3, ...), custom_call_target="tpu_custom_call" | custom-call | bytes 4320000 | tf_op jit(solution)/shard_map/along_x/pallas_call | solution.py:468
  52.3 2.1 %collective-permute-start.10 = (f32[3,64,128]{2,1,0:T(8,128)S(1)}, f32[3,64,128]{2,1,0:T(8,128)S(1)}, u32[]{:S(2)}, u32[]{:S(2)}) collective-permute-start(f32[3,64,128]{2,1,0:T(8,128)S(1)} %get-tuple-element.57), channel_id=1, source_target_pairs={{0,1},{1,0},{2,3},{3,2},{4,5},{5,4},{6,7},{7,6},{8,9},{9,8},{10,11... | collective-permute-start | bytes 294920 | tf_op jit(solution)/shard_map/ppermute | solution.py:594
  54.3 1.5 %collective-permute-start.11 = (f32[3,64,128]{2,1,0:T(8,128)S(1)}, f32[3,64,128]{2,1,0:T(8,128)S(1)}, u32[]{:S(2)}, u32[]{:S(2)}) collective-permute-start(f32[3,64,128]{2,1,0:T(8,128)S(1)} %get-tuple-element.58), channel_id=1, source_target_pairs={{0,2},{1,3},{2,0},{3,1},{4,6},{5,7},{6,4},{7,5},{8,10},{9,11},{10,... | collective-permute-start | bytes 294920 | tf_op jit(solution)/shard_map/ppermute | solution.py:594
  55.8 2.4 %collective-permute-start.12 = (f32[3,64,128]{2,1,0:T(8,128)S(1)}, f32[3,64,128]{2,1,0:T(8,128)S(1)}, u32[]{:S(2)}, u32[]{:S(2)}) collective-permute-start(f32[3,64,128]{2,1,0:T(8,128)S(1)} %get-tuple-element.59), channel_id=1, source_target_pairs={{0,7},{1,6},{2,5},{3,4},{4,3},{5,2},{6,1},{7,0},{8,15},{9,14},{10,... | collective-permute-start | bytes 294920 | tf_op jit(solution)/shard_map/ppermute | solution.py:594
  58.2 1.5 %collective-permute-start.13 = (f32[3,64,128]{2,1,0:T(8,128)S(1)}, f32[3,64,128]{2,1,0:T(8,128)S(1)}, u32[]{:S(2)}, u32[]{:S(2)}) collective-permute-start(f32[3,64,128]{2,1,0:T(8,128)S(1)} %get-tuple-element.60), channel_id=1, source_target_pairs={{0,6},{1,7},{2,4},{3,5},{4,2},{5,3},{6,0},{7,1},{8,14},{9,15},{10,... | collective-permute-start | bytes 294920 | tf_op jit(solution)/shard_map/ppermute | solution.py:594
  59.6 1.5 %collective-permute-start.14 = (f32[3,64,128]{2,1,0:T(8,128)S(1)}, f32[3,64,128]{2,1,0:T(8,128)S(1)}, u32[]{:S(2)}, u32[]{:S(2)}) collective-permute-start(f32[3,64,128]{2,1,0:T(8,128)S(1)} %get-tuple-element.61), channel_id=1, source_target_pairs={{0,5},{1,4},{2,7},{3,6},{4,1},{5,0},{6,3},{7,2},{8,13},{9,12},{10,... | collective-permute-start | bytes 294920 | tf_op jit(solution)/shard_map/ppermute | solution.py:594
  61.1 2.4 %collective-permute-start.15 = (f32[3,64,128]{2,1,0:T(8,128)S(1)}, f32[3,64,128]{2,1,0:T(8,128)S(1)}, u32[]{:S(2)}, u32[]{:S(2)}) collective-permute-start(f32[3,64,128]{2,1,0:T(8,128)S(1)} %get-tuple-element.62), channel_id=1, source_target_pairs={{0,4},{1,5},{2,6},{3,7},{4,0},{5,1},{6,2},{7,3},{8,12},{9,13},{10,... | collective-permute-start | bytes 294920 | tf_op jit(solution)/shard_map/ppermute | solution.py:594
  63.5 3.4 %collective-permute-done.11.rest_2_ = f32[3,64,128]{2,1,0:T(8,128)S(1)} collective-permute-done((f32[3,64,128]{2,1,0:T(8,128)S(1)}, f32[3,64,128]{2,1,0:T(8,128)S(1)}, u32[]{:S(2)}, u32[]{:S(2)}) %collective-permute-start.11) | collective-permute-done | bytes 98336 | tf_op jit(solution)/shard_map/ppermute | solution.py:594
  66.9 3.4 %all-to-all-done.rest_0_ = f32[8,5,64,128]{3,2,1,0:T(8,128)} async-done(((f32[8,5,64,128]{3,2,1,0:T(8,128)}), f32[8,5,64,128]{3,2,1,0:T(8,128)}, u32[]{:S(2)}, u32[]{:S(2)}) %all-to-all-start) | async-done | bytes 1310752 | tf_op jit(solution)/shard_map/all_to_all | solution.py:625
  70.3 2.2 %copy-done.1 = bf16[8,1024,256]{2,1,0:T(8,128)(2,1)S(1)} copy-done((bf16[8,1024,256]{2,1,0:T(8,128)(2,1)S(1)}, bf16[8,1024,256]{2,1,0:T(8,128)(2,1)}, u32[]{:S(2)}) %copy-start.1) | copy-done | bytes 4194328
  72.5 5.3 %along_y.2 = (f32[8,64,1024]{2,1,0:T(8,128)}, f32[8,128]{1,0:T(8,128)S(1)}) custom-call(s32[3]{0:T(128)S(1)} %copy-done.4, s32[3]{0:T(128)S(1)} %copy-done.5, bf16[8,1024,256]{2,1,0:T(8,128)(2,1)S(1)} %copy-done.1, f32[8,5,64,128]{3,2,1,0:T(8,128)} %all-to-all-done.rest_0_, f32[8,128]{1,0:T(8,128)S(1)} %get-tuple-element.65.rest_1_), custom_call_target="tpu_custom_call" | custom-call | bytes 18000000 | tf_op jit(solution)/shard_map/along_y/pallas_call | solution.py:568
  77.8 3.7 %along_y.3 = (f32[8,64,1024]{2,1,0:T(8,128)}, f32[8,128]{1,0:T(8,128)}) custom-call(s32[3]{0:T(128)S(1)} %copy-done.4, s32[3]{0:T(128)S(1)} %copy-done.5, bf16[8,1024,256]{2,1,0:T(8,128)(2,1)S(1)} %copy-done.1, f32[3,64,128]{2,1,0:T(8,128)S(1)} %get-tuple-element.56.rest_0_, ...), custom_call_target="tpu_custom_call", output_to_operand_aliasing={{0}: (11, {})} | custom-call | bytes 10800000 | tf_op jit(solution)/shard_map/along_y/pallas_call | solution.py:568
  (25 shorter events, 0.2 us)
Async XLA Ops:
  0.0 6.2 %copy-start.5 = (s32[3]{0:T(128)S(1)}, s32[3]{0:T(128)}, u32[]{:S(2)}) copy-start(s32[3]{0:T(128)} %anchor.7) | copy-start | bytes 40
  0.0 6.2 %copy-start.4 = (s32[3]{0:T(128)S(1)}, s32[3]{0:T(128)}, u32[]{:S(2)}) copy-start(s32[3]{0:T(128)} %spacing.7) | copy-start | bytes 40
  2.4 11.9 %collective-permute-start.4 = (f32[5,128,128]{2,1,0:T(8,128)S(1)}, f32[5,128,128]{2,1,0:T(8,128)S(1)}, u32[]{:S(2)}, u32[]{:S(2)}) collective-permute-start(f32[5,128,128]{2,1,0:T(8,128)S(1)} %get-tuple-element.45), channel_id=1, source_target_pairs={{0,8},{8,0},{16,24},{24,16},{1,9},{9,1},{17,25},{25,17},{2,10},{10... | collective-permute-start | bytes 983048 | tf_op jit(solution)/shard_map/ppermute | solution.py:594
  2.9 11.3 %collective-permute-start.5 = (f32[5,128,128]{2,1,0:T(8,128)S(1)}, f32[5,128,128]{2,1,0:T(8,128)S(1)}, u32[]{:S(2)}, u32[]{:S(2)}) collective-permute-start(f32[5,128,128]{2,1,0:T(8,128)S(1)} %get-tuple-element.46), channel_id=1, source_target_pairs={{0,16},{8,24},{16,0},{24,8},{1,17},{9,25},{17,1},{25,9},{2,18},{10... | collective-permute-start | bytes 983048 | tf_op jit(solution)/shard_map/ppermute | solution.py:594
  5.5 15.1 %collective-permute-start.6 = (f32[5,128,128]{2,1,0:T(8,128)S(1)}, f32[5,128,128]{2,1,0:T(8,128)S(1)}, u32[]{:S(2)}, u32[]{:S(2)}) collective-permute-start(f32[5,128,128]{2,1,0:T(8,128)S(1)} %get-tuple-element.47), channel_id=1, source_target_pairs={{0,24},{8,16},{16,8},{24,0},{1,25},{9,17},{17,9},{25,1},{2,26},{10... | collective-permute-start | bytes 983048 | tf_op jit(solution)/shard_map/ppermute | solution.py:594
  6.2 14.3 %copy-start.2 = (bf16[512,512]{1,0:T(8,128)(2,1)S(1)}, bf16[512,512]{1,0:T(8,128)(2,1)}, u32[]{:S(2)}) copy-start(bf16[512,512]{1,0:T(8,128)(2,1)} %constant.7.clone.c_low) | copy-start | bytes 1572868
  6.2 14.3 %copy-start.3 = (bf16[512,512]{1,0:T(8,128)(2,1)S(1)}, bf16[512,512]{1,0:T(8,128)(2,1)}, u32[]{:S(2)}) copy-start(bf16[512,512]{1,0:T(8,128)(2,1)} %constant.6.clone.c_high) | copy-start | bytes 1572868
  9.8 4.4 %collective-permute-start = (f32[1,128,128]{2,1,0:T(8,128)S(1)}, f32[1,128,128]{2,1,0:T(8,128)S(1)}, u32[]{:S(2)}, u32[]{:S(2)}) collective-permute-start(f32[1,128,128]{2,1,0:T(8,128)S(1)} %get-tuple-element.40), channel_id=1, source_target_pairs={{0,1},{2,3},{4,5},{6,7},{1,0},{3,2},{5,4},{7,6},{8,9},{10,11},{12,... | collective-permute-start | bytes 196616 | tf_op jit(solution)/shard_map/ppermute | solution.py:606
  11.6 2.6 %collective-permute-start.1 = (f32[1,128,128]{2,1,0:T(8,128)S(1)}, f32[1,128,128]{2,1,0:T(8,128)S(1)}, u32[]{:S(2)}, u32[]{:S(2)}) collective-permute-start(f32[1,128,128]{2,1,0:T(8,128)S(1)} %get-tuple-element.41), channel_id=1, source_target_pairs={{1,2},{3,4},{5,6},{2,1},{4,3},{6,5},{9,10},{11,12},{13,14},{10,9},... | collective-permute-start | bytes 196616 | tf_op jit(solution)/shard_map/ppermute | solution.py:606
  23.0 47.3 %all-to-all-start = ((f32[8,5,64,128]{3,2,1,0:T(8,128)}), f32[8,5,64,128]{3,2,1,0:T(8,128)}, u32[]{:S(2)}, u32[]{:S(2)}) async-start(f32[8,5,64,128]{3,2,1,0:T(8,128)} %get-tuple-element.64), calls=%async_computation | async-start | bytes 2621440 | tf_op jit(solution)/shard_map/all_to_all | solution.py:625
  29.0 1.4 %collective-permute-start.2 = (f32[28,8,128]{2,1,0:T(8,128)S(1)}, f32[28,8,128]{2,1,0:T(8,128)S(1)}, u32[]{:S(2)}, u32[]{:S(2)}) collective-permute-start(f32[28,8,128]{2,1,0:T(8,128)S(1)} %get-tuple-element.42), channel_id=1, source_target_pairs={{0,8},{16,24},{8,0},{24,16},{1,9},{17,25},{9,1},{25,17},{2,10},{18... | collective-permute-start | bytes 344072 | tf_op jit(solution)/shard_map/ppermute | solution.py:606
  29.1 1.3 %collective-permute-start.3 = (f32[28,8,128]{2,1,0:T(8,128)S(1)}, f32[28,8,128]{2,1,0:T(8,128)S(1)}, u32[]{:S(2)}, u32[]{:S(2)}) collective-permute-start(f32[28,8,128]{2,1,0:T(8,128)S(1)} %get-tuple-element.43), channel_id=1, source_target_pairs={{8,16},{16,8},{9,17},{17,9},{10,18},{18,10},{11,19},{19,11},{12,20... | collective-permute-start | bytes 344072 | tf_op jit(solution)/shard_map/ppermute | solution.py:606
  35.1 11.4 %collective-permute-start.7 = (f32[3,128,128]{2,1,0:T(8,128)S(1)}, f32[3,128,128]{2,1,0:T(8,128)S(1)}, u32[]{:S(2)}, u32[]{:S(2)}) collective-permute-start(f32[3,128,128]{2,1,0:T(8,128)S(1)} %get-tuple-element.52), channel_id=1, source_target_pairs={{0,8},{8,0},{16,24},{24,16},{1,9},{9,1},{17,25},{25,17},{2,10},{10... | collective-permute-start | bytes 589832 | tf_op jit(solution)/shard_map/ppermute | solution.py:594
  40.9 7.8 %collective-permute-start.8 = (f32[3,128,128]{2,1,0:T(8,128)S(1)}, f32[3,128,128]{2,1,0:T(8,128)S(1)}, u32[]{:S(2)}, u32[]{:S(2)}) collective-permute-start(f32[3,128,128]{2,1,0:T(8,128)S(1)} %get-tuple-element.53), channel_id=1, source_target_pairs={{0,16},{8,24},{16,0},{24,8},{1,17},{9,25},{17,1},{25,9},{2,18},{10... | collective-permute-start | bytes 589832 | tf_op jit(solution)/shard_map/ppermute | solution.py:594
  41.6 9.5 %collective-permute-start.9 = (f32[3,128,128]{2,1,0:T(8,128)S(1)}, f32[3,128,128]{2,1,0:T(8,128)S(1)}, u32[]{:S(2)}, u32[]{:S(2)}) collective-permute-start(f32[3,128,128]{2,1,0:T(8,128)S(1)} %get-tuple-element.54), channel_id=1, source_target_pairs={{0,24},{8,16},{16,8},{24,0},{1,25},{9,17},{17,9},{25,1},{2,26},{10... | collective-permute-start | bytes 589832 | tf_op jit(solution)/shard_map/ppermute | solution.py:594
  44.5 2.0 %copy-start = (bf16[8,1024,256]{2,1,0:T(8,128)(2,1)}, bf16[8,1024,256]{2,1,0:T(8,128)(2,1)S(1)}, u32[]{:S(2)}) copy-start(bf16[8,1024,256]{2,1,0:T(8,128)(2,1)S(1)} %get-tuple-element.50.cosines) | copy-start | bytes 12582916
  52.3 8.8 %collective-permute-start.10 = (f32[3,64,128]{2,1,0:T(8,128)S(1)}, f32[3,64,128]{2,1,0:T(8,128)S(1)}, u32[]{:S(2)}, u32[]{:S(2)}) collective-permute-start(f32[3,64,128]{2,1,0:T(8,128)S(1)} %get-tuple-element.57), channel_id=1, source_target_pairs={{0,1},{1,0},{2,3},{3,2},{4,5},{5,4},{6,7},{7,6},{8,9},{9,8},{10,11... | collective-permute-start | bytes 294920 | tf_op jit(solution)/shard_map/ppermute | solution.py:594
  54.3 12.6 %collective-permute-start.11 = (f32[3,64,128]{2,1,0:T(8,128)S(1)}, f32[3,64,128]{2,1,0:T(8,128)S(1)}, u32[]{:S(2)}, u32[]{:S(2)}) collective-permute-start(f32[3,64,128]{2,1,0:T(8,128)S(1)} %get-tuple-element.58), channel_id=1, source_target_pairs={{0,2},{1,3},{2,0},{3,1},{4,6},{5,7},{6,4},{7,5},{8,10},{9,11},{10,... | collective-permute-start | bytes 294920 | tf_op jit(solution)/shard_map/ppermute | solution.py:594
  55.8 22.0 %collective-permute-start.12 = (f32[3,64,128]{2,1,0:T(8,128)S(1)}, f32[3,64,128]{2,1,0:T(8,128)S(1)}, u32[]{:S(2)}, u32[]{:S(2)}) collective-permute-start(f32[3,64,128]{2,1,0:T(8,128)S(1)} %get-tuple-element.59), channel_id=1, source_target_pairs={{0,7},{1,6},{2,5},{3,4},{4,3},{5,2},{6,1},{7,0},{8,15},{9,14},{10,... | collective-permute-start | bytes 294920 | tf_op jit(solution)/shard_map/ppermute | solution.py:594
  58.2 19.6 %collective-permute-start.13 = (f32[3,64,128]{2,1,0:T(8,128)S(1)}, f32[3,64,128]{2,1,0:T(8,128)S(1)}, u32[]{:S(2)}, u32[]{:S(2)}) collective-permute-start(f32[3,64,128]{2,1,0:T(8,128)S(1)} %get-tuple-element.60), channel_id=1, source_target_pairs={{0,6},{1,7},{2,4},{3,5},{4,2},{5,3},{6,0},{7,1},{8,14},{9,15},{10,... | collective-permute-start | bytes 294920 | tf_op jit(solution)/shard_map/ppermute | solution.py:594
  59.6 18.1 %collective-permute-start.14 = (f32[3,64,128]{2,1,0:T(8,128)S(1)}, f32[3,64,128]{2,1,0:T(8,128)S(1)}, u32[]{:S(2)}, u32[]{:S(2)}) collective-permute-start(f32[3,64,128]{2,1,0:T(8,128)S(1)} %get-tuple-element.61), channel_id=1, source_target_pairs={{0,5},{1,4},{2,7},{3,6},{4,1},{5,0},{6,3},{7,2},{8,13},{9,12},{10,... | collective-permute-start | bytes 294920 | tf_op jit(solution)/shard_map/ppermute | solution.py:594
  61.1 16.7 %collective-permute-start.15 = (f32[3,64,128]{2,1,0:T(8,128)S(1)}, f32[3,64,128]{2,1,0:T(8,128)S(1)}, u32[]{:S(2)}, u32[]{:S(2)}) collective-permute-start(f32[3,64,128]{2,1,0:T(8,128)S(1)} %get-tuple-element.62), channel_id=1, source_target_pairs={{0,4},{1,5},{2,6},{3,7},{4,0},{5,1},{6,2},{7,3},{8,12},{9,13},{10,... | collective-permute-start | bytes 294920 | tf_op jit(solution)/shard_map/ppermute | solution.py:594
  66.9 10.9 %collective-permute-start.16 = (f32[3,64,128]{2,1,0:T(8,128)S(1)}, f32[3,64,128]{2,1,0:T(8,128)S(1)}, u32[]{:S(2)}, u32[]{:S(2)}) collective-permute-start(f32[3,64,128]{2,1,0:T(8,128)S(1)} %get-tuple-element.63), channel_id=1, source_target_pairs={{0,3},{1,2},{2,1},{3,0},{4,7},{5,6},{6,5},{7,4},{8,11},{9,10},{10,... | collective-permute-start | bytes 294920 | tf_op jit(solution)/shard_map/ppermute | solution.py:594
  70.3 2.2 %copy-start.1 = (bf16[8,1024,256]{2,1,0:T(8,128)(2,1)S(1)}, bf16[8,1024,256]{2,1,0:T(8,128)(2,1)}, u32[]{:S(2)}) copy-start(bf16[8,1024,256]{2,1,0:T(8,128)(2,1)} %copy-done) | copy-start | bytes 12582916

commit v4 on v3

--- a/solution.py
+++ b/solution.py
@@ -54,7 +54,7 @@
 
 
 def partner(n, size):
-    return n if n < 3 else size + 2 - n
+    return n if n < 4 else size + 3 - n
 
 
 def column_of(lane):
@@ -64,6 +64,10 @@
 
 def is_even(axis, shape):
     return jnp.full(shape, lax.rem(lax.axis_index(axis), 2)) == 0
+
+
+def early_pieces(parts):
+    return parts // 2 + 1
 
 
 def partners(size):
@@ -486,28 +490,96 @@
     return [part.T.reshape(length, -1, step).swapaxes(0, 1) for part in cosine_split(length)]
 
 
-def keep_kernel(source, *rest):
-    kept, token, sems = rest[-3:]
-    token[...] = jnp.zeros(token.shape, jnp.float32)
-    copies = [pltpu.make_async_copy(source.at[n], kept.at[n], sems.at[n]) for n in range(source.shape[0])]
-    for copy in copies:
-        copy.start()
+def y_part_kernel(parts, cosines, *rest):
+    out, a_high, a_low = rest[-3:]
+    steps = out.shape[0]
+    early = early_pieces(parts)
+    pieces = rest[:early]
+    count, rows, _ = pieces[0].shape
+    row = lax.axis_index("gy")
+    for n in range(parts):
+        cols = pl.ds(pl.multiple_of((row ^ partner(n, parts)) * LANES, LANES), LANES)
+        for layer in range(count):
+            at = pl.ds(layer * rows, rows)
+            if n < early:
+                a_high[at, cols], a_low[at, cols] = split(pieces[n][layer])
+            else:
+                a_high[at, cols] = jnp.zeros((rows, LANES), jnp.bfloat16)
+                a_low[at, cols] = jnp.zeros((rows, LANES), jnp.bfloat16)
+    for tile in range(steps):
+        out[tile] = dot3(a_high[...], a_low[...], cosines[tile], cosines[steps + tile], ((1,), (0,)))
+
+
+def along_y_part(tiles, pieces, parts, after):
+    count, rows, _ = pieces[0].shape
+    _, length, step = tiles.shape
+    return pl.pallas_call(
+        functools.partial(y_part_kernel, parts),
+        out_shape=jax.ShapeDtypeStruct((length // step, count * rows, step), jnp.float32),
+        in_specs=[VMEM] * (1 + len(pieces)) + [ANY] * len(after),
+        out_specs=VMEM,
+        scratch_shapes=[pltpu.VMEM((count * rows, length), jnp.bfloat16)] * 2,
+        compiler_params=params(length),
+        cost_estimate=cost(2.0),
+        name="along_y_part",
+    )(in_vmem(tiles), *pieces, *after)
+
+
+def y_rest_kernel(parts, slot, chained, spacing, anchor, cosines, partial, *rest):
+    out, acc, table, sems = rest[-4:]
+    early = early_pieces(parts)
+    pieces = rest[: parts - early]
+    steps = partial.shape[0]
+    step = partial.shape[2]
+    count, rows, _ = pieces[0].shape
+    depth = out.shape[0]
+    first = lax.axis_index("gx") * depth
+    order_layers(table, 0, first, depth, spacing[0], anchor[0])
+    row = lax.axis_index("gy")
+    halves, places = [], []
+    for n, piece in enumerate(pieces):
+        halves.append(split(jnp.concatenate([piece[layer] for layer in range(count)], axis=0)))
+        start = (row ^ partner(early + n, parts)) * LANES
+        places.append(pl.ds(pl.multiple_of(start, LANES), LANES))
+    copies = []
+    for tile in range(steps):
+        value = partial[tile]
+        for (high, low), at in zip(halves, places):
+            value = value + dot3(high, low, cosines[tile, at], cosines[steps + tile, at], ((1,), (0,)))
+        acc[tile] = value
+        for layer in range(count):
+            copies.append(
+                pltpu.make_async_copy(
+                    acc.at[tile, pl.ds(layer * rows, rows)],
+                    out.at[table[slot + layer] - first, :, pl.ds(tile * step, step)],
+                    sems.at[tile, layer],
+                )
+            )
+            copies[-1].start()
     for copy in copies:
         copy.wait()
 
 
-def kept_tiles(length, after):
-    tiles = jnp.asarray(np.concatenate(column_tiles(length, min(256, length))))
+def along_y_rest(tiles, spacing, anchor, partial, pieces, slot, depth, before, parts):
+    count, rows, _ = pieces[0].shape
+    _, length, step = tiles.shape
+    steps = length // step
+    chained = before is not None
     return pl.pallas_call(
-        keep_kernel,
-        out_shape=[pltpu.VMEM(tiles.shape, jnp.bfloat16), TOKEN],
-        in_specs=[HBM] + [ANY] * len(after),
-        out_specs=[VMEM, VMEM],
-        scratch_shapes=[pltpu.SemaphoreType.DMA((tiles.shape[0],))],
+        functools.partial(y_rest_kernel, parts, slot, chained),
+        out_shape=jax.ShapeDtypeStruct((depth, rows, length), jnp.float32),
+        in_specs=[SMEM, SMEM] + [VMEM] * (2 + len(pieces)) + ([HBM] if chained else []),
+        out_specs=HBM,
+        scratch_shapes=[
+            pltpu.VMEM((steps, count * rows, step), jnp.float32),
+            pltpu.SMEM((depth,), jnp.int32),
+            pltpu.SemaphoreType.DMA((steps, count)),
+        ],
+        input_output_aliases={4 + len(pieces): 0} if chained else {},
         compiler_params=params(length),
         cost_estimate=cost(2.0),
-        name="keep_tiles",
-    )(in_hbm(tiles), *after)
+        name="along_y_rest",
+    )(spacing, anchor, in_vmem(tiles), partial, *pieces, *([before] if chained else []))
 
 
 def y_kernel(slot, chained, apart, spacing, anchor, cosines, *rest):
@@ -641,13 +713,17 @@
     *filled, token = fill(
         spacing, anchor, reach, v, w, [own] + sides, ends, mine, groups, held, depth, full, [token]
     )
-    tiles, token = kept_tiles(full[1], [token])
+    tiles = jnp.asarray(np.concatenate(column_tiles(full[1], min(256, full[1]))))
     pieces = filled[:1] + exchange([filled[k] for k in partners(groups)], "gx")
     *spectrum, token = along_x(pieces, parts, LAST_APART, [token])
     chunks.append((early, to_rows(spectrum, LAST_APART)))
     out = None
-    for slot, pieces in chunks:
+    for slot, pieces in chunks[:-1]:
         out, token = along_y(tiles, spacing, anchor, pieces, slot, depth, out, parts, [token])
+    slot, pieces = chunks[-1]
+    some = early_pieces(parts)
+    partial = along_y_part(tiles, pieces[:some], parts, [token])
+    out = along_y_rest(tiles, spacing, anchor, partial, pieces[some:], slot, depth, out, parts)
     return out
 
 

time: 81.9 us -> 81.1 us (level)
  waiting for transfers between devices: 20.3 us -> 24.3 us
  local copies, waits for them, and re-layouts: 4.16 us -> 2.21 us
  Pallas kernels: 25.5 us -> 23.9 us
  starting transfers between devices: 30.7 us -> 29.5 us
    ppermute x13, waiting for transfers between devices: 14.3 us -> 21.7 us  [swap(): return lax.ppermute(value, axis, [(i, i ^ k) for i in range(size)])]
    pallas_call x2 -> x1, Pallas kernels: 8.94 us -> 5.51 us  [along_y(): pl.pallas_call(functools.partial(y_kernel, slot, chained, apart), out_sha...]
    all_to_all x1, waiting for transfers between devices: 3.4 us -> 0.01 us  [to_rows(): lax.all_to_all(spectrum[0], 'gy', split_axis=0, concat_axis=0, tiled=True)]
    unnamed x12, local copies, waits for them, and re-layouts: 4.16 us -> 2.21 us
    pallas_call x1 -> x2, Pallas kernels: 2.21 us -> 4.04 us  [the longest x1 2.46 us: along_y_rest(): pl.pallas_call(functools.partial(y_rest_kernel, parts, slot, chained), ou...]
    ppermute x13, starting transfers between devices: 21.5 us -> 20.4 us  [swap(): return lax.ppermute(value, axis, [(i, i ^ k) for i in range(size)])]
  transfers between devices with their start and end apart: 18 -> 18, of which waited for: 7 -> 8; matrix products, arithmetic and copies ran while one was open for 0% -> 0% of each run, Pallas kernels for 21% -> 21%
where the time goes in v4:
time: 81.1 us; the launch traced here: 80.8 us
  starting transfers between devices  29.5 us (36%)
  waiting for transfers between devices  24.3 us (30%)
  Pallas kernels  23.9 us (29%)
  local copies, waits for them, and re-layouts  2.21 us (3%)
  between operations  0.83 us (1%)
    ppermute x13, waiting for transfers between devices, swap(): return lax.ppermute(value, axis, [(i, i ^ k) for i in range(size)])  21.7 us
    ppermute x13, starting transfers between devices, swap(): return lax.ppermute(value, axis, [(i, i ^ k) for i in range(size)])  20.4 us
    all_to_all x1, starting transfers between devices, to_rows(): lax.all_to_all(spectrum[0], 'gy', split_axis=0, concat_axis=0, tiled=True)  5.92 us
    pallas_call x1, Pallas kernels, along_y(): pl.pallas_call(functools.partial(y_kernel, slot, chained, apart), out_sha...  5.51 us
    pallas_call x1, Pallas kernels, fill(): pl.pallas_call(functools.partial(fill_kernel, (groups, depth, held, count...  4.75 us
    pallas_call x2, Pallas kernels, along_x(): pl.pallas_call(functools.partial(x_kernel, groups, len(shapes), step), ou...  3.65 us
    pallas_call x1, Pallas kernels, punch(): pl.pallas_call(functools.partial(punch_kernel, (groups, depth, held), ear...  3.58 us
    ppermute x4, starting transfers between devices, swap_neighbours(): lax.ppermute(value, axis, pairs + [(j, i) for i, j in pairs])  3.21 us
  transfers between devices with their start and end apart: 18, of which 8 were waited for; matrix products, arithmetic and copies ran while one was open for 0% of the time, Pallas kernels for 21%

profile of v4, /device:TPU:0, one launch (start us, length us, event | category | flops | bytes accessed | tf_op | source)
XLA Modules:
  0.0 80.8 jit_solution(4553939602924554395)
XLA Ops:
  0.0 2.4 %gather_clean.1 = (f32[5,128,128]{2,1,0:T(8,128)S(1)}, f32[5,128,128]{2,1,0:T(8,128)S(1)}, f32[5,128,128]{2,1,0:T(8,128)S(1)}) custom-call(s32[3]{0:T(128)} %spacing.7, s32[3]{0:T(128)} %anchor.7, f32[32,128,128]{2,1,0:T(8,128)} %layers.3), custom_call_target="tpu_custom_call" | custom-call | bytes 5400000 | tf_op jit(solution)/shard_map/gather_clean/pallas_call | solution.py:148
  2.4 0.5 collective-permute-start.4
  2.9 2.6 %collective-permute-start.5 = (f32[5,128,128]{2,1,0:T(8,128)S(1)}, f32[5,128,128]{2,1,0:T(8,128)S(1)}, u32[]{:S(2)}, u32[]{:S(2)}) collective-permute-start(f32[5,128,128]{2,1,0:T(8,128)S(1)} %get-tuple-element.43), channel_id=1, source_target_pairs={{0,16},{8,24},{16,0},{24,8},{1,17},{9,25},{17,1},{25,9},{2,18},{10... | collective-permute-start | bytes 983048 | tf_op jit(solution)/shard_map/ppermute | solution.py:666
  6.2 3.6 %punch.1 = (f32[12,128,128]{2,1,0:T(8,128)S(1)}, f32[12,128,128]{2,1,0:T(8,128)S(1)}, f32[2,1,128,128]{3,2,1,0:T(8,128)S(1)}, f32[1,128,128]{2,1,0:T(8,128)S(1)}...) custom-call(s32[3]{0:T(128)S(1)} %copy-done.4, s32[3]{0:T(128)S(1)} %copy-done.5, ...), custom_call_target="tpu_custom_call" | custom-call | bytes 12600000 | tf_op jit(solution)/shard_map/punch/pallas_call | solution.py:227
  9.8 1.8 %collective-permute-start = (f32[1,128,128]{2,1,0:T(8,128)S(1)}, f32[1,128,128]{2,1,0:T(8,128)S(1)}, u32[]{:S(2)}, u32[]{:S(2)}) collective-permute-start(f32[1,128,128]{2,1,0:T(8,128)S(1)} %get-tuple-element.37), channel_id=1, source_target_pairs={{0,1},{2,3},{4,5},{6,7},{1,0},{3,2},{5,4},{7,6},{8,9},{10,11},{12,... | collective-permute-start | bytes 196616 | tf_op jit(solution)/shard_map/ppermute | solution.py:678
  11.6 0.7 collective-permute-start.1
  12.3 1.9 %collective-permute-done.one.rest_4_.one_side = f32[1,128,128]{2,1,0:T(8,128)S(1)} collective-permute-done((f32[1,128,128]{2,1,0:T(8,128)S(1)}, f32[1,128,128]{2,1,0:T(8,128)S(1)}, u32[]{:S(2)}, u32[]{:S(2)}) %collective-permute-start) | collective-permute-done | bytes 65568 | tf_op jit(solution)/shard_map/ppermute | solution.py:678
  14.3 6.3 %collective-permute-done.6.rest_3_ = f32[5,128,128]{2,1,0:T(8,128)S(1)} collective-permute-done((f32[5,128,128]{2,1,0:T(8,128)S(1)}, f32[5,128,128]{2,1,0:T(8,128)S(1)}, u32[]{:S(2)}, u32[]{:S(2)}) %collective-permute-start.6) | collective-permute-done | bytes 327712 | tf_op jit(solution)/shard_map/ppermute | solution.py:666
  20.5 2.5 %along_x.2 = (f32[8,5,64,128]{3,2,1,0:T(8,128)}, f32[8,128]{1,0:T(8,128)S(1)}) custom-call(bf16[512,512]{1,0:T(8,128)(2,1)S(1)} %copy-done.3, bf16[512,512]{1,0:T(8,128)(2,1)S(1)} %copy-done.2, f32[5,128,128]{2,1,0:T(8,128)S(1)} %get-tuple-element.41.rest_0_, f32[5,128,128]{2,1,0:T(8,128)S(1)} %collective-permute-done.4.rest_1_, ...), custom_call_target="tpu_custom_call" | custom-call | bytes 7200000 | tf_op jit(solution)/shard_map/along_x/pallas_call | solution.py:472
  23.0 5.9 %all-to-all-start = ((f32[8,5,64,128]{3,2,1,0:T(8,128)}), f32[8,5,64,128]{3,2,1,0:T(8,128)}, u32[]{:S(2)}, u32[]{:S(2)}) async-start(f32[8,5,64,128]{3,2,1,0:T(8,128)} %get-tuple-element.56), calls=%async_computation | async-start | bytes 2621440 | tf_op jit(solution)/shard_map/all_to_all | solution.py:697
  29.1 0.7 collective-permute-start.3
  29.7 0.6 collective-permute-done.2.one_end
  30.4 4.7 %fill.1 = (f32[3,128,128]{2,1,0:T(8,128)S(1)}, f32[3,128,128]{2,1,0:T(8,128)S(1)}, f32[3,128,128]{2,1,0:T(8,128)S(1)}, f32[3,128,128]{2,1,0:T(8,128)S(1)}, f32[8,128]{1,0:T(8,128)S(1)}) custom-call(s32[3]{0:T(128)S(1)} %copy-done.4, s32[3]{0:T(128)S(1)} %copy-done.5, s32[1]{0:T(128)S(6)} %copy.11.reach, f32[12,128,128]{2,1,0:T(8,128)S(1)} %get-tuple-element.34.v.v_in, ...), custom_call_target="tpu_custom_call" | custom-call | bytes 25200000 | tf_op jit(solution)/shard_map/fill/pallas_call | solution.py:395
  35.1 5.7 %collective-permute-start.7 = (f32[3,128,128]{2,1,0:T(8,128)S(1)}, f32[3,128,128]{2,1,0:T(8,128)S(1)}, u32[]{:S(2)}, u32[]{:S(2)}) collective-permute-start(f32[3,128,128]{2,1,0:T(8,128)S(1)} %get-tuple-element.47), channel_id=1, source_target_pairs={{0,8},{8,0},{16,24},{24,16},{1,9},{9,1},{17,25},{25,17},{2,10},{10... | collective-permute-start | bytes 589832 | tf_op jit(solution)/shard_map/ppermute | solution.py:666
  40.9 0.7 collective-permute-start.8
  41.6 0.7 collective-permute-start.9
  42.3 6.3 %collective-permute-done.8.rest_2_ = f32[3,128,128]{2,1,0:T(8,128)S(1)} collective-permute-done((f32[3,128,128]{2,1,0:T(8,128)S(1)}, f32[3,128,128]{2,1,0:T(8,128)S(1)}, u32[]{:S(2)}, u32[]{:S(2)}) %collective-permute-start.8) | collective-permute-done | bytes 196640 | tf_op jit(solution)/shard_map/ppermute | solution.py:666
  48.6 2.5 %collective-permute-done.9.rest_3_ = f32[3,128,128]{2,1,0:T(8,128)S(1)} collective-permute-done((f32[3,128,128]{2,1,0:T(8,128)S(1)}, f32[3,128,128]{2,1,0:T(8,128)S(1)}, u32[]{:S(2)}, u32[]{:S(2)}) %collective-permute-start.9) | collective-permute-done | bytes 196640 | tf_op jit(solution)/shard_map/ppermute | solution.py:666
  51.1 1.2 %along_x.3 = (f32[3,64,128]{2,1,0:T(8,128)S(1)}, f32[3,64,128]{2,1,0:T(8,128)S(1)}, f32[3,64,128]{2,1,0:T(8,128)S(1)}, f32[3,64,128]{2,1,0:T(8,128)S(1)}, f32[3,...) custom-call(bf16[512,512]{1,0:T(8,128)(2,1)S(1)} %copy-done.3, ...), custom_call_target="tpu_custom_call" | custom-call | bytes 4320000 | tf_op jit(solution)/shard_map/along_x/pallas_call | solution.py:472
  52.3 2.1 %collective-permute-start.10 = (f32[3,64,128]{2,1,0:T(8,128)S(1)}, f32[3,64,128]{2,1,0:T(8,128)S(1)}, u32[]{:S(2)}, u32[]{:S(2)}) collective-permute-start(f32[3,64,128]{2,1,0:T(8,128)S(1)} %get-tuple-element.52), channel_id=1, source_target_pairs={{0,1},{1,0},{2,3},{3,2},{4,5},{5,4},{6,7},{7,6},{8,9},{9,8},{10,11... | collective-permute-start | bytes 294920 | tf_op jit(solution)/shard_map/ppermute | solution.py:666
  54.3 1.5 %collective-permute-start.11 = (f32[3,64,128]{2,1,0:T(8,128)S(1)}, f32[3,64,128]{2,1,0:T(8,128)S(1)}, u32[]{:S(2)}, u32[]{:S(2)}) collective-permute-start(f32[3,64,128]{2,1,0:T(8,128)S(1)} %get-tuple-element.53), channel_id=1, source_target_pairs={{0,2},{1,3},{2,0},{3,1},{4,6},{5,7},{6,4},{7,5},{8,10},{9,11},{10,... | collective-permute-start | bytes 294920 | tf_op jit(solution)/shard_map/ppermute | solution.py:666
  55.9 4.7 %collective-permute-start.13 = (f32[3,64,128]{2,1,0:T(8,128)S(1)}, f32[3,64,128]{2,1,0:T(8,128)S(1)}, u32[]{:S(2)}, u32[]{:S(2)}) collective-permute-start(f32[3,64,128]{2,1,0:T(8,128)S(1)} %get-tuple-element.55), channel_id=1, source_target_pairs={{0,7},{1,6},{2,5},{3,4},{4,3},{5,2},{6,1},{7,0},{8,15},{9,14},{10,... | collective-permute-start | bytes 294920 | tf_op jit(solution)/shard_map/ppermute | solution.py:666
  60.5 0.6 collective-permute-start.14
  61.1 0.6 collective-permute-start.15
  61.7 1.2 %collective-permute-done.11.rest_2_ = f32[3,64,128]{2,1,0:T(8,128)S(1)} collective-permute-done((f32[3,64,128]{2,1,0:T(8,128)S(1)}, f32[3,64,128]{2,1,0:T(8,128)S(1)}, u32[]{:S(2)}, u32[]{:S(2)}) %collective-permute-start.11) | collective-permute-done | bytes 98336 | tf_op jit(solution)/shard_map/ppermute | solution.py:666
  62.9 0.7 collective-permute-start.16
  63.6 2.2 %copy-done = bf16[8,1024,256]{2,1,0:T(8,128)(2,1)S(1)} copy-done((bf16[8,1024,256]{2,1,0:T(8,128)(2,1)S(1)}, bf16[8,1024,256]{2,1,0:T(8,128)(2,1)}, u32[]{:S(2)}) %copy-start) | copy-done | bytes 4194328
  65.7 5.5 %along_y.1 = (f32[8,64,1024]{2,1,0:T(8,128)}, f32[8,128]{1,0:T(8,128)S(1)}) custom-call(s32[3]{0:T(128)S(1)} %copy-done.4, s32[3]{0:T(128)S(1)} %copy-done.5, bf16[8,1024,256]{2,1,0:T(8,128)(2,1)S(1)} %copy-done, f32[8,5,64,128]{3,2,1,0:T(8,128)} %all-to-all-done.rest_0_, f32[8,128]{1,0:T(8,128)S(1)} %get-tuple-element.57.rest_1_), custom_call_target="tpu_custom_call" | custom-call | bytes 18000000 | tf_op jit(solution)/shard_map/along_y/pallas_call | solution.py:640
  71.3 1.6 %along_y_part.1.partial = f32[4,192,256]{2,1,0:T(8,128)S(1)} custom-call(bf16[8,1024,256]{2,1,0:T(8,128)(2,1)S(1)} %copy-done.1, f32[3,64,128]{2,1,0:T(8,128)S(1)} %get-tuple-element.51.rest_0_, f32[3,64,128]{2,1,0:T(8,128)S(1)} %collective-permute-done.10.rest_1_, f32[3,64,128]{2,1,0:T(8,128)S(1)} %collective-permute-done.11.rest_2_, ...), custom_call_target="tpu_custom_call" | custom-call | bytes 7200000 | tf_op jit(solution)/shard_map/along_y_part/pallas_call | solution.py:516
  72.9 4.6 %collective-permute-done.15.rest_1_ = f32[3,64,128]{2,1,0:T(8,128)S(1)} collective-permute-done((f32[3,64,128]{2,1,0:T(8,128)S(1)}, f32[3,64,128]{2,1,0:T(8,128)S(1)}, u32[]{:S(2)}, u32[]{:S(2)}) %collective-permute-start.15) | collective-permute-done | bytes 98336 | tf_op jit(solution)/shard_map/ppermute | solution.py:666
  77.5 0.8 %collective-permute-done.16.rest_2_ = f32[3,64,128]{2,1,0:T(8,128)S(1)} collective-permute-done((f32[3,64,128]{2,1,0:T(8,128)S(1)}, f32[3,64,128]{2,1,0:T(8,128)S(1)}, u32[]{:S(2)}, u32[]{:S(2)}) %collective-permute-start.16) | collective-permute-done | bytes 98336 | tf_op jit(solution)/shard_map/ppermute | solution.py:666
  78.3 2.5 %along_y_rest.1 = f32[8,64,1024]{2,1,0:T(8,128)} custom-call(s32[3]{0:T(128)S(1)} %copy-done.4, s32[3]{0:T(128)S(1)} %copy-done.5, bf16[8,1024,256]{2,1,0:T(8,128)(2,1)S(1)} %copy-done.1, f32[4,192,256]{2,1,0:T(8,128)S(1)} %along_y_part.1.partial, f32[3,64,128]{2,1,0:T(8,128)S(1)} %collective-permute-done.14.rest_0_, ...), custom_call_target="tpu_custom_call", output_to_operand_aliasing={{}: (7, {})} | custom-call | bytes 7200000 | tf_op jit(solution)/shard_map/along_y_rest/pallas_call | solution.py:568
  (25 shorter events, 0.3 us)
Async XLA Ops:
  0.0 6.2 %copy-start.5 = (s32[3]{0:T(128)S(1)}, s32[3]{0:T(128)}, u32[]{:S(2)}) copy-start(s32[3]{0:T(128)} %anchor.7) | copy-start | bytes 40
  0.0 6.2 %copy-start.4 = (s32[3]{0:T(128)S(1)}, s32[3]{0:T(128)}, u32[]{:S(2)}) copy-start(s32[3]{0:T(128)} %spacing.7) | copy-start | bytes 40
  2.4 11.9 %collective-permute-start.4 = (f32[5,128,128]{2,1,0:T(8,128)S(1)}, f32[5,128,128]{2,1,0:T(8,128)S(1)}, u32[]{:S(2)}, u32[]{:S(2)}) collective-permute-start(f32[5,128,128]{2,1,0:T(8,128)S(1)} %get-tuple-element.42), channel_id=1, source_target_pairs={{0,8},{8,0},{16,24},{24,16},{1,9},{9,1},{17,25},{25,17},{2,10},{10... | collective-permute-start | bytes 983048 | tf_op jit(solution)/shard_map/ppermute | solution.py:666
  2.9 11.3 %collective-permute-start.5 = (f32[5,128,128]{2,1,0:T(8,128)S(1)}, f32[5,128,128]{2,1,0:T(8,128)S(1)}, u32[]{:S(2)}, u32[]{:S(2)}) collective-permute-start(f32[5,128,128]{2,1,0:T(8,128)S(1)} %get-tuple-element.43), channel_id=1, source_target_pairs={{0,16},{8,24},{16,0},{24,8},{1,17},{9,25},{17,1},{25,9},{2,18},{10... | collective-permute-start | bytes 983048 | tf_op jit(solution)/shard_map/ppermute | solution.py:666
  5.5 15.1 %collective-permute-start.6 = (f32[5,128,128]{2,1,0:T(8,128)S(1)}, f32[5,128,128]{2,1,0:T(8,128)S(1)}, u32[]{:S(2)}, u32[]{:S(2)}) collective-permute-start(f32[5,128,128]{2,1,0:T(8,128)S(1)} %get-tuple-element.44), channel_id=1, source_target_pairs={{0,24},{8,16},{16,8},{24,0},{1,25},{9,17},{17,9},{25,1},{2,26},{10... | collective-permute-start | bytes 983048 | tf_op jit(solution)/shard_map/ppermute | solution.py:666
  6.2 14.3 %copy-start.2 = (bf16[512,512]{1,0:T(8,128)(2,1)S(1)}, bf16[512,512]{1,0:T(8,128)(2,1)}, u32[]{:S(2)}) copy-start(bf16[512,512]{1,0:T(8,128)(2,1)} %constant.7.clone.c_low) | copy-start | bytes 1572868
  6.2 14.3 %copy-start.3 = (bf16[512,512]{1,0:T(8,128)(2,1)S(1)}, bf16[512,512]{1,0:T(8,128)(2,1)}, u32[]{:S(2)}) copy-start(bf16[512,512]{1,0:T(8,128)(2,1)} %constant.6.clone.c_high) | copy-start | bytes 1572868
  9.8 4.4 %collective-permute-start = (f32[1,128,128]{2,1,0:T(8,128)S(1)}, f32[1,128,128]{2,1,0:T(8,128)S(1)}, u32[]{:S(2)}, u32[]{:S(2)}) collective-permute-start(f32[1,128,128]{2,1,0:T(8,128)S(1)} %get-tuple-element.37), channel_id=1, source_target_pairs={{0,1},{2,3},{4,5},{6,7},{1,0},{3,2},{5,4},{7,6},{8,9},{10,11},{12,... | collective-permute-start | bytes 196616 | tf_op jit(solution)/shard_map/ppermute | solution.py:678
  11.6 2.6 %collective-permute-start.1 = (f32[1,128,128]{2,1,0:T(8,128)S(1)}, f32[1,128,128]{2,1,0:T(8,128)S(1)}, u32[]{:S(2)}, u32[]{:S(2)}) collective-permute-start(f32[1,128,128]{2,1,0:T(8,128)S(1)} %get-tuple-element.38), channel_id=1, source_target_pairs={{1,2},{3,4},{5,6},{2,1},{4,3},{6,5},{9,10},{11,12},{13,14},{10,9},... | collective-permute-start | bytes 196616 | tf_op jit(solution)/shard_map/ppermute | solution.py:678
  23.0 40.5 %all-to-all-start = ((f32[8,5,64,128]{3,2,1,0:T(8,128)}), f32[8,5,64,128]{3,2,1,0:T(8,128)}, u32[]{:S(2)}, u32[]{:S(2)}) async-start(f32[8,5,64,128]{3,2,1,0:T(8,128)} %get-tuple-element.56), calls=%async_computation | async-start | bytes 2621440 | tf_op jit(solution)/shard_map/all_to_all | solution.py:697
  29.0 1.4 %collective-permute-start.2 = (f32[28,8,128]{2,1,0:T(8,128)S(1)}, f32[28,8,128]{2,1,0:T(8,128)S(1)}, u32[]{:S(2)}, u32[]{:S(2)}) collective-permute-start(f32[28,8,128]{2,1,0:T(8,128)S(1)} %get-tuple-element.39), channel_id=1, source_target_pairs={{0,8},{16,24},{8,0},{24,16},{1,9},{17,25},{9,1},{25,17},{2,10},{18... | collective-permute-start | bytes 344072 | tf_op jit(solution)/shard_map/ppermute | solution.py:678
  29.1 1.3 %collective-permute-start.3 = (f32[28,8,128]{2,1,0:T(8,128)S(1)}, f32[28,8,128]{2,1,0:T(8,128)S(1)}, u32[]{:S(2)}, u32[]{:S(2)}) collective-permute-start(f32[28,8,128]{2,1,0:T(8,128)S(1)} %get-tuple-element.40), channel_id=1, source_target_pairs={{8,16},{16,8},{9,17},{17,9},{10,18},{18,10},{11,19},{19,11},{12,20... | collective-permute-start | bytes 344072 | tf_op jit(solution)/shard_map/ppermute | solution.py:678
  35.1 7.2 %collective-permute-start.7 = (f32[3,128,128]{2,1,0:T(8,128)S(1)}, f32[3,128,128]{2,1,0:T(8,128)S(1)}, u32[]{:S(2)}, u32[]{:S(2)}) collective-permute-start(f32[3,128,128]{2,1,0:T(8,128)S(1)} %get-tuple-element.47), channel_id=1, source_target_pairs={{0,8},{8,0},{16,24},{24,16},{1,9},{9,1},{17,25},{25,17},{2,10},{10... | collective-permute-start | bytes 589832 | tf_op jit(solution)/shard_map/ppermute | solution.py:666
  40.9 7.8 %collective-permute-start.8 = (f32[3,128,128]{2,1,0:T(8,128)S(1)}, f32[3,128,128]{2,1,0:T(8,128)S(1)}, u32[]{:S(2)}, u32[]{:S(2)}) collective-permute-start(f32[3,128,128]{2,1,0:T(8,128)S(1)} %get-tuple-element.48), channel_id=1, source_target_pairs={{0,16},{8,24},{16,0},{24,8},{1,17},{9,25},{17,1},{25,9},{2,18},{10... | collective-permute-start | bytes 589832 | tf_op jit(solution)/shard_map/ppermute | solution.py:666
  41.6 9.5 %collective-permute-start.9 = (f32[3,128,128]{2,1,0:T(8,128)S(1)}, f32[3,128,128]{2,1,0:T(8,128)S(1)}, u32[]{:S(2)}, u32[]{:S(2)}) collective-permute-start(f32[3,128,128]{2,1,0:T(8,128)S(1)} %get-tuple-element.49), channel_id=1, source_target_pairs={{0,24},{8,16},{16,8},{24,0},{1,25},{9,17},{17,9},{25,1},{2,26},{10... | collective-permute-start | bytes 589832 | tf_op jit(solution)/shard_map/ppermute | solution.py:666
  52.3 8.8 %collective-permute-start.10 = (f32[3,64,128]{2,1,0:T(8,128)S(1)}, f32[3,64,128]{2,1,0:T(8,128)S(1)}, u32[]{:S(2)}, u32[]{:S(2)}) collective-permute-start(f32[3,64,128]{2,1,0:T(8,128)S(1)} %get-tuple-element.52), channel_id=1, source_target_pairs={{0,1},{1,0},{2,3},{3,2},{4,5},{5,4},{6,7},{7,6},{8,9},{9,8},{10,11... | collective-permute-start | bytes 294920 | tf_op jit(solution)/shard_map/ppermute | solution.py:666
  54.3 8.5 %collective-permute-start.11 = (f32[3,64,128]{2,1,0:T(8,128)S(1)}, f32[3,64,128]{2,1,0:T(8,128)S(1)}, u32[]{:S(2)}, u32[]{:S(2)}) collective-permute-start(f32[3,64,128]{2,1,0:T(8,128)S(1)} %get-tuple-element.53), channel_id=1, source_target_pairs={{0,2},{1,3},{2,0},{3,1},{4,6},{5,7},{6,4},{7,5},{8,10},{9,11},{10,... | collective-permute-start | bytes 294920 | tf_op jit(solution)/shard_map/ppermute | solution.py:666
  55.8 15.5 %collective-permute-start.12 = (f32[3,64,128]{2,1,0:T(8,128)S(1)}, f32[3,64,128]{2,1,0:T(8,128)S(1)}, u32[]{:S(2)}, u32[]{:S(2)}) collective-permute-start(f32[3,64,128]{2,1,0:T(8,128)S(1)} %get-tuple-element.54), channel_id=1, source_target_pairs={{0,3},{1,2},{2,1},{3,0},{4,7},{5,6},{6,5},{7,4},{8,11},{9,10},{10,... | collective-permute-start | bytes 294920 | tf_op jit(solution)/shard_map/ppermute | solution.py:666
  55.9 15.4 %collective-permute-start.13 = (f32[3,64,128]{2,1,0:T(8,128)S(1)}, f32[3,64,128]{2,1,0:T(8,128)S(1)}, u32[]{:S(2)}, u32[]{:S(2)}) collective-permute-start(f32[3,64,128]{2,1,0:T(8,128)S(1)} %get-tuple-element.55), channel_id=1, source_target_pairs={{0,7},{1,6},{2,5},{3,4},{4,3},{5,2},{6,1},{7,0},{8,15},{9,14},{10,... | collective-permute-start | bytes 294920 | tf_op jit(solution)/shard_map/ppermute | solution.py:666
  60.5 12.3 %collective-permute-start.14 = (f32[3,64,128]{2,1,0:T(8,128)S(1)}, f32[3,64,128]{2,1,0:T(8,128)S(1)}, u32[]{:S(2)}, u32[]{:S(2)}) collective-permute-start(f32[3,64,128]{2,1,0:T(8,128)S(1)} %get-tuple-element.59), channel_id=1, source_target_pairs={{0,6},{1,7},{2,4},{3,5},{4,2},{5,3},{6,0},{7,1},{8,14},{9,15},{10,... | collective-permute-start | bytes 294920 | tf_op jit(solution)/shard_map/ppermute | solution.py:666
  61.1 16.4 %collective-permute-start.15 = (f32[3,64,128]{2,1,0:T(8,128)S(1)}, f32[3,64,128]{2,1,0:T(8,128)S(1)}, u32[]{:S(2)}, u32[]{:S(2)}) collective-permute-start(f32[3,64,128]{2,1,0:T(8,128)S(1)} %get-tuple-element.60), channel_id=1, source_target_pairs={{0,5},{1,4},{2,7},{3,6},{4,1},{5,0},{6,3},{7,2},{8,13},{9,12},{10,... | collective-permute-start | bytes 294920 | tf_op jit(solution)/shard_map/ppermute | solution.py:666
  62.9 15.4 %collective-permute-start.16 = (f32[3,64,128]{2,1,0:T(8,128)S(1)}, f32[3,64,128]{2,1,0:T(8,128)S(1)}, u32[]{:S(2)}, u32[]{:S(2)}) collective-permute-start(f32[3,64,128]{2,1,0:T(8,128)S(1)} %get-tuple-element.61), channel_id=1, source_target_pairs={{0,4},{1,5},{2,6},{3,7},{4,0},{5,1},{6,2},{7,3},{8,12},{9,13},{10,... | collective-permute-start | bytes 294920 | tf_op jit(solution)/shard_map/ppermute | solution.py:666
  63.5 2.2 %copy-start = (bf16[8,1024,256]{2,1,0:T(8,128)(2,1)S(1)}, bf16[8,1024,256]{2,1,0:T(8,128)(2,1)}, u32[]{:S(2)}) copy-start(bf16[8,1024,256]{2,1,0:T(8,128)(2,1)} %constant.8.clone.cosines) | copy-start | bytes 12582916
  65.7 5.5 %copy-start.1 = (bf16[8,1024,256]{2,1,0:T(8,128)(2,1)S(1)}, bf16[8,1024,256]{2,1,0:T(8,128)(2,1)}, u32[]{:S(2)}) copy-start(bf16[8,1024,256]{2,1,0:T(8,128)(2,1)} %constant.8.clone.cosines) | copy-start | bytes 12582916

commit v5 on v4

--- a/solution.py
+++ b/solution.py
@@ -54,7 +54,11 @@
 
 
 def partner(n, size):
-    return n if n < 4 else size + 3 - n
+    if n < 3 or size <= 4:
+        return n
+    if n < 5:
+        return size - 1 if n == 3 else 3
+    return size + 3 - n
 
 
 def column_of(lane):

time: 81.1 us -> 80.5 us (level)
  waiting for transfers between devices: 24.3 us -> 23 us
    ppermute x13, waiting for transfers between devices: 21.7 us -> 20.4 us  [swap(): return lax.ppermute(value, axis, [(i, i ^ k) for i in range(size)])]
where the time goes in v5:
time: 80.5 us; the launch traced here: 80.1 us
  starting transfers between devices  30.2 us (38%)
  Pallas kernels  23.9 us (30%)
  waiting for transfers between devices  23 us (29%)
  local copies, waits for them, and re-layouts  2.21 us (3%)
  between operations  0.83 us (1%)
    ppermute x13, starting transfers between devices, swap(): return lax.ppermute(value, axis, [(i, i ^ k) for i in range(size)])  21.1 us
    ppermute x13, waiting for transfers between devices, swap(): return lax.ppermute(value, axis, [(i, i ^ k) for i in range(size)])  20.4 us
    all_to_all x1, starting transfers between devices, to_rows(): lax.all_to_all(spectrum[0], 'gy', split_axis=0, concat_axis=0, tiled=True)  5.92 us
    pallas_call x1, Pallas kernels, along_y(): pl.pallas_call(functools.partial(y_kernel, slot, chained, apart), out_sha...  5.51 us
    pallas_call x1, Pallas kernels, fill(): pl.pallas_call(functools.partial(fill_kernel, (groups, depth, held, count...  4.75 us
    pallas_call x2, Pallas kernels, along_x(): pl.pallas_call(functools.partial(x_kernel, groups, len(shapes), step), ou...  3.65 us
    pallas_call x1, Pallas kernels, punch(): pl.pallas_call(functools.partial(punch_kernel, (groups, depth, held), ear...  3.58 us
    ppermute x4, starting transfers between devices, swap_neighbours(): lax.ppermute(value, axis, pairs + [(j, i) for i, j in pairs])  3.21 us
  transfers between devices with their start and end apart: 18, of which 8 were waited for; matrix products, arithmetic and copies ran while one was open for 0% of the time, Pallas kernels for 21%

profile of v5, /device:TPU:0, one launch (start us, length us, event | category | flops | bytes accessed | tf_op | source)
XLA Modules:
  0.0 80.1 jit_solution(17641553855543073528)
XLA Ops:
  0.0 2.4 %gather_clean.1 = (f32[5,128,128]{2,1,0:T(8,128)S(1)}, f32[5,128,128]{2,1,0:T(8,128)S(1)}, f32[5,128,128]{2,1,0:T(8,128)S(1)}) custom-call(s32[3]{0:T(128)} %spacing.7, s32[3]{0:T(128)} %anchor.7, f32[32,128,128]{2,1,0:T(8,128)} %layers.3), custom_call_target="tpu_custom_call" | custom-call | bytes 5400000 | tf_op jit(solution)/shard_map/gather_clean/pallas_call | solution.py:152
  2.4 0.5 collective-permute-start.4
  2.9 2.6 %collective-permute-start.5 = (f32[5,128,128]{2,1,0:T(8,128)S(1)}, f32[5,128,128]{2,1,0:T(8,128)S(1)}, u32[]{:S(2)}, u32[]{:S(2)}) collective-permute-start(f32[5,128,128]{2,1,0:T(8,128)S(1)} %get-tuple-element.43), channel_id=1, source_target_pairs={{0,16},{8,24},{16,0},{24,8},{1,17},{9,25},{17,1},{25,9},{2,18},{10... | collective-permute-start | bytes 983048 | tf_op jit(solution)/shard_map/ppermute | solution.py:670
  6.2 3.6 %punch.1 = (f32[12,128,128]{2,1,0:T(8,128)S(1)}, f32[12,128,128]{2,1,0:T(8,128)S(1)}, f32[2,1,128,128]{3,2,1,0:T(8,128)S(1)}, f32[1,128,128]{2,1,0:T(8,128)S(1)}...) custom-call(s32[3]{0:T(128)S(1)} %copy-done.4, s32[3]{0:T(128)S(1)} %copy-done.5, ...), custom_call_target="tpu_custom_call" | custom-call | bytes 12600000 | tf_op jit(solution)/shard_map/punch/pallas_call | solution.py:231
  9.8 1.8 %collective-permute-start = (f32[1,128,128]{2,1,0:T(8,128)S(1)}, f32[1,128,128]{2,1,0:T(8,128)S(1)}, u32[]{:S(2)}, u32[]{:S(2)}) collective-permute-start(f32[1,128,128]{2,1,0:T(8,128)S(1)} %get-tuple-element.37), channel_id=1, source_target_pairs={{0,1},{2,3},{4,5},{6,7},{1,0},{3,2},{5,4},{7,6},{8,9},{10,11},{12,... | collective-permute-start | bytes 196616 | tf_op jit(solution)/shard_map/ppermute | solution.py:682
  11.6 0.7 collective-permute-start.1
  12.3 1.9 %collective-permute-done.one.rest_4_.one_side = f32[1,128,128]{2,1,0:T(8,128)S(1)} collective-permute-done((f32[1,128,128]{2,1,0:T(8,128)S(1)}, f32[1,128,128]{2,1,0:T(8,128)S(1)}, u32[]{:S(2)}, u32[]{:S(2)}) %collective-permute-start) | collective-permute-done | bytes 65568 | tf_op jit(solution)/shard_map/ppermute | solution.py:682
  14.3 6.3 %collective-permute-done.6.rest_3_ = f32[5,128,128]{2,1,0:T(8,128)S(1)} collective-permute-done((f32[5,128,128]{2,1,0:T(8,128)S(1)}, f32[5,128,128]{2,1,0:T(8,128)S(1)}, u32[]{:S(2)}, u32[]{:S(2)}) %collective-permute-start.6) | collective-permute-done | bytes 327712 | tf_op jit(solution)/shard_map/ppermute | solution.py:670
  20.5 2.5 %along_x.2 = (f32[8,5,64,128]{3,2,1,0:T(8,128)}, f32[8,128]{1,0:T(8,128)S(1)}) custom-call(bf16[512,512]{1,0:T(8,128)(2,1)S(1)} %copy-done.3, bf16[512,512]{1,0:T(8,128)(2,1)S(1)} %copy-done.2, f32[5,128,128]{2,1,0:T(8,128)S(1)} %get-tuple-element.41.rest_0_, f32[5,128,128]{2,1,0:T(8,128)S(1)} %collective-permute-done.4.rest_1_, ...), custom_call_target="tpu_custom_call" | custom-call | bytes 7200000 | tf_op jit(solution)/shard_map/along_x/pallas_call | solution.py:476
  23.0 5.9 %all-to-all-start = ((f32[8,5,64,128]{3,2,1,0:T(8,128)}), f32[8,5,64,128]{3,2,1,0:T(8,128)}, u32[]{:S(2)}, u32[]{:S(2)}) async-start(f32[8,5,64,128]{3,2,1,0:T(8,128)} %get-tuple-element.56), calls=%async_computation | async-start | bytes 2621440 | tf_op jit(solution)/shard_map/all_to_all | solution.py:701
  29.1 0.7 collective-permute-start.3
  29.7 0.6 collective-permute-done.2.one_end
  30.4 4.7 %fill.1 = (f32[3,128,128]{2,1,0:T(8,128)S(1)}, f32[3,128,128]{2,1,0:T(8,128)S(1)}, f32[3,128,128]{2,1,0:T(8,128)S(1)}, f32[3,128,128]{2,1,0:T(8,128)S(1)}, f32[8,128]{1,0:T(8,128)S(1)}) custom-call(s32[3]{0:T(128)S(1)} %copy-done.4, s32[3]{0:T(128)S(1)} %copy-done.5, s32[1]{0:T(128)S(6)} %copy.11.reach, f32[12,128,128]{2,1,0:T(8,128)S(1)} %get-tuple-element.34.v.v_in, ...), custom_call_target="tpu_custom_call" | custom-call | bytes 25200000 | tf_op jit(solution)/shard_map/fill/pallas_call | solution.py:399
  35.1 5.7 %collective-permute-start.7 = (f32[3,128,128]{2,1,0:T(8,128)S(1)}, f32[3,128,128]{2,1,0:T(8,128)S(1)}, u32[]{:S(2)}, u32[]{:S(2)}) collective-permute-start(f32[3,128,128]{2,1,0:T(8,128)S(1)} %get-tuple-element.47), channel_id=1, source_target_pairs={{0,8},{8,0},{16,24},{24,16},{1,9},{9,1},{17,25},{25,17},{2,10},{10... | collective-permute-start | bytes 589832 | tf_op jit(solution)/shard_map/ppermute | solution.py:670
  40.9 0.7 collective-permute-start.8
  41.6 0.7 collective-permute-start.9
  42.3 6.3 %collective-permute-done.8.rest_2_ = f32[3,128,128]{2,1,0:T(8,128)S(1)} collective-permute-done((f32[3,128,128]{2,1,0:T(8,128)S(1)}, f32[3,128,128]{2,1,0:T(8,128)S(1)}, u32[]{:S(2)}, u32[]{:S(2)}) %collective-permute-start.8) | collective-permute-done | bytes 196640 | tf_op jit(solution)/shard_map/ppermute | solution.py:670
  48.6 2.5 %collective-permute-done.9.rest_3_ = f32[3,128,128]{2,1,0:T(8,128)S(1)} collective-permute-done((f32[3,128,128]{2,1,0:T(8,128)S(1)}, f32[3,128,128]{2,1,0:T(8,128)S(1)}, u32[]{:S(2)}, u32[]{:S(2)}) %collective-permute-start.9) | collective-permute-done | bytes 196640 | tf_op jit(solution)/shard_map/ppermute | solution.py:670
  51.1 1.2 %along_x.3 = (f32[3,64,128]{2,1,0:T(8,128)S(1)}, f32[3,64,128]{2,1,0:T(8,128)S(1)}, f32[3,64,128]{2,1,0:T(8,128)S(1)}, f32[3,64,128]{2,1,0:T(8,128)S(1)}, f32[3,...) custom-call(bf16[512,512]{1,0:T(8,128)(2,1)S(1)} %copy-done.3, ...), custom_call_target="tpu_custom_call" | custom-call | bytes 4320000 | tf_op jit(solution)/shard_map/along_x/pallas_call | solution.py:476
  52.3 2.1 %collective-permute-start.10 = (f32[3,64,128]{2,1,0:T(8,128)S(1)}, f32[3,64,128]{2,1,0:T(8,128)S(1)}, u32[]{:S(2)}, u32[]{:S(2)}) collective-permute-start(f32[3,64,128]{2,1,0:T(8,128)S(1)} %get-tuple-element.52), channel_id=1, source_target_pairs={{0,1},{1,0},{2,3},{3,2},{4,5},{5,4},{6,7},{7,6},{8,9},{9,8},{10,11... | collective-permute-start | bytes 294920 | tf_op jit(solution)/shard_map/ppermute | solution.py:670
  54.3 1.5 %collective-permute-start.11 = (f32[3,64,128]{2,1,0:T(8,128)S(1)}, f32[3,64,128]{2,1,0:T(8,128)S(1)}, u32[]{:S(2)}, u32[]{:S(2)}) collective-permute-start(f32[3,64,128]{2,1,0:T(8,128)S(1)} %get-tuple-element.53), channel_id=1, source_target_pairs={{0,2},{1,3},{2,0},{3,1},{4,6},{5,7},{6,4},{7,5},{8,10},{9,11},{10,... | collective-permute-start | bytes 294920 | tf_op jit(solution)/shard_map/ppermute | solution.py:670
  55.8 2.4 %collective-permute-start.12 = (f32[3,64,128]{2,1,0:T(8,128)S(1)}, f32[3,64,128]{2,1,0:T(8,128)S(1)}, u32[]{:S(2)}, u32[]{:S(2)}) collective-permute-start(f32[3,64,128]{2,1,0:T(8,128)S(1)} %get-tuple-element.54), channel_id=1, source_target_pairs={{0,7},{1,6},{2,5},{3,4},{4,3},{5,2},{6,1},{7,0},{8,15},{9,14},{10,... | collective-permute-start | bytes 294920 | tf_op jit(solution)/shard_map/ppermute | solution.py:670
  58.2 1.5 %collective-permute-start.13 = (f32[3,64,128]{2,1,0:T(8,128)S(1)}, f32[3,64,128]{2,1,0:T(8,128)S(1)}, u32[]{:S(2)}, u32[]{:S(2)}) collective-permute-start(f32[3,64,128]{2,1,0:T(8,128)S(1)} %get-tuple-element.55), channel_id=1, source_target_pairs={{0,3},{1,2},{2,1},{3,0},{4,7},{5,6},{6,5},{7,4},{8,11},{9,10},{10,... | collective-permute-start | bytes 294920 | tf_op jit(solution)/shard_map/ppermute | solution.py:670
  59.6 0.6 collective-permute-start.14
  60.2 2.4 %collective-permute-start.15 = (f32[3,64,128]{2,1,0:T(8,128)S(1)}, f32[3,64,128]{2,1,0:T(8,128)S(1)}, u32[]{:S(2)}, u32[]{:S(2)}) collective-permute-start(f32[3,64,128]{2,1,0:T(8,128)S(1)} %get-tuple-element.60), channel_id=1, source_target_pairs={{0,5},{1,4},{2,7},{3,6},{4,1},{5,0},{6,3},{7,2},{8,13},{9,12},{10,... | collective-permute-start | bytes 294920 | tf_op jit(solution)/shard_map/ppermute | solution.py:670
  62.6 2.4 %collective-permute-done.11.rest_2_ = f32[3,64,128]{2,1,0:T(8,128)S(1)} collective-permute-done((f32[3,64,128]{2,1,0:T(8,128)S(1)}, f32[3,64,128]{2,1,0:T(8,128)S(1)}, u32[]{:S(2)}, u32[]{:S(2)}) %collective-permute-start.11) | collective-permute-done | bytes 98336 | tf_op jit(solution)/shard_map/ppermute | solution.py:670
  65.0 0.4 collective-permute-start.16
  65.4 2.2 %copy-done = bf16[8,1024,256]{2,1,0:T(8,128)(2,1)S(1)} copy-done((bf16[8,1024,256]{2,1,0:T(8,128)(2,1)S(1)}, bf16[8,1024,256]{2,1,0:T(8,128)(2,1)}, u32[]{:S(2)}) %copy-start) | copy-done | bytes 4194328
  67.6 5.5 %along_y.1 = (f32[8,64,1024]{2,1,0:T(8,128)}, f32[8,128]{1,0:T(8,128)S(1)}) custom-call(s32[3]{0:T(128)S(1)} %copy-done.4, s32[3]{0:T(128)S(1)} %copy-done.5, bf16[8,1024,256]{2,1,0:T(8,128)(2,1)S(1)} %copy-done, f32[8,5,64,128]{3,2,1,0:T(8,128)} %all-to-all-done.rest_0_, f32[8,128]{1,0:T(8,128)S(1)} %get-tuple-element.57.rest_1_), custom_call_target="tpu_custom_call" | custom-call | bytes 18000000 | tf_op jit(solution)/shard_map/along_y/pallas_call | solution.py:644
  73.2 1.6 %along_y_part.1.partial = f32[4,192,256]{2,1,0:T(8,128)S(1)} custom-call(bf16[8,1024,256]{2,1,0:T(8,128)(2,1)S(1)} %copy-done.1, f32[3,64,128]{2,1,0:T(8,128)S(1)} %get-tuple-element.51.rest_0_, f32[3,64,128]{2,1,0:T(8,128)S(1)} %collective-permute-done.10.rest_1_, f32[3,64,128]{2,1,0:T(8,128)S(1)} %collective-permute-done.11.rest_2_, ...), custom_call_target="tpu_custom_call" | custom-call | bytes 7200000 | tf_op jit(solution)/shard_map/along_y_part/pallas_call | solution.py:520
  74.8 2.6 %collective-permute-done.15.rest_1_ = f32[3,64,128]{2,1,0:T(8,128)S(1)} collective-permute-done((f32[3,64,128]{2,1,0:T(8,128)S(1)}, f32[3,64,128]{2,1,0:T(8,128)S(1)}, u32[]{:S(2)}, u32[]{:S(2)}) %collective-permute-start.15) | collective-permute-done | bytes 98336 | tf_op jit(solution)/shard_map/ppermute | solution.py:670
  77.7 2.5 %along_y_rest.1 = f32[8,64,1024]{2,1,0:T(8,128)} custom-call(s32[3]{0:T(128)S(1)} %copy-done.4, s32[3]{0:T(128)S(1)} %copy-done.5, bf16[8,1024,256]{2,1,0:T(8,128)(2,1)S(1)} %copy-done.1, f32[4,192,256]{2,1,0:T(8,128)S(1)} %along_y_part.1.partial, f32[3,64,128]{2,1,0:T(8,128)S(1)} %collective-permute-done.14.rest_0_, ...), custom_call_target="tpu_custom_call", output_to_operand_aliasing={{}: (7, {})} | custom-call | bytes 7200000 | tf_op jit(solution)/shard_map/along_y_rest/pallas_call | solution.py:572
  (25 shorter events, 0.5 us)
Async XLA Ops:
  0.0 6.2 %copy-start.5 = (s32[3]{0:T(128)S(1)}, s32[3]{0:T(128)}, u32[]{:S(2)}) copy-start(s32[3]{0:T(128)} %anchor.7) | copy-start | bytes 40
  0.0 6.2 %copy-start.4 = (s32[3]{0:T(128)S(1)}, s32[3]{0:T(128)}, u32[]{:S(2)}) copy-start(s32[3]{0:T(128)} %spacing.7) | copy-start | bytes 40
  2.4 11.9 %collective-permute-start.4 = (f32[5,128,128]{2,1,0:T(8,128)S(1)}, f32[5,128,128]{2,1,0:T(8,128)S(1)}, u32[]{:S(2)}, u32[]{:S(2)}) collective-permute-start(f32[5,128,128]{2,1,0:T(8,128)S(1)} %get-tuple-element.42), channel_id=1, source_target_pairs={{0,8},{8,0},{16,24},{24,16},{1,9},{9,1},{17,25},{25,17},{2,10},{10... | collective-permute-start | bytes 983048 | tf_op jit(solution)/shard_map/ppermute | solution.py:670
  2.9 11.3 %collective-permute-start.5 = (f32[5,128,128]{2,1,0:T(8,128)S(1)}, f32[5,128,128]{2,1,0:T(8,128)S(1)}, u32[]{:S(2)}, u32[]{:S(2)}) collective-permute-start(f32[5,128,128]{2,1,0:T(8,128)S(1)} %get-tuple-element.43), channel_id=1, source_target_pairs={{0,16},{8,24},{16,0},{24,8},{1,17},{9,25},{17,1},{25,9},{2,18},{10... | collective-permute-start | bytes 983048 | tf_op jit(solution)/shard_map/ppermute | solution.py:670
  5.5 15.1 %collective-permute-start.6 = (f32[5,128,128]{2,1,0:T(8,128)S(1)}, f32[5,128,128]{2,1,0:T(8,128)S(1)}, u32[]{:S(2)}, u32[]{:S(2)}) collective-permute-start(f32[5,128,128]{2,1,0:T(8,128)S(1)} %get-tuple-element.44), channel_id=1, source_target_pairs={{0,24},{8,16},{16,8},{24,0},{1,25},{9,17},{17,9},{25,1},{2,26},{10... | collective-permute-start | bytes 983048 | tf_op jit(solution)/shard_map/ppermute | solution.py:670
  6.2 14.3 %copy-start.2 = (bf16[512,512]{1,0:T(8,128)(2,1)S(1)}, bf16[512,512]{1,0:T(8,128)(2,1)}, u32[]{:S(2)}) copy-start(bf16[512,512]{1,0:T(8,128)(2,1)} %constant.7.clone.c_low) | copy-start | bytes 1572868
  6.2 14.3 %copy-start.3 = (bf16[512,512]{1,0:T(8,128)(2,1)S(1)}, bf16[512,512]{1,0:T(8,128)(2,1)}, u32[]{:S(2)}) copy-start(bf16[512,512]{1,0:T(8,128)(2,1)} %constant.6.clone.c_high) | copy-start | bytes 1572868
  9.8 4.4 %collective-permute-start = (f32[1,128,128]{2,1,0:T(8,128)S(1)}, f32[1,128,128]{2,1,0:T(8,128)S(1)}, u32[]{:S(2)}, u32[]{:S(2)}) collective-permute-start(f32[1,128,128]{2,1,0:T(8,128)S(1)} %get-tuple-element.37), channel_id=1, source_target_pairs={{0,1},{2,3},{4,5},{6,7},{1,0},{3,2},{5,4},{7,6},{8,9},{10,11},{12,... | collective-permute-start | bytes 196616 | tf_op jit(solution)/shard_map/ppermute | solution.py:682
  11.6 2.6 %collective-permute-start.1 = (f32[1,128,128]{2,1,0:T(8,128)S(1)}, f32[1,128,128]{2,1,0:T(8,128)S(1)}, u32[]{:S(2)}, u32[]{:S(2)}) collective-permute-start(f32[1,128,128]{2,1,0:T(8,128)S(1)} %get-tuple-element.38), channel_id=1, source_target_pairs={{1,2},{3,4},{5,6},{2,1},{4,3},{6,5},{9,10},{11,12},{13,14},{10,9},... | collective-permute-start | bytes 196616 | tf_op jit(solution)/shard_map/ppermute | solution.py:682
  23.0 42.4 %all-to-all-start = ((f32[8,5,64,128]{3,2,1,0:T(8,128)}), f32[8,5,64,128]{3,2,1,0:T(8,128)}, u32[]{:S(2)}, u32[]{:S(2)}) async-start(f32[8,5,64,128]{3,2,1,0:T(8,128)} %get-tuple-element.56), calls=%async_computation | async-start | bytes 2621440 | tf_op jit(solution)/shard_map/all_to_all | solution.py:701
  29.0 1.4 %collective-permute-start.2 = (f32[28,8,128]{2,1,0:T(8,128)S(1)}, f32[28,8,128]{2,1,0:T(8,128)S(1)}, u32[]{:S(2)}, u32[]{:S(2)}) collective-permute-start(f32[28,8,128]{2,1,0:T(8,128)S(1)} %get-tuple-element.39), channel_id=1, source_target_pairs={{0,8},{16,24},{8,0},{24,16},{1,9},{17,25},{9,1},{25,17},{2,10},{18... | collective-permute-start | bytes 344072 | tf_op jit(solution)/shard_map/ppermute | solution.py:682
  29.1 1.3 %collective-permute-start.3 = (f32[28,8,128]{2,1,0:T(8,128)S(1)}, f32[28,8,128]{2,1,0:T(8,128)S(1)}, u32[]{:S(2)}, u32[]{:S(2)}) collective-permute-start(f32[28,8,128]{2,1,0:T(8,128)S(1)} %get-tuple-element.40), channel_id=1, source_target_pairs={{8,16},{16,8},{9,17},{17,9},{10,18},{18,10},{11,19},{19,11},{12,20... | collective-permute-start | bytes 344072 | tf_op jit(solution)/shard_map/ppermute | solution.py:682
  35.1 7.2 %collective-permute-start.7 = (f32[3,128,128]{2,1,0:T(8,128)S(1)}, f32[3,128,128]{2,1,0:T(8,128)S(1)}, u32[]{:S(2)}, u32[]{:S(2)}) collective-permute-start(f32[3,128,128]{2,1,0:T(8,128)S(1)} %get-tuple-element.47), channel_id=1, source_target_pairs={{0,8},{8,0},{16,24},{24,16},{1,9},{9,1},{17,25},{25,17},{2,10},{10... | collective-permute-start | bytes 589832 | tf_op jit(solution)/shard_map/ppermute | solution.py:670
  40.9 7.8 %collective-permute-start.8 = (f32[3,128,128]{2,1,0:T(8,128)S(1)}, f32[3,128,128]{2,1,0:T(8,128)S(1)}, u32[]{:S(2)}, u32[]{:S(2)}) collective-permute-start(f32[3,128,128]{2,1,0:T(8,128)S(1)} %get-tuple-element.48), channel_id=1, source_target_pairs={{0,16},{8,24},{16,0},{24,8},{1,17},{9,25},{17,1},{25,9},{2,18},{10... | collective-permute-start | bytes 589832 | tf_op jit(solution)/shard_map/ppermute | solution.py:670
  41.6 9.5 %collective-permute-start.9 = (f32[3,128,128]{2,1,0:T(8,128)S(1)}, f32[3,128,128]{2,1,0:T(8,128)S(1)}, u32[]{:S(2)}, u32[]{:S(2)}) collective-permute-start(f32[3,128,128]{2,1,0:T(8,128)S(1)} %get-tuple-element.49), channel_id=1, source_target_pairs={{0,24},{8,16},{16,8},{24,0},{1,25},{9,17},{17,9},{25,1},{2,26},{10... | collective-permute-start | bytes 589832 | tf_op jit(solution)/shard_map/ppermute | solution.py:670
  52.3 7.9 %collective-permute-start.10 = (f32[3,64,128]{2,1,0:T(8,128)S(1)}, f32[3,64,128]{2,1,0:T(8,128)S(1)}, u32[]{:S(2)}, u32[]{:S(2)}) collective-permute-start(f32[3,64,128]{2,1,0:T(8,128)S(1)} %get-tuple-element.52), channel_id=1, source_target_pairs={{0,1},{1,0},{2,3},{3,2},{4,5},{5,4},{6,7},{7,6},{8,9},{9,8},{10,11... | collective-permute-start | bytes 294920 | tf_op jit(solution)/shard_map/ppermute | solution.py:670
  54.3 10.7 %collective-permute-start.11 = (f32[3,64,128]{2,1,0:T(8,128)S(1)}, f32[3,64,128]{2,1,0:T(8,128)S(1)}, u32[]{:S(2)}, u32[]{:S(2)}) collective-permute-start(f32[3,64,128]{2,1,0:T(8,128)S(1)} %get-tuple-element.53), channel_id=1, source_target_pairs={{0,2},{1,3},{2,0},{3,1},{4,6},{5,7},{6,4},{7,5},{8,10},{9,11},{10,... | collective-permute-start | bytes 294920 | tf_op jit(solution)/shard_map/ppermute | solution.py:670
  55.8 17.3 %collective-permute-start.12 = (f32[3,64,128]{2,1,0:T(8,128)S(1)}, f32[3,64,128]{2,1,0:T(8,128)S(1)}, u32[]{:S(2)}, u32[]{:S(2)}) collective-permute-start(f32[3,64,128]{2,1,0:T(8,128)S(1)} %get-tuple-element.54), channel_id=1, source_target_pairs={{0,7},{1,6},{2,5},{3,4},{4,3},{5,2},{6,1},{7,0},{8,15},{9,14},{10,... | collective-permute-start | bytes 294920 | tf_op jit(solution)/shard_map/ppermute | solution.py:670
  58.2 15.0 %collective-permute-start.13 = (f32[3,64,128]{2,1,0:T(8,128)S(1)}, f32[3,64,128]{2,1,0:T(8,128)S(1)}, u32[]{:S(2)}, u32[]{:S(2)}) collective-permute-start(f32[3,64,128]{2,1,0:T(8,128)S(1)} %get-tuple-element.55), channel_id=1, source_target_pairs={{0,3},{1,2},{2,1},{3,0},{4,7},{5,6},{6,5},{7,4},{8,11},{9,10},{10,... | collective-permute-start | bytes 294920 | tf_op jit(solution)/shard_map/ppermute | solution.py:670
  59.6 15.1 %collective-permute-start.14 = (f32[3,64,128]{2,1,0:T(8,128)S(1)}, f32[3,64,128]{2,1,0:T(8,128)S(1)}, u32[]{:S(2)}, u32[]{:S(2)}) collective-permute-start(f32[3,64,128]{2,1,0:T(8,128)S(1)} %get-tuple-element.59), channel_id=1, source_target_pairs={{0,6},{1,7},{2,4},{3,5},{4,2},{5,3},{6,0},{7,1},{8,14},{9,15},{10,... | collective-permute-start | bytes 294920 | tf_op jit(solution)/shard_map/ppermute | solution.py:670
  60.2 17.2 %collective-permute-start.15 = (f32[3,64,128]{2,1,0:T(8,128)S(1)}, f32[3,64,128]{2,1,0:T(8,128)S(1)}, u32[]{:S(2)}, u32[]{:S(2)}) collective-permute-start(f32[3,64,128]{2,1,0:T(8,128)S(1)} %get-tuple-element.60), channel_id=1, source_target_pairs={{0,5},{1,4},{2,7},{3,6},{4,1},{5,0},{6,3},{7,2},{8,13},{9,12},{10,... | collective-permute-start | bytes 294920 | tf_op jit(solution)/shard_map/ppermute | solution.py:670
  65.0 12.7 %collective-permute-start.16 = (f32[3,64,128]{2,1,0:T(8,128)S(1)}, f32[3,64,128]{2,1,0:T(8,128)S(1)}, u32[]{:S(2)}, u32[]{:S(2)}) collective-permute-start(f32[3,64,128]{2,1,0:T(8,128)S(1)} %get-tuple-element.61), channel_id=1, source_target_pairs={{0,4},{1,5},{2,6},{3,7},{4,0},{5,1},{6,2},{7,3},{8,12},{9,13},{10,... | collective-permute-start | bytes 294920 | tf_op jit(solution)/shard_map/ppermute | solution.py:670
  65.4 2.2 %copy-start = (bf16[8,1024,256]{2,1,0:T(8,128)(2,1)S(1)}, bf16[8,1024,256]{2,1,0:T(8,128)(2,1)}, u32[]{:S(2)}) copy-start(bf16[8,1024,256]{2,1,0:T(8,128)(2,1)} %constant.8.clone.cosines) | copy-start | bytes 12582916
  67.6 5.5 %copy-start.1 = (bf16[8,1024,256]{2,1,0:T(8,128)(2,1)S(1)}, bf16[8,1024,256]{2,1,0:T(8,128)(2,1)}, u32[]{:S(2)}) copy-start(bf16[8,1024,256]{2,1,0:T(8,128)(2,1)} %constant.8.clone.cosines) | copy-start | bytes 12582916

commit v6 on v5

--- a/solution.py
+++ b/solution.py
@@ -71,7 +71,7 @@
 
 
 def early_pieces(parts):
-    return parts // 2 + 1
+    return parts // 2 + 2
 
 
 def partners(size):

time: 80.5 us -> 80.2 us (level)
  no operation moved by 1% of the time
where the time goes in v6:
time: 80.2 us; the launch traced here: 79.8 us
  starting transfers between devices  30.2 us (38%)
  Pallas kernels  23.6 us (29%)
  waiting for transfers between devices  23 us (29%)
  local copies, waits for them, and re-layouts  2.21 us (3%)
  between operations  0.83 us (1%)
    ppermute x13, starting transfers between devices, swap(): return lax.ppermute(value, axis, [(i, i ^ k) for i in range(size)])  21.1 us
    ppermute x13, waiting for transfers between devices, swap(): return lax.ppermute(value, axis, [(i, i ^ k) for i in range(size)])  20.4 us
    all_to_all x1, starting transfers between devices, to_rows(): lax.all_to_all(spectrum[0], 'gy', split_axis=0, concat_axis=0, tiled=True)  5.92 us
    pallas_call x1, Pallas kernels, along_y(): pl.pallas_call(functools.partial(y_kernel, slot, chained, apart), out_sha...  5.51 us
    pallas_call x1, Pallas kernels, fill(): pl.pallas_call(functools.partial(fill_kernel, (groups, depth, held, count...  4.75 us
    pallas_call x2, Pallas kernels, along_x(): pl.pallas_call(functools.partial(x_kernel, groups, len(shapes), step), ou...  3.65 us
    pallas_call x1, Pallas kernels, punch(): pl.pallas_call(functools.partial(punch_kernel, (groups, depth, held), ear...  3.58 us
    ppermute x4, starting transfers between devices, swap_neighbours(): lax.ppermute(value, axis, pairs + [(j, i) for i, j in pairs])  3.21 us
  transfers between devices with their start and end apart: 18, of which 8 were waited for; matrix products, arithmetic and copies ran while one was open for 0% of the time, Pallas kernels for 21%

profile of v6, /device:TPU:0, one launch (start us, length us, event | category | flops | bytes accessed | tf_op | source)
XLA Modules:
  0.0 79.8 jit_solution(14344742872056888093)
XLA Ops:
  0.0 2.4 %gather_clean.1 = (f32[5,128,128]{2,1,0:T(8,128)S(1)}, f32[5,128,128]{2,1,0:T(8,128)S(1)}, f32[5,128,128]{2,1,0:T(8,128)S(1)}) custom-call(s32[3]{0:T(128)} %spacing.7, s32[3]{0:T(128)} %anchor.7, f32[32,128,128]{2,1,0:T(8,128)} %layers.3), custom_call_target="tpu_custom_call" | custom-call | bytes 5400000 | tf_op jit(solution)/shard_map/gather_clean/pallas_call | solution.py:152
  2.4 0.5 collective-permute-start.4
  2.9 2.6 %collective-permute-start.5 = (f32[5,128,128]{2,1,0:T(8,128)S(1)}, f32[5,128,128]{2,1,0:T(8,128)S(1)}, u32[]{:S(2)}, u32[]{:S(2)}) collective-permute-start(f32[5,128,128]{2,1,0:T(8,128)S(1)} %get-tuple-element.43), channel_id=1, source_target_pairs={{0,16},{8,24},{16,0},{24,8},{1,17},{9,25},{17,1},{25,9},{2,18},{10... | collective-permute-start | bytes 983048 | tf_op jit(solution)/shard_map/ppermute | solution.py:670
  6.2 3.6 %punch.1 = (f32[12,128,128]{2,1,0:T(8,128)S(1)}, f32[12,128,128]{2,1,0:T(8,128)S(1)}, f32[2,1,128,128]{3,2,1,0:T(8,128)S(1)}, f32[1,128,128]{2,1,0:T(8,128)S(1)}...) custom-call(s32[3]{0:T(128)S(1)} %copy-done.4, s32[3]{0:T(128)S(1)} %copy-done.5, ...), custom_call_target="tpu_custom_call" | custom-call | bytes 12600000 | tf_op jit(solution)/shard_map/punch/pallas_call | solution.py:231
  9.8 1.8 %collective-permute-start = (f32[1,128,128]{2,1,0:T(8,128)S(1)}, f32[1,128,128]{2,1,0:T(8,128)S(1)}, u32[]{:S(2)}, u32[]{:S(2)}) collective-permute-start(f32[1,128,128]{2,1,0:T(8,128)S(1)} %get-tuple-element.37), channel_id=1, source_target_pairs={{0,1},{2,3},{4,5},{6,7},{1,0},{3,2},{5,4},{7,6},{8,9},{10,11},{12,... | collective-permute-start | bytes 196616 | tf_op jit(solution)/shard_map/ppermute | solution.py:682
  11.6 0.7 collective-permute-start.1
  12.3 1.9 %collective-permute-done.one.rest_4_.one_side = f32[1,128,128]{2,1,0:T(8,128)S(1)} collective-permute-done((f32[1,128,128]{2,1,0:T(8,128)S(1)}, f32[1,128,128]{2,1,0:T(8,128)S(1)}, u32[]{:S(2)}, u32[]{:S(2)}) %collective-permute-start) | collective-permute-done | bytes 65568 | tf_op jit(solution)/shard_map/ppermute | solution.py:682
  14.3 6.3 %collective-permute-done.6.rest_3_ = f32[5,128,128]{2,1,0:T(8,128)S(1)} collective-permute-done((f32[5,128,128]{2,1,0:T(8,128)S(1)}, f32[5,128,128]{2,1,0:T(8,128)S(1)}, u32[]{:S(2)}, u32[]{:S(2)}) %collective-permute-start.6) | collective-permute-done | bytes 327712 | tf_op jit(solution)/shard_map/ppermute | solution.py:670
  20.5 2.5 %along_x.2 = (f32[8,5,64,128]{3,2,1,0:T(8,128)}, f32[8,128]{1,0:T(8,128)S(1)}) custom-call(bf16[512,512]{1,0:T(8,128)(2,1)S(1)} %copy-done.3, bf16[512,512]{1,0:T(8,128)(2,1)S(1)} %copy-done.2, f32[5,128,128]{2,1,0:T(8,128)S(1)} %get-tuple-element.41.rest_0_, f32[5,128,128]{2,1,0:T(8,128)S(1)} %collective-permute-done.4.rest_1_, ...), custom_call_target="tpu_custom_call" | custom-call | bytes 7200000 | tf_op jit(solution)/shard_map/along_x/pallas_call | solution.py:476
  23.0 5.9 %all-to-all-start = ((f32[8,5,64,128]{3,2,1,0:T(8,128)}), f32[8,5,64,128]{3,2,1,0:T(8,128)}, u32[]{:S(2)}, u32[]{:S(2)}) async-start(f32[8,5,64,128]{3,2,1,0:T(8,128)} %get-tuple-element.57), calls=%async_computation | async-start | bytes 2621440 | tf_op jit(solution)/shard_map/all_to_all | solution.py:701
  29.1 0.7 collective-permute-start.3
  29.7 0.6 collective-permute-done.2.one_end
  30.4 4.7 %fill.1 = (f32[3,128,128]{2,1,0:T(8,128)S(1)}, f32[3,128,128]{2,1,0:T(8,128)S(1)}, f32[3,128,128]{2,1,0:T(8,128)S(1)}, f32[3,128,128]{2,1,0:T(8,128)S(1)}, f32[8,128]{1,0:T(8,128)S(1)}) custom-call(s32[3]{0:T(128)S(1)} %copy-done.4, s32[3]{0:T(128)S(1)} %copy-done.5, s32[1]{0:T(128)S(6)} %copy.11.reach, f32[12,128,128]{2,1,0:T(8,128)S(1)} %get-tuple-element.34.v.v_in, ...), custom_call_target="tpu_custom_call" | custom-call | bytes 25200000 | tf_op jit(solution)/shard_map/fill/pallas_call | solution.py:399
  35.1 5.7 %collective-permute-start.7 = (f32[3,128,128]{2,1,0:T(8,128)S(1)}, f32[3,128,128]{2,1,0:T(8,128)S(1)}, u32[]{:S(2)}, u32[]{:S(2)}) collective-permute-start(f32[3,128,128]{2,1,0:T(8,128)S(1)} %get-tuple-element.47), channel_id=1, source_target_pairs={{0,8},{8,0},{16,24},{24,16},{1,9},{9,1},{17,25},{25,17},{2,10},{10... | collective-permute-start | bytes 589832 | tf_op jit(solution)/shard_map/ppermute | solution.py:670
  40.9 0.7 collective-permute-start.8
  41.6 0.7 collective-permute-start.9
  42.3 6.3 %collective-permute-done.8.rest_2_ = f32[3,128,128]{2,1,0:T(8,128)S(1)} collective-permute-done((f32[3,128,128]{2,1,0:T(8,128)S(1)}, f32[3,128,128]{2,1,0:T(8,128)S(1)}, u32[]{:S(2)}, u32[]{:S(2)}) %collective-permute-start.8) | collective-permute-done | bytes 196640 | tf_op jit(solution)/shard_map/ppermute | solution.py:670
  48.6 2.5 %collective-permute-done.9.rest_3_ = f32[3,128,128]{2,1,0:T(8,128)S(1)} collective-permute-done((f32[3,128,128]{2,1,0:T(8,128)S(1)}, f32[3,128,128]{2,1,0:T(8,128)S(1)}, u32[]{:S(2)}, u32[]{:S(2)}) %collective-permute-start.9) | collective-permute-done | bytes 196640 | tf_op jit(solution)/shard_map/ppermute | solution.py:670
  51.1 1.2 %along_x.3 = (f32[3,64,128]{2,1,0:T(8,128)S(1)}, f32[3,64,128]{2,1,0:T(8,128)S(1)}, f32[3,64,128]{2,1,0:T(8,128)S(1)}, f32[3,64,128]{2,1,0:T(8,128)S(1)}, f32[3,...) custom-call(bf16[512,512]{1,0:T(8,128)(2,1)S(1)} %copy-done.3, ...), custom_call_target="tpu_custom_call" | custom-call | bytes 4320000 | tf_op jit(solution)/shard_map/along_x/pallas_call | solution.py:476
  52.3 2.1 %collective-permute-start.10 = (f32[3,64,128]{2,1,0:T(8,128)S(1)}, f32[3,64,128]{2,1,0:T(8,128)S(1)}, u32[]{:S(2)}, u32[]{:S(2)}) collective-permute-start(f32[3,64,128]{2,1,0:T(8,128)S(1)} %get-tuple-element.52), channel_id=1, source_target_pairs={{0,1},{1,0},{2,3},{3,2},{4,5},{5,4},{6,7},{7,6},{8,9},{9,8},{10,11... | collective-permute-start | bytes 294920 | tf_op jit(solution)/shard_map/ppermute | solution.py:670
  54.3 1.5 %collective-permute-start.11 = (f32[3,64,128]{2,1,0:T(8,128)S(1)}, f32[3,64,128]{2,1,0:T(8,128)S(1)}, u32[]{:S(2)}, u32[]{:S(2)}) collective-permute-start(f32[3,64,128]{2,1,0:T(8,128)S(1)} %get-tuple-element.53), channel_id=1, source_target_pairs={{0,2},{1,3},{2,0},{3,1},{4,6},{5,7},{6,4},{7,5},{8,10},{9,11},{10,... | collective-permute-start | bytes 294920 | tf_op jit(solution)/shard_map/ppermute | solution.py:670
  55.8 2.4 %collective-permute-start.12 = (f32[3,64,128]{2,1,0:T(8,128)S(1)}, f32[3,64,128]{2,1,0:T(8,128)S(1)}, u32[]{:S(2)}, u32[]{:S(2)}) collective-permute-start(f32[3,64,128]{2,1,0:T(8,128)S(1)} %get-tuple-element.54), channel_id=1, source_target_pairs={{0,7},{1,6},{2,5},{3,4},{4,3},{5,2},{6,1},{7,0},{8,15},{9,14},{10,... | collective-permute-start | bytes 294920 | tf_op jit(solution)/shard_map/ppermute | solution.py:670
  58.2 1.5 %collective-permute-start.13 = (f32[3,64,128]{2,1,0:T(8,128)S(1)}, f32[3,64,128]{2,1,0:T(8,128)S(1)}, u32[]{:S(2)}, u32[]{:S(2)}) collective-permute-start(f32[3,64,128]{2,1,0:T(8,128)S(1)} %get-tuple-element.55), channel_id=1, source_target_pairs={{0,3},{1,2},{2,1},{3,0},{4,7},{5,6},{6,5},{7,4},{8,11},{9,10},{10,... | collective-permute-start | bytes 294920 | tf_op jit(solution)/shard_map/ppermute | solution.py:670
  59.6 0.6 collective-permute-start.14
  60.2 2.4 %collective-permute-start.15 = (f32[3,64,128]{2,1,0:T(8,128)S(1)}, f32[3,64,128]{2,1,0:T(8,128)S(1)}, u32[]{:S(2)}, u32[]{:S(2)}) collective-permute-start(f32[3,64,128]{2,1,0:T(8,128)S(1)} %get-tuple-element.60), channel_id=1, source_target_pairs={{0,5},{1,4},{2,7},{3,6},{4,1},{5,0},{6,3},{7,2},{8,13},{9,12},{10,... | collective-permute-start | bytes 294920 | tf_op jit(solution)/shard_map/ppermute | solution.py:670
  62.6 2.4 %collective-permute-done.11.rest_2_ = f32[3,64,128]{2,1,0:T(8,128)S(1)} collective-permute-done((f32[3,64,128]{2,1,0:T(8,128)S(1)}, f32[3,64,128]{2,1,0:T(8,128)S(1)}, u32[]{:S(2)}, u32[]{:S(2)}) %collective-permute-start.11) | collective-permute-done | bytes 98336 | tf_op jit(solution)/shard_map/ppermute | solution.py:670
  65.0 0.4 collective-permute-start.16
  65.4 2.2 %copy-done = bf16[8,1024,256]{2,1,0:T(8,128)(2,1)S(1)} copy-done((bf16[8,1024,256]{2,1,0:T(8,128)(2,1)S(1)}, bf16[8,1024,256]{2,1,0:T(8,128)(2,1)}, u32[]{:S(2)}) %copy-start) | copy-done | bytes 4194328
  67.6 5.5 %along_y.1 = (f32[8,64,1024]{2,1,0:T(8,128)}, f32[8,128]{1,0:T(8,128)S(1)}) custom-call(s32[3]{0:T(128)S(1)} %copy-done.4, s32[3]{0:T(128)S(1)} %copy-done.5, bf16[8,1024,256]{2,1,0:T(8,128)(2,1)S(1)} %copy-done, f32[8,5,64,128]{3,2,1,0:T(8,128)} %all-to-all-done.rest_0_, f32[8,128]{1,0:T(8,128)S(1)} %get-tuple-element.58.rest_1_), custom_call_target="tpu_custom_call" | custom-call | bytes 18000000 | tf_op jit(solution)/shard_map/along_y/pallas_call | solution.py:644
  73.2 1.6 %along_y_part.1.partial = f32[4,192,256]{2,1,0:T(8,128)S(1)} custom-call(bf16[8,1024,256]{2,1,0:T(8,128)(2,1)S(1)} %copy-done.1, f32[3,64,128]{2,1,0:T(8,128)S(1)} %get-tuple-element.51.rest_0_, f32[3,64,128]{2,1,0:T(8,128)S(1)} %collective-permute-done.10.rest_1_, f32[3,64,128]{2,1,0:T(8,128)S(1)} %collective-permute-done.11.rest_2_, ...), custom_call_target="tpu_custom_call" | custom-call | bytes 7200000 | tf_op jit(solution)/shard_map/along_y_part/pallas_call | solution.py:520
  74.8 2.6 %collective-permute-done.15.rest_0_ = f32[3,64,128]{2,1,0:T(8,128)S(1)} collective-permute-done((f32[3,64,128]{2,1,0:T(8,128)S(1)}, f32[3,64,128]{2,1,0:T(8,128)S(1)}, u32[]{:S(2)}, u32[]{:S(2)}) %collective-permute-start.15) | collective-permute-done | bytes 98336 | tf_op jit(solution)/shard_map/ppermute | solution.py:670
  77.7 2.2 %along_y_rest.1 = f32[8,64,1024]{2,1,0:T(8,128)} custom-call(s32[3]{0:T(128)S(1)} %copy-done.4, s32[3]{0:T(128)S(1)} %copy-done.5, bf16[8,1024,256]{2,1,0:T(8,128)(2,1)S(1)} %copy-done.1, f32[4,192,256]{2,1,0:T(8,128)S(1)} %along_y_part.1.partial, f32[3,64,128]{2,1,0:T(8,128)S(1)} %collective-permute-done.15.rest_0_, ...), custom_call_target="tpu_custom_call", output_to_operand_aliasing={{}: (6, {})} | custom-call | bytes 7200000 | tf_op jit(solution)/shard_map/along_y_rest/pallas_call | solution.py:572
  (25 shorter events, 0.5 us)
Async XLA Ops:
  0.0 6.2 %copy-start.5 = (s32[3]{0:T(128)S(1)}, s32[3]{0:T(128)}, u32[]{:S(2)}) copy-start(s32[3]{0:T(128)} %anchor.7) | copy-start | bytes 40
  0.0 6.2 %copy-start.4 = (s32[3]{0:T(128)S(1)}, s32[3]{0:T(128)}, u32[]{:S(2)}) copy-start(s32[3]{0:T(128)} %spacing.7) | copy-start | bytes 40
  2.4 11.9 %collective-permute-start.4 = (f32[5,128,128]{2,1,0:T(8,128)S(1)}, f32[5,128,128]{2,1,0:T(8,128)S(1)}, u32[]{:S(2)}, u32[]{:S(2)}) collective-permute-start(f32[5,128,128]{2,1,0:T(8,128)S(1)} %get-tuple-element.42), channel_id=1, source_target_pairs={{0,8},{8,0},{16,24},{24,16},{1,9},{9,1},{17,25},{25,17},{2,10},{10... | collective-permute-start | bytes 983048 | tf_op jit(solution)/shard_map/ppermute | solution.py:670
  2.9 11.3 %collective-permute-start.5 = (f32[5,128,128]{2,1,0:T(8,128)S(1)}, f32[5,128,128]{2,1,0:T(8,128)S(1)}, u32[]{:S(2)}, u32[]{:S(2)}) collective-permute-start(f32[5,128,128]{2,1,0:T(8,128)S(1)} %get-tuple-element.43), channel_id=1, source_target_pairs={{0,16},{8,24},{16,0},{24,8},{1,17},{9,25},{17,1},{25,9},{2,18},{10... | collective-permute-start | bytes 983048 | tf_op jit(solution)/shard_map/ppermute | solution.py:670
  5.5 15.1 %collective-permute-start.6 = (f32[5,128,128]{2,1,0:T(8,128)S(1)}, f32[5,128,128]{2,1,0:T(8,128)S(1)}, u32[]{:S(2)}, u32[]{:S(2)}) collective-permute-start(f32[5,128,128]{2,1,0:T(8,128)S(1)} %get-tuple-element.44), channel_id=1, source_target_pairs={{0,24},{8,16},{16,8},{24,0},{1,25},{9,17},{17,9},{25,1},{2,26},{10... | collective-permute-start | bytes 983048 | tf_op jit(solution)/shard_map/ppermute | solution.py:670
  6.2 14.3 %copy-start.2 = (bf16[512,512]{1,0:T(8,128)(2,1)S(1)}, bf16[512,512]{1,0:T(8,128)(2,1)}, u32[]{:S(2)}) copy-start(bf16[512,512]{1,0:T(8,128)(2,1)} %constant.7.clone.c_low) | copy-start | bytes 1572868
  6.2 14.3 %copy-start.3 = (bf16[512,512]{1,0:T(8,128)(2,1)S(1)}, bf16[512,512]{1,0:T(8,128)(2,1)}, u32[]{:S(2)}) copy-start(bf16[512,512]{1,0:T(8,128)(2,1)} %constant.6.clone.c_high) | copy-start | bytes 1572868
  9.8 4.4 %collective-permute-start = (f32[1,128,128]{2,1,0:T(8,128)S(1)}, f32[1,128,128]{2,1,0:T(8,128)S(1)}, u32[]{:S(2)}, u32[]{:S(2)}) collective-permute-start(f32[1,128,128]{2,1,0:T(8,128)S(1)} %get-tuple-element.37), channel_id=1, source_target_pairs={{0,1},{2,3},{4,5},{6,7},{1,0},{3,2},{5,4},{7,6},{8,9},{10,11},{12,... | collective-permute-start | bytes 196616 | tf_op jit(solution)/shard_map/ppermute | solution.py:682
  11.6 2.6 %collective-permute-start.1 = (f32[1,128,128]{2,1,0:T(8,128)S(1)}, f32[1,128,128]{2,1,0:T(8,128)S(1)}, u32[]{:S(2)}, u32[]{:S(2)}) collective-permute-start(f32[1,128,128]{2,1,0:T(8,128)S(1)} %get-tuple-element.38), channel_id=1, source_target_pairs={{1,2},{3,4},{5,6},{2,1},{4,3},{6,5},{9,10},{11,12},{13,14},{10,9},... | collective-permute-start | bytes 196616 | tf_op jit(solution)/shard_map/ppermute | solution.py:682
  23.0 42.4 %all-to-all-start = ((f32[8,5,64,128]{3,2,1,0:T(8,128)}), f32[8,5,64,128]{3,2,1,0:T(8,128)}, u32[]{:S(2)}, u32[]{:S(2)}) async-start(f32[8,5,64,128]{3,2,1,0:T(8,128)} %get-tuple-element.57), calls=%async_computation | async-start | bytes 2621440 | tf_op jit(solution)/shard_map/all_to_all | solution.py:701
  29.0 1.4 %collective-permute-start.2 = (f32[28,8,128]{2,1,0:T(8,128)S(1)}, f32[28,8,128]{2,1,0:T(8,128)S(1)}, u32[]{:S(2)}, u32[]{:S(2)}) collective-permute-start(f32[28,8,128]{2,1,0:T(8,128)S(1)} %get-tuple-element.39), channel_id=1, source_target_pairs={{0,8},{16,24},{8,0},{24,16},{1,9},{17,25},{9,1},{25,17},{2,10},{18... | collective-permute-start | bytes 344072 | tf_op jit(solution)/shard_map/ppermute | solution.py:682
  29.1 1.3 %collective-permute-start.3 = (f32[28,8,128]{2,1,0:T(8,128)S(1)}, f32[28,8,128]{2,1,0:T(8,128)S(1)}, u32[]{:S(2)}, u32[]{:S(2)}) collective-permute-start(f32[28,8,128]{2,1,0:T(8,128)S(1)} %get-tuple-element.40), channel_id=1, source_target_pairs={{8,16},{16,8},{9,17},{17,9},{10,18},{18,10},{11,19},{19,11},{12,20... | collective-permute-start | bytes 344072 | tf_op jit(solution)/shard_map/ppermute | solution.py:682
  35.1 7.2 %collective-permute-start.7 = (f32[3,128,128]{2,1,0:T(8,128)S(1)}, f32[3,128,128]{2,1,0:T(8,128)S(1)}, u32[]{:S(2)}, u32[]{:S(2)}) collective-permute-start(f32[3,128,128]{2,1,0:T(8,128)S(1)} %get-tuple-element.47), channel_id=1, source_target_pairs={{0,8},{8,0},{16,24},{24,16},{1,9},{9,1},{17,25},{25,17},{2,10},{10... | collective-permute-start | bytes 589832 | tf_op jit(solution)/shard_map/ppermute | solution.py:670
  40.9 7.8 %collective-permute-start.8 = (f32[3,128,128]{2,1,0:T(8,128)S(1)}, f32[3,128,128]{2,1,0:T(8,128)S(1)}, u32[]{:S(2)}, u32[]{:S(2)}) collective-permute-start(f32[3,128,128]{2,1,0:T(8,128)S(1)} %get-tuple-element.48), channel_id=1, source_target_pairs={{0,16},{8,24},{16,0},{24,8},{1,17},{9,25},{17,1},{25,9},{2,18},{10... | collective-permute-start | bytes 589832 | tf_op jit(solution)/shard_map/ppermute | solution.py:670
  41.6 9.5 %collective-permute-start.9 = (f32[3,128,128]{2,1,0:T(8,128)S(1)}, f32[3,128,128]{2,1,0:T(8,128)S(1)}, u32[]{:S(2)}, u32[]{:S(2)}) collective-permute-start(f32[3,128,128]{2,1,0:T(8,128)S(1)} %get-tuple-element.49), channel_id=1, source_target_pairs={{0,24},{8,16},{16,8},{24,0},{1,25},{9,17},{17,9},{25,1},{2,26},{10... | collective-permute-start | bytes 589832 | tf_op jit(solution)/shard_map/ppermute | solution.py:670
  52.3 7.9 %collective-permute-start.10 = (f32[3,64,128]{2,1,0:T(8,128)S(1)}, f32[3,64,128]{2,1,0:T(8,128)S(1)}, u32[]{:S(2)}, u32[]{:S(2)}) collective-permute-start(f32[3,64,128]{2,1,0:T(8,128)S(1)} %get-tuple-element.52), channel_id=1, source_target_pairs={{0,1},{1,0},{2,3},{3,2},{4,5},{5,4},{6,7},{7,6},{8,9},{9,8},{10,11... | collective-permute-start | bytes 294920 | tf_op jit(solution)/shard_map/ppermute | solution.py:670
  54.3 10.7 %collective-permute-start.11 = (f32[3,64,128]{2,1,0:T(8,128)S(1)}, f32[3,64,128]{2,1,0:T(8,128)S(1)}, u32[]{:S(2)}, u32[]{:S(2)}) collective-permute-start(f32[3,64,128]{2,1,0:T(8,128)S(1)} %get-tuple-element.53), channel_id=1, source_target_pairs={{0,2},{1,3},{2,0},{3,1},{4,6},{5,7},{6,4},{7,5},{8,10},{9,11},{10,... | collective-permute-start | bytes 294920 | tf_op jit(solution)/shard_map/ppermute | solution.py:670
  55.8 17.3 %collective-permute-start.12 = (f32[3,64,128]{2,1,0:T(8,128)S(1)}, f32[3,64,128]{2,1,0:T(8,128)S(1)}, u32[]{:S(2)}, u32[]{:S(2)}) collective-permute-start(f32[3,64,128]{2,1,0:T(8,128)S(1)} %get-tuple-element.54), channel_id=1, source_target_pairs={{0,7},{1,6},{2,5},{3,4},{4,3},{5,2},{6,1},{7,0},{8,15},{9,14},{10,... | collective-permute-start | bytes 294920 | tf_op jit(solution)/shard_map/ppermute | solution.py:670
  58.2 15.0 %collective-permute-start.13 = (f32[3,64,128]{2,1,0:T(8,128)S(1)}, f32[3,64,128]{2,1,0:T(8,128)S(1)}, u32[]{:S(2)}, u32[]{:S(2)}) collective-permute-start(f32[3,64,128]{2,1,0:T(8,128)S(1)} %get-tuple-element.55), channel_id=1, source_target_pairs={{0,3},{1,2},{2,1},{3,0},{4,7},{5,6},{6,5},{7,4},{8,11},{9,10},{10,... | collective-permute-start | bytes 294920 | tf_op jit(solution)/shard_map/ppermute | solution.py:670
  59.6 13.5 %collective-permute-start.14 = (f32[3,64,128]{2,1,0:T(8,128)S(1)}, f32[3,64,128]{2,1,0:T(8,128)S(1)}, u32[]{:S(2)}, u32[]{:S(2)}) collective-permute-start(f32[3,64,128]{2,1,0:T(8,128)S(1)} %get-tuple-element.56), channel_id=1, source_target_pairs={{0,6},{1,7},{2,4},{3,5},{4,2},{5,3},{6,0},{7,1},{8,14},{9,15},{10,... | collective-permute-start | bytes 294920 | tf_op jit(solution)/shard_map/ppermute | solution.py:670
  60.2 17.2 %collective-permute-start.15 = (f32[3,64,128]{2,1,0:T(8,128)S(1)}, f32[3,64,128]{2,1,0:T(8,128)S(1)}, u32[]{:S(2)}, u32[]{:S(2)}) collective-permute-start(f32[3,64,128]{2,1,0:T(8,128)S(1)} %get-tuple-element.60), channel_id=1, source_target_pairs={{0,5},{1,4},{2,7},{3,6},{4,1},{5,0},{6,3},{7,2},{8,13},{9,12},{10,... | collective-permute-start | bytes 294920 | tf_op jit(solution)/shard_map/ppermute | solution.py:670
  65.0 12.7 %collective-permute-start.16 = (f32[3,64,128]{2,1,0:T(8,128)S(1)}, f32[3,64,128]{2,1,0:T(8,128)S(1)}, u32[]{:S(2)}, u32[]{:S(2)}) collective-permute-start(f32[3,64,128]{2,1,0:T(8,128)S(1)} %get-tuple-element.61), channel_id=1, source_target_pairs={{0,4},{1,5},{2,6},{3,7},{4,0},{5,1},{6,2},{7,3},{8,12},{9,13},{10,... | collective-permute-start | bytes 294920 | tf_op jit(solution)/shard_map/ppermute | solution.py:670
  65.4 2.2 %copy-start = (bf16[8,1024,256]{2,1,0:T(8,128)(2,1)S(1)}, bf16[8,1024,256]{2,1,0:T(8,128)(2,1)}, u32[]{:S(2)}) copy-start(bf16[8,1024,256]{2,1,0:T(8,128)(2,1)} %constant.8.clone.cosines) | copy-start | bytes 12582916
  67.6 5.6 %copy-start.1 = (bf16[8,1024,256]{2,1,0:T(8,128)(2,1)S(1)}, bf16[8,1024,256]{2,1,0:T(8,128)(2,1)}, u32[]{:S(2)}) copy-start(bf16[8,1024,256]{2,1,0:T(8,128)(2,1)} %constant.8.clone.cosines) | copy-start | bytes 12582916
